TPU v7x, 256 devices: a whole 4x4x8 slice. The times are simulated.
256 devices in a mesh: region: 64 (over z, x, core), batch: 4 (over y).
Axes of the slice: x: 4, y: 4, z: 8, core: 2. Of those that a mesh axis runs over, the one named last changes fastest.
Arguments:
- features: bfloat16 [64, 63, 32768], P('region', None, 'batch'), may hold values from -1 to 1
- spacing: float32 [64, 32768], P('region', 'batch'), may hold values from 6.8359375e-05 to 0.59375
- counts: int32 [64, 512], P('region', 'batch'), may hold values from 0 to 64, as said below
- depth_rank: int32 [512, 64], P('batch'), may hold values from 0 to 63, each once within a row
- target: float32 [3, 512], P(None, 'batch'), may hold values from 0 to 1
- w_in: float32 [64, 64, 256], P('region', 'batch'), may hold values from -0.75 to 0.75
- w_hid: float32 [64, 2, 256, 256], P('region', None, 'batch'), may hold values from -0.375 to 0.375
- b_hid: float32 [64, 2, 256], P('region', None, 'batch'), may hold values from -1.2 to 1.2
- w_out: float32 [64, 4, 256], P('region', None, 'batch'), may hold values from -0.375 to 0.375
- mom_in: float32 [2, 64, 64, 256], P(None, 'region', 'batch'), may hold values from -1 to 4, as said below
- mom_hid: float32 [2, 64, 2, 256, 256], P(None, 'region', None, 'batch'), may hold values from -1 to 4, as said below
- mom_bias: float32 [2, 64, 2, 256], P(None, 'region', None, 'batch'), may hold values from -1 to 4, as said below
- mom_out: float32 [2, 64, 4, 256], P(None, 'region', None, 'batch'), may hold values from -1 to 4, as said below
Outputs:
- new_w_in: float32 [64, 64, 256], P('region')
- new_w_hid: float32 [64, 2, 256, 256], P('region')
- new_b_hid: float32 [64, 2, 256], P('region')
- new_w_out: float32 [64, 4, 256], P('region')
- new_mom_in: float32 [2, 64, 64, 256], P(None, 'region', 'batch')
- new_mom_hid: float32 [2, 64, 2, 256, 256], P(None, 'region', None, 'batch')
- new_mom_bias: float32 [2, 64, 2, 256], P(None, 'region', None, 'batch')
- new_mom_out: float32 [2, 64, 4, 256], P(None, 'region', None, 'batch')
Inputs may be any that keep to these rules, and one draw needn't show every extreme that they name: The first counts[c, ray] slots of a segment are live. `mom_in`: slice 0 is the first moment, slice 1 the second moment, which lies between 0.1 and 4. `mom_hid`: as for mom_in. `mom_bias`: as for mom_in. `mom_out`: as for mom_in.
All inputs are finite; a program needn't handle non-finite values.
Results may differ from a plain program's by a relative error of at most 0.012.
The roundings to bfloat16 on the way count: a program that leaves them out, or rounds other values in their place, can miss the bound.
Values may be sent and summed in bfloat16 or wider, within the bound.
No kernel may reach another device: no remote copies, remote signals or barrier semaphores. Data moves between devices by JAX's collectives and lax.ppermute only.
A program may use at most 128 MiB of HBM per device.

v0:
```python
import jax
import jax.numpy as jnp
from jax import lax
from jax.sharding import PartitionSpec as P

ENC = 63
HID = 256
S = 64


beta_first = 0.9
beta_second = 0.95
learn_rate = 0.01
norm_eps = 1e-06
adam_eps = 1e-08


def contract_first(left, right):
    return lax.dot_general(
        left, right, (((0,), (0,)), ((), ())), preferred_element_type=jnp.float32
    )


def contract_last(left, right):
    return lax.dot_general(
        left, right, (((1,), (1,)), ((), ())), preferred_element_type=jnp.float32
    )


def network(samples, wide_in, wide_hid, bias_hid, wide_out):
    enc_rows = samples.shape[0]
    pre_one = contract_first(wide_in[:enc_rows], samples) + wide_in[enc_rows][:, None].astype(
        jnp.float32
    )
    act_one = jnp.maximum(pre_one, 0.0).astype(jnp.bfloat16)
    pre_two = contract_first(wide_hid[0], act_one) + bias_hid[0][:, None]
    act_two = jnp.maximum(pre_two, 0.0).astype(jnp.bfloat16)
    pre_three = contract_first(wide_hid[1], act_two) + bias_hid[1][:, None]
    act_three = jnp.maximum(pre_three, 0.0).astype(jnp.bfloat16)
    heads = jnp.dot(wide_out, act_three, preferred_element_type=jnp.float32)
    return ((pre_one, act_one, pre_two, act_two, pre_three, act_three), heads)


def optical(heads, gaps, live_counts):
    rays = live_counts.shape[0]
    slot = lax.broadcasted_iota(jnp.int32, (rays, S), 1)
    live = (slot < live_counts[:, None]).astype(jnp.float32)
    density = jax.nn.softplus(heads[0]).reshape(rays, S)
    depth = density * gaps.reshape(rays, S) * live
    colours = jax.nn.sigmoid(heads[1:4])
    return (live, depth, colours)


def summarize(depth, colours):
    rays = depth.shape[0]
    cum_in = jnp.cumsum(depth, axis=1)
    weight = jnp.exp(-(cum_in - depth)) * -jnp.expm1(-depth)
    shade = colours.reshape(3, rays, S)
    seg_colour = jnp.sum(weight[None] * shade, axis=2)
    log_trans = -cum_in[:, -1]
    return (seg_colour, log_trans, cum_in, weight)


def by_cell(table, ranks, own, target):
    seg_all = table[:, 0:3]
    log_all = table[:, 3]
    earlier = ranks[None, :, :] < ranks[:, None, :]
    prefix = jnp.sum(jnp.where(earlier, log_all[None], 0.0), axis=1)
    reach = jnp.exp(prefix)
    lit = reach[:, None] * seg_all
    colour = jnp.sum(lit, axis=0)
    grad_colour = 2.0 * (colour - target)
    own_rank = lax.dynamic_index_in_dim(ranks, own, 0, keepdims=False)
    own_reach = lax.dynamic_index_in_dim(reach, own, 0, keepdims=False)
    later = (ranks > own_rank[None])[:, None, :]
    behind = jnp.sum(jnp.where(later, lit, 0.0), axis=0)
    return (own_reach[None] * grad_colour, jnp.sum(grad_colour * behind, axis=0))


def backward(
    samples, gaps, live, depth, cum_in, weight, colours, heads, acts, mats, grad_seg, grad_log
):
    pre_one, act_one, pre_two, act_two, pre_three, act_three = acts
    wide_in, wide_hid, wide_out = mats
    rays = depth.shape[0]
    shade = colours.reshape(3, rays, S)
    emit = jnp.sum(grad_seg[:, :, None] * shade, axis=0)
    carried = emit * weight
    after = jnp.sum(carried, axis=1, keepdims=True) - jnp.cumsum(carried, axis=1)
    grad_depth = emit * jnp.exp(-cum_in) - after - grad_log[:, None]
    grad_density = (grad_depth * live * gaps.reshape(rays, S)).reshape(1, -1) * jax.nn.sigmoid(
        heads[0:1]
    )
    grad_shade = (grad_seg[:, :, None] * weight[None]).reshape(3, -1) * colours * (1.0 - colours)
    grad_heads = jnp.concatenate([grad_density, grad_shade], axis=0).astype(jnp.bfloat16)
    grad_out = contract_last(grad_heads, act_three)
    back_three = jnp.where(pre_three > 0, contract_first(wide_out, grad_heads), 0.0).astype(
        jnp.bfloat16
    )
    grad_third = contract_last(act_two, back_three)
    bias_third = jnp.sum(back_three.astype(jnp.float32), axis=1)
    back_two = jnp.where(
        pre_two > 0, jnp.dot(wide_hid[1], back_three, preferred_element_type=jnp.float32), 0.0
    ).astype(jnp.bfloat16)
    grad_second = contract_last(act_one, back_two)
    bias_second = jnp.sum(back_two.astype(jnp.float32), axis=1)
    back_one = jnp.where(
        pre_one > 0, jnp.dot(wide_hid[0], back_two, preferred_element_type=jnp.float32), 0.0
    ).astype(jnp.bfloat16)
    grad_first = contract_last(samples, back_one)
    bias_first = jnp.sum(back_one.astype(jnp.float32), axis=1)
    grad_in = jnp.concatenate([grad_first, bias_first[None]], axis=0)
    grad_hid = jnp.stack([grad_second, grad_third])
    grad_bias = jnp.stack([bias_second, bias_third])
    return (grad_in, grad_hid, grad_bias, grad_out)


def adam_step(grad, param, moment, scale):
    scaled = grad * scale
    first = beta_first * moment[0] + (1.0 - beta_first) * scaled
    second = beta_second * moment[1] + (1.0 - beta_second) * scaled * scaled
    fresh = param - learn_rate * first / (jnp.sqrt(second) + adam_eps)
    return (fresh, jnp.stack([first, second]))


def squares_of(tensors):
    return (
        jnp.sum(tensors[0] * tensors[0])
        + jnp.sum(tensors[1] * tensors[1])
        + jnp.sum(tensors[2] * tensors[2])
        + jnp.sum(tensors[3] * tensors[3])
    )


def body(
    features,
    spacing,
    counts,
    depth_rank,
    target,
    w_in,
    w_hid,
    b_hid,
    w_out,
    mom_in,
    mom_hid,
    mom_bias,
    mom_out,
):
    param_count = (ENC + 1) * HID + 2 * HID * HID + 6 * HID
    short_in = w_in[0].astype(jnp.bfloat16)
    short_hid = w_hid[0].astype(jnp.bfloat16)
    short_out = w_out[0].astype(jnp.bfloat16)
    wide_in, wide_hid, wide_out = (
        lax.all_gather(short_in, "batch", axis=0, tiled=True),
        lax.all_gather(short_hid, "batch", axis=1, tiled=True),
        lax.all_gather(short_out, "batch", axis=1, tiled=True),
    )
    full_bias = lax.all_gather(b_hid[0], "batch", axis=1, tiled=True)
    mats = (wide_in, wide_hid, wide_out)
    samples = features[0]
    gaps = spacing[0]
    acts, heads = network(samples, mats[0], mats[1], full_bias, mats[2])
    live, depth, colours = optical(heads, gaps, counts[0])
    seg_colour, log_trans, cum_in, weight = summarize(depth, colours)
    ranks = depth_rank.T
    own = lax.axis_index("region")
    summary = jnp.concatenate([seg_colour, log_trans[None]], axis=0)[None]
    table = lax.all_gather(summary, "region", axis=0, tiled=True)
    grad_seg, grad_log = by_cell(table, ranks, own, target)
    grads = backward(
        samples, gaps, live, depth, cum_in, weight, colours, heads, acts, mats, grad_seg, grad_log
    )
    part_in, part_hid, part_bias, part_out = (
        lax.psum_scatter(grads[0], "batch", scatter_dimension=0, tiled=True),
        lax.psum_scatter(grads[1], "batch", scatter_dimension=1, tiled=True),
        lax.psum_scatter(grads[2], "batch", scatter_dimension=1, tiled=True),
        lax.psum_scatter(grads[3], "batch", scatter_dimension=1, tiled=True),
    )
    local_sq = squares_of((part_in, part_hid, part_bias, part_out))
    total_sq = lax.psum(local_sq, "batch")
    scale = lax.rsqrt(total_sq / param_count + norm_eps)
    fresh_in, moment_first = adam_step(part_in, w_in[0], mom_in[:, 0], scale)
    fresh_hid, moment_second = adam_step(part_hid, w_hid[0], mom_hid[:, 0], scale)
    fresh_bias, moment_third = adam_step(part_bias, b_hid[0], mom_bias[:, 0], scale)
    fresh_out, moment_fourth = adam_step(part_out, w_out[0], mom_out[:, 0], scale)
    whole_in, whole_hid, whole_bias, whole_out = (
        lax.all_gather(fresh_in, "batch", axis=0, tiled=True),
        lax.all_gather(fresh_hid, "batch", axis=1, tiled=True),
        lax.all_gather(fresh_bias, "batch", axis=1, tiled=True),
        lax.all_gather(fresh_out, "batch", axis=1, tiled=True),
    )
    return (
        whole_in[None],
        whole_hid[None],
        whole_bias[None],
        whole_out[None],
        moment_first[:, None],
        moment_second[:, None],
        moment_third[:, None],
        moment_fourth[:, None],
    )


def solution(mesh):
    return jax.shard_map(
        body,
        mesh=mesh,
        in_specs=(
            P("region", None, "batch"),
            P("region", "batch"),
            P("region", "batch"),
            P("batch", None),
            P(None, "batch"),
            P("region", "batch", None),
            P("region", None, "batch", None),
            P("region", None, "batch"),
            P("region", None, "batch"),
            P(None, "region", "batch", None),
            P(None, "region", None, "batch", None),
            P(None, "region", None, "batch"),
            P(None, "region", None, "batch"),
        ),
        out_specs=(
            P("region", None, None),
            P("region", None, None, None),
            P("region", None, None),
            P("region", None, None),
            P(None, "region", "batch", None),
            P(None, "region", None, "batch", None),
            P(None, "region", None, "batch"),
            P(None, "region", None, "batch"),
        ),
        check_vma=False,
    )
```

profile of v0, /device:TPU:2, one launch (start us, length us, event | category | flops | bytes accessed | tf_op | source)
XLA Modules:
  0.0 311.1 jit_solution(11402221975103101179)
XLA Ops:
  7.2 0.8 bitcast_convert_fusion.1
  8.0 12.4 %all_gather.27 = bf16[64,256]{1,0:T(8,128)(2,1)S(1)} all-gather(bf16[16,256]{1,0:T(8,128)(2,1)S(1)} %bitcast_convert_fusion.1), channel_id=1, replica_groups=mesh['region'=64,'batch'=4] {'batch'}, dimensions={0}, use_global_device_ids=true | all-gather | bytes 40960 | tf_op jit(solution)/shard_map/all_gather | solution.py:155
  20.4 0.9 bitcast_convert_fusion
  21.4 12.3 %all_gather.28 = bf16[2,256,256]{2,1,0:T(8,128)(2,1)S(1)} all-gather(bf16[2,64,256]{2,1,0:T(8,128)(2,1)S(1)} %bitcast_convert_fusion), channel_id=1, replica_groups=mesh['region'=64,'batch'=4] {'batch'}, dimensions={1}, use_global_device_ids=true | all-gather | bytes 327680 | tf_op jit(solution)/shard_map/all_gather | solution.py:156
  33.6 0.8 copy.97
  34.4 12.0 %all-gather = f32[1,2,256]{1,0,2:T(1,128)S(1)} all-gather(f32[1,2,64]{1,0,2:T(1,128)S(1)} %copy.97), channel_id=2, replica_groups=mesh['region'=64,'batch'=4] {'batch'}, dimensions={2}, use_global_device_ids=true | all-gather | bytes 2560 | tf_op jit(solution)/shard_map/all_gather | solution.py:159
  46.4 3.6 %slice_reduce_fusion.1 = (f32[256]{0:T(256)S(1)}, f32[256]{0:T(256)S(1)}) fusion(f32[1,2,256]{1,0,2:T(1,128)S(1)} %all-gather), kind=kLoop, calls=%fused_computation.39 | loop fusion | bytes 4096 | tf_op jit(solution)/shard_map/slice | solution.py:36
  50.0 0.7 fusion.31
  50.7 9.4 %all-gather.2 = bf16[4,64,4]{1,2,0:T(4,128)(2,1)S(1)} all-gather(bf16[1,64,4]{1,2,0:T(4,128)(2,1)S(1)} %fusion.31), channel_id=1, replica_groups=mesh['region'=64,'batch'=4] {'batch'}, dimensions={0}, use_global_device_ids=true | all-gather | bytes 2560 | tf_op jit(solution)/shard_map/all_gather | solution.py:157
  60.2 1.3 convolution_add_fusion.2
  61.5 1.3 convolution_add_fusion.1
  62.8 1.9 copy-done.2
  64.7 1.2 convolution_add_fusion
  66.0 2.0 copy-done.1
  67.9 1.2 convolution_bitcast_fusion.1
  69.1 2.0 copy-done.3
  72.0 0.7 reduce.14
  73.6 52.5 %all-gather.3 = f32[64,4,128]{2,1,0:T(4,128)S(1)} all-gather(f32[1,4,128]{2,1,0:T(4,128)S(1)} %maximum_bitcast_fusion.3), channel_id=3, replica_groups=mesh['region'=64,'batch'=4] {'region'}, dimensions={0}, use_global_device_ids=true | all-gather | bytes 133120 | tf_op jit(solution)/shard_map/all_gather | solution.py:169
  128.8 5.2 %convert_reduce_fusion = (f32[256]{0:T(256)S(1)}, bf16[8192,256]{1,0:T(8,128)(2,1)S(1)}) fusion(bf16[256,4]{0,1:T(4,128)(2,1)S(1)} %reshape.252, bf16[3,8192]{1,0:T(4,128)(2,1)S(1)} %get-tuple-element.58, bf16[1,8192]{1,0:T(2,128)(2,1)S(1)} %fusion.22, f32[8192,256]{1,0:T(8,128)} %copy-done.3), kind=kOutput, calls=%fused_computation.11 | convolution fusion | flops 27393792 | bytes 12651520 | tf_op jit(solution)/shard_map/dot_general | solution.py:19
  134.0 8.7 %convert_reduce_fusion.1 = (f32[256]{0:T(256)S(1)}, bf16[8192,256]{1,0:T(8,128)(2,1)}) fusion(bf16[8192,256]{1,0:T(8,128)(2,1)S(1)} %get-tuple-element.77, bf16[2,256,256]{2,1,0:T(8,128)(2,1)S(1)} %all_gather.28, f32[8192,256]{1,0:T(8,128)} %copy-done.1), kind=kOutput, calls=%fused_computation.12 | convolution fusion | flops 1084227328 | bytes 16909312 | tf_op jit(solution)/shard_map/dot_general | solution.py:103
  142.7 0.8 copy.119
  143.6 5.8 %fusion.9 = f32[256,4]{1,0:T(8,128)} fusion(f32[8192,256]{1,0:T(8,128)} %copy-done.3, bf16[3,8192]{1,0:T(4,128)(2,1)S(1)} %get-tuple-element.58, bf16[1,8192]{1,0:T(2,128)(2,1)S(1)} %fusion.22), kind=kOutput, calls=%fused_computation.23 | convolution fusion | flops 21102592 | bytes 8458240
  149.5 6.1 %convert_reduce_fusion.2 = (f32[256]{0:T(256)S(1)}, bf16[256,8192]{1,0:T(8,128)(2,1)S(1)}) fusion(bf16[8192,256]{1,0:T(8,128)(2,1)} %get-tuple-element.79, bf16[2,256,256]{2,1,0:T(8,128)(2,1)S(1)} %all_gather.28, f32[256,8192]{1,0:T(8,128)} %copy-done.2), kind=kOutput, calls=%fused_computation.13 | convolution fusion | flops 1084227328 | bytes 16909312 | tf_op jit(solution)/shard_map/dot_general | solution.py:108
  155.5 1.4 convolution_bitcast_fusion.2
  156.9 0.6 pad_maximum_fusion.2
  157.9 6.0 %fusion.7 = f32[1,256,256]{2,1,0:T(8,128)S(1)} fusion(bf16[8192,256]{1,0:T(8,128)(2,1)} %copy-done.5, f32[8192,256]{1,0:T(8,128)} %copy-done.1), kind=kOutput, calls=%fused_computation.21 | convolution fusion | flops 1077936128 | bytes 12845056 | tf_op jit(solution)/shard_map/dot_general | solution.py:25
  164.0 4.7 %fusion.8 = f32[1,256,256]{2,1,0:T(8,128)S(1)} fusion(bf16[8192,256]{1,0:T(8,128)(2,1)S(1)} %copy-done.4, f32[256,8192]{1,0:T(8,128)} %copy-done.2), kind=kOutput, calls=%fused_computation.22 | convolution fusion | flops 1077936128 | bytes 12845056 | tf_op jit(solution)/shard_map/dot_general | solution.py:25
  168.7 0.8 pad_maximum_fusion
  169.6 0.8 copy.120
  171.0 16.9 %reduce-scatter.15.cloned.1.call-done = f32[64,4]{1,0:T(8,128)} async-done(((f32[256,4]{1,0:T(8,128)}), f32[64,4]{1,0:T(8,128)}) %reduce-scatter.15.cloned.1.call-update) | async-done | bytes 1040
  188.0 0.8 copy.122
  189.4 24.3 %reduce-scatter.9.cloned.1.call-done = f32[16,256]{1,0:T(8,128)} async-done(((f32[64,256]{1,0:T(8,128)}), f32[16,256]{1,0:T(8,128)}) %reduce-scatter.9.cloned.1.call-update) | async-done | bytes 16400 | tf_op jit(solution)/shard_map/reduce_scatter | solution.py:175
  213.7 1.3 multiply_reduce_fusion.3
  215.0 25.5 %reduce-scatter.11.cloned.1.call-done = f32[2,64,256]{2,1,0:T(8,128)} async-done(((f32[2,256,256]{2,1,0:T(8,128)}), f32[2,64,256]{2,1,0:T(8,128)}) %reduce-scatter.11.cloned.1.call-update) | async-done | bytes 131088 | tf_op jit(solution)/shard_map/reduce_scatter | solution.py:176
  240.6 1.5 multiply_reduce_fusion.1
  244.7 8.9 %psum.7 = f32[]{:T(128)} all-reduce(f32[]{:T(128)S(6)} %add.139), channel_id=1, replica_groups=mesh['region'=64,'batch'=4] {'batch'}, use_global_device_ids=true, to_apply=%region_20.21 | all-reduce | flops 1 | bytes 8 | tf_op jit(solution)/shard_map/psum | solution.py:181
  254.4 10.4 %all-gather.5 = f32[4,64,4]{1,2,0:T(4,128)S(1)} all-gather(f32[1,64,4]{1,2,0:T(4,128)S(1)} %get-tuple-element.68), channel_id=1, replica_groups=mesh['region'=64,'batch'=4] {'batch'}, dimensions={0}, use_global_device_ids=true | all-gather | bytes 5120 | tf_op jit(solution)/shard_map/all_gather | solution.py:191
  264.7 0.7 reshape.258
  265.4 8.1 %all-gather.4 = f32[4,64,2]{1,2,0:T(2,128)S(1)} all-gather(f32[1,64,2]{1,2,0:T(2,128)S(1)} %get-tuple-element.73), channel_id=1, replica_groups=mesh['region'=64,'batch'=4] {'batch'}, dimensions={0}, use_global_device_ids=true | all-gather | bytes 2560 | tf_op jit(solution)/shard_map/all_gather | solution.py:190
  273.5 0.7 reshape.256
  274.2 1.0 fusion.23
  275.2 12.9 %all_gather.33 = f32[2,256,256]{2,1,0:T(8,128)S(1)} all-gather(f32[2,64,256]{2,1,0:T(8,128)S(1)} %get-tuple-element.56), channel_id=1, replica_groups=mesh['region'=64,'batch'=4] {'batch'}, dimensions={1}, use_global_device_ids=true | all-gather | bytes 655360 | tf_op jit(solution)/shard_map/all_gather | solution.py:189
  288.1 0.7 fusion.26
  288.8 11.9 %all_gather.32 = f32[64,256]{1,0:T(8,128)S(1)} all-gather(f32[16,256]{1,0:T(8,128)S(1)} %get-tuple-element.63), channel_id=1, replica_groups=mesh['region'=64,'batch'=4] {'batch'}, dimensions={0}, use_global_device_ids=true | all-gather | bytes 81920 | tf_op jit(solution)/shard_map/all_gather | solution.py:188
  301.8 0.7 maximum_bitcast_fusion
  302.6 0.6 maximum_bitcast_fusion.1
  303.2 0.6 copy.125
  303.8 0.8 copy.126
  (102 shorter events, 7.3 us)
Async XLA Ops:
  7.2 53.0 %copy-start = (bf16[1,63,8192]{2,1,0:T(8,128)(2,1)S(1)}, bf16[1,63,8192]{2,1,0:T(8,128)(2,1)}, u32[]{:S(2)}) copy-start(bf16[1,63,8192]{2,1,0:T(8,128)(2,1)} %param.13) | copy-start | bytes 3096580
  7.2 162.4 %reduce-scatter.13.cloned.1.call-start = ((), (), s32[]{:S(2)}) async-start(), calls=%async_computation.6 | async-start | bytes 163840
  61.5 3.2 %copy-start.2 = (f32[256,8192]{1,0:T(8,128)}, f32[256,8192]{1,0:T(8,128)S(1)}, u32[]{:S(2)}) copy-start(f32[256,8192]{1,0:T(8,128)S(1)} %convolution_add_fusion.2) | copy-start | bytes 25165828
  64.7 3.2 %copy-start.1 = (f32[8192,256]{1,0:T(8,128)}, f32[8192,256]{1,0:T(8,128)S(1)}, u32[]{:S(2)}) copy-start(f32[8192,256]{1,0:T(8,128)S(1)} %convolution_add_fusion.1) | copy-start | bytes 25165828
  67.9 3.2 %copy-start.3 = (f32[8192,256]{1,0:T(8,128)}, f32[8192,256]{1,0:T(8,128)S(1)}, u32[]{:S(2)}) copy-start(f32[8192,256]{1,0:T(8,128)S(1)} %convolution_add_fusion) | copy-start | bytes 25165828
  67.9 4.1 %copy-start.8 = (f32[1,8192]{1,0:T(1,128)S(1)}, f32[1,8192]{1,0:T(1,128)}, u32[]{:S(2)}) copy-start(f32[1,8192]{1,0:T(1,128)} %param.14) | copy-start | bytes 98308
  67.9 5.0 %copy-start.13 = (s32[1,128]{1,0:T(1,128)S(1)}, s32[1,128]{1,0:T(1,128)}, u32[]{:S(2)}) copy-start(s32[1,128]{1,0:T(1,128)} %param.15) | copy-start | bytes 1540
  67.9 58.2 %copy-start.7 = (s32[128,64]{0,1:T(8,128)S(1)}, s32[128,64]{0,1:T(8,128)}, u32[]{:S(2)}) copy-start(s32[128,64]{0,1:T(8,128)} %param.16) | copy-start | bytes 98308
  67.9 58.7 %copy-start.16 = (f32[3,128]{1,0:T(4,128)S(1)}, f32[3,128]{1,0:T(4,128)}, u32[]{:S(2)}) copy-start(f32[3,128]{1,0:T(4,128)} %param.17) | copy-start | bytes 4612
  134.0 8.7 %copy-start.5 = (bf16[8192,256]{1,0:T(8,128)(2,1)}, bf16[8192,256]{1,0:T(8,128)(2,1)S(1)}, u32[]{:S(2)}) copy-start(bf16[8192,256]{1,0:T(8,128)(2,1)S(1)} %get-tuple-element.77) | copy-start | bytes 12582916
  143.6 44.4 %reduce-scatter.15.cloned.1.call-start = ((), (), s32[]{:S(2)}) async-start(), calls=%async_computation.7 | async-start | bytes 163840
  149.4 64.3 %reduce-scatter.9.cloned.1.call-start = ((), (), s32[]{:S(2)}) async-start(), calls=%async_computation.4 | async-start | bytes 81920 | tf_op jit(solution)/shard_map/reduce_scatter | solution.py:175
  157.6 83.0 %reduce-scatter.11.cloned.1.call-start = ((), (), s32[]{:S(2)}) async-start(), calls=%async_computation.5 | async-start | bytes 655360 | tf_op jit(solution)/shard_map/reduce_scatter | solution.py:176
  157.9 6.0 %copy-start.4 = (bf16[8192,256]{1,0:T(8,128)(2,1)S(1)}, bf16[8192,256]{1,0:T(8,128)(2,1)}, u32[]{:S(2)}) copy-start(bf16[8192,256]{1,0:T(8,128)(2,1)} %get-tuple-element.79) | copy-start | bytes 12582916
  163.9 90.4 %copy-start.12 = (f32[1,4,64]{2,1,0:T(4,128)S(1)}, f32[1,4,64]{2,1,0:T(4,128)}, u32[]{:S(2)}) copy-start(f32[1,4,64]{2,1,0:T(4,128)} %param.21) | copy-start | bytes 3076
  163.9 90.4 %copy-start.15 = (f32[2,1,4,64]{3,2,1,0:T(4,128)S(1)}, f32[2,1,4,64]{3,2,1,0:T(4,128)}, u32[]{:S(2)}) copy-start(f32[2,1,4,64]{3,2,1,0:T(4,128)} %param.25) | copy-start | bytes 6148
  164.0 90.4 %copy-start.14 = (f32[1,2,64]{2,1,0:T(2,128)S(1)}, f32[1,2,64]{2,1,0:T(2,128)}, u32[]{:S(2)}) copy-start(f32[1,2,64]{2,1,0:T(2,128)} %param.20) | copy-start | bytes 1540
  164.0 90.4 %copy-start.17 = (f32[2,1,2,64]{3,2,1,0:T(2,128)S(1)}, f32[2,1,2,64]{3,2,1,0:T(2,128)}, u32[]{:S(2)}) copy-start(f32[2,1,2,64]{3,2,1,0:T(2,128)} %param.24) | copy-start | bytes 3076
  164.0 110.2 %copy-start.6 = (f32[1,2,64,256]{3,2,1,0:T(8,128)S(1)}, f32[1,2,64,256]{3,2,1,0:T(8,128)}, u32[]{:S(2)}) copy-start(f32[1,2,64,256]{3,2,1,0:T(8,128)} %param.19) | copy-start | bytes 393220
  164.0 110.2 %copy-start.9 = (f32[2,1,2,64,256]{4,3,2,1,0:T(8,128)S(1)}, f32[2,1,2,64,256]{4,3,2,1,0:T(8,128)}, u32[]{:S(2)}) copy-start(f32[2,1,2,64,256]{4,3,2,1,0:T(8,128)} %param.23) | copy-start | bytes 786436
  164.0 124.0 %copy-start.10 = (f32[1,16,256]{2,1,0:T(8,128)S(1)}, f32[1,16,256]{2,1,0:T(8,128)}, u32[]{:S(2)}) copy-start(f32[1,16,256]{2,1,0:T(8,128)} %param.18) | copy-start | bytes 49156
  164.0 124.0 %copy-start.11 = (f32[2,1,16,256]{3,2,1,0:T(8,128)S(1)}, f32[2,1,16,256]{3,2,1,0:T(8,128)}, u32[]{:S(2)}) copy-start(f32[2,1,16,256]{3,2,1,0:T(8,128)} %param.22) | copy-start | bytes 98308
Sparse Core Ops, SparseCore 0:
  143.7 18.8 reduce-scatter.12
  165.3 22.6 reduce-scatter.14
  191.1 22.5 reduce-scatter.8
  216.8 23.6 reduce-scatter.10
where the time goes:
time: 312 us; the launch traced here: 311 us
  blocking collectives  151 us (48%)
  waiting for transfers between devices  66.8 us (21%)
  matrix products  42.9 us (14%)
  local copies, waits for them, and re-layouts  18.4 us (6%)
  between operations  17.5 us (6%)
  other arithmetic  14.4 us (5%)
    all_gather x1, blocking collectives, body(): table = lax.all_gather(summary, 'region', axis=0, tiled=True)  52.5 us
    reduce_scatter x1, waiting for transfers between devices, body(): lax.psum_scatter(grads[1], 'batch', scatter_dimension=1, tiled=True)  25.5 us
    reduce_scatter x1, waiting for transfers between devices, body(): lax.psum_scatter(grads[0], 'batch', scatter_dimension=0, tiled=True)  24.3 us
    unnamed x6, waiting for transfers between devices  17 us
    all_gather x1, blocking collectives, body(): lax.all_gather(fresh_hid, 'batch', axis=1, tiled=True)  12.9 us
    unnamed x46, local copies, waits for them, and re-layouts  12.5 us
    all_gather x1, blocking collectives, body(): lax.all_gather(short_in, 'batch', axis=0, tiled=True)  12.4 us
    all_gather x1, blocking collectives, body(): lax.all_gather(short_hid, 'batch', axis=1, tiled=True)  12.3 us
  transfers between devices with their start and end apart: 4, of which 3 were waited for; matrix products, arithmetic and copies ran while one was open for 10% of the time, Pallas kernels for 0%

commit v1 on v0

v1 whole, which is shorter than its diff:
```python
import functools

import jax
import jax.numpy as jnp
from jax import lax
from jax.experimental import pallas as pl
from jax.experimental.pallas import tpu as pltpu
from jax.sharding import PartitionSpec as P

ENC = 63
HID = 256
S = 64
N_BATCH = 4
CHUNK = 1024
MIB = 1 << 20

beta_first = 0.9
beta_second = 0.95
learn_rate = 0.01
norm_eps = 1e-06
adam_eps = 1e-08

f32 = jnp.float32
bf16 = jnp.bfloat16

ROWS_IN = HID // 16
ROWS_HID = HID // N_BATCH
MISC = ROWS_IN + 2 * ROWS_HID
BLOCK = MISC + 16

VMEM_WHOLE = pl.BlockSpec(memory_space=pltpu.VMEM)
SMEM_WHOLE = pl.BlockSpec(memory_space=pltpu.SMEM)


def dot(left, right):
    return lax.dot_general(left, right, (((1,), (0,)), ((), ())), preferred_element_type=f32)


def dot_last(left, right):
    return lax.dot_general(left, right, (((1,), (1,)), ((), ())), preferred_element_type=f32)


def at_own_lanes(rows, own):
    source = lax.broadcasted_iota(jnp.int32, (ROWS_HID, HID), 0)
    lane = lax.broadcasted_iota(jnp.int32, (ROWS_HID, HID), 1)
    place = jnp.where(lane == source + own * ROWS_HID, 1.0, 0.0).astype(bf16)
    return dot(rows, place).astype(bf16)


def pack_weights(idx, w_in, w_hid, b_hid, w_out, out):
    out[0:ROWS_IN, :] = w_in[0].astype(bf16)
    for layer in range(2):
        at = ROWS_IN + layer * ROWS_HID
        out[at : at + ROWS_HID, :] = w_hid[0, layer].astype(bf16)
    bias = b_hid[0]
    top = bias.astype(bf16).astype(f32)
    middle = (bias - top).astype(bf16).astype(f32)
    rest = bias - top - middle
    rows = jnp.concatenate(
        [w_out[0], top, middle, rest, jnp.zeros((6, ROWS_HID), f32)], axis=0
    ).astype(bf16)
    out[MISC:BLOCK, :] = at_own_lanes(rows, idx[1])


def pack_state(idx, w_in, w_hid, w_out, mom_in, mom_hid, mom_bias, mom_out, out):
    def low(value):
        return (value - value.astype(bf16).astype(f32)).astype(bf16)

    out[0:ROWS_IN, :] = low(w_in[0])
    for layer in range(2):
        at = ROWS_IN + layer * ROWS_HID
        out[at : at + ROWS_HID, :] = low(w_hid[0, layer])
    rest = w_out[0] - w_out[0].astype(bf16).astype(f32)
    rows = jnp.concatenate([rest, jnp.zeros((12, ROWS_HID), f32)], axis=0)
    out[MISC:BLOCK, :] = at_own_lanes(rows.astype(bf16), idx[1])
    for moment in range(2):
        base = BLOCK * (moment + 1)
        out[base : base + ROWS_IN, :] = mom_in[moment, 0].astype(bf16)
        for layer in range(2):
            at = base + ROWS_IN + layer * ROWS_HID
            out[at : at + ROWS_HID, :] = mom_hid[moment, 0, layer].astype(bf16)
        rows = jnp.concatenate(
            [mom_out[moment, 0], mom_bias[moment, 0], jnp.zeros((10, ROWS_HID), f32)], axis=0
        )
        out[base + MISC : base + BLOCK, :] = at_own_lanes(rows.astype(bf16), idx[1])


def turn(rows):
    turned = jnp.concatenate([rows, rows], axis=0).T
    lane = lax.broadcasted_iota(jnp.int32, (S, 2 * S), 1)
    return jnp.where(lane < S, turned[:S], turned[S:])


def running_sum(values):
    row = lax.broadcasted_iota(jnp.int32, values.shape, 0)
    step = 1
    while step < S:
        values = values + jnp.where(row >= step, pltpu.roll(values, step, 0), 0.0)
        step *= 2
    return values


def one_minus_exp(depth):
    small = depth * (1.0 - depth * (0.5 - depth * (1.0 / 6.0 - depth * (1.0 / 24.0 - depth * (1.0 / 120.0)))))
    return jnp.where(depth < 0.1, small, 1.0 - jnp.exp(-depth))


def sigmoid(value):
    return 1.0 / (1.0 + jnp.exp(-value))


def forward_kernel(
    idx, own, from_one, from_two, from_three, feats, gaps, counts,
    act_one, act_two, act_three, wide_in, wide_hid, wide_misc, shading, summary,
    turned_in, turned_hid, bias_cols, out_rows, heads_rows,
):
    step = pl.program_id(0)
    tiles = CHUNK // 128

    @pl.when(step == 0)
    def _():
        misc = jnp.zeros((16, HID), f32)
        for back, block in enumerate((own, from_one, from_two, from_three)):
            owner = (idx[1] + N_BATCH - back) % N_BATCH
            wide_in[pl.ds(pl.multiple_of(owner * ROWS_IN, 16), ROWS_IN), :] = block[0:ROWS_IN, :]
            for layer in range(2):
                at = ROWS_IN + layer * ROWS_HID
                wide_hid[layer, pl.ds(pl.multiple_of(owner * ROWS_HID, 16), ROWS_HID), :] = block[
                    at : at + ROWS_HID, :
                ]
            misc = misc + block[MISC:BLOCK, :].astype(f32)
        wide_misc[...] = misc
        turned_in[...] = wide_in[...].astype(f32).T.astype(bf16)
        for layer in range(2):
            turned_hid[layer] = wide_hid[layer].astype(f32).T.astype(bf16)
        bias = misc[4:6] + misc[6:8] + misc[8:10]
        bias_cols[...] = jnp.concatenate([bias, jnp.zeros((6, HID), f32)], axis=0).T
        row = lax.broadcasted_iota(jnp.int32, (16, HID), 0)
        out_rows[...] = jnp.where(row < 4, misc, 0.0).astype(bf16)

    one = jnp.maximum(dot(turned_in[...], feats[...]), 0.0).astype(bf16)
    act_one[...] = one
    two = jnp.maximum(dot(turned_hid[0], one) + bias_cols[:, 0:1], 0.0).astype(bf16)
    act_two[...] = two
    three = jnp.maximum(dot(turned_hid[1], two) + bias_cols[:, 1:2], 0.0).astype(bf16)
    act_three[...] = three
    heads = dot(out_rows[...], three)
    for tile in range(tiles):
        at = pl.multiple_of((step * tiles + tile) * 8, 8)
        heads_rows[pl.ds(at, 8), :] = heads[0:8, tile * 128 : (tile + 1) * 128]

    @pl.when(step == pl.num_programs(0) - 1)
    def _():
        density = turn(heads_rows[pl.ds(0, S, stride=8), :])
        gap = turn(gaps[...])
        slot = lax.broadcasted_iota(jnp.int32, (S, 128), 0)
        live = jnp.where(slot < counts[...], 1.0, 0.0)
        soft = jnp.maximum(density, 0.0) + jnp.log1p(jnp.exp(-jnp.abs(density)))
        depth = soft * gap * live
        total = running_sum(depth)
        weight = jnp.exp(-(total - depth)) * one_minus_exp(depth)
        for channel in range(3):
            colour = sigmoid(turn(heads_rows[pl.ds(channel + 1, S, stride=8), :]))
            shading[channel] = colour
            summary[channel : channel + 1, :] = jnp.sum(weight * colour, axis=0, keepdims=True)
        summary[3:4, :] = -total[S - 1 : S]
        shading[3] = weight
        shading[4] = jnp.exp(-total)
        shading[5] = live * gap * sigmoid(density)


def composite(idx, table, ranks, target, shading, reach_rows, grad_rows):
    cells = ranks.shape[0]
    order = ranks[...]
    logs = table[pl.ds(3, cells, stride=4), :]
    prefix = jnp.zeros((cells, 128), f32)
    for cell in range(cells):
        prefix = prefix + jnp.where(
            ranks[cell : cell + 1, :] < order, table[4 * cell + 3 : 4 * cell + 4, :], 0.0
        )
    del logs
    reach = jnp.exp(prefix)
    reach_rows[...] = reach
    own_reach = reach_rows[pl.ds(idx[0], 1), :]
    later = order > ranks[pl.ds(idx[0], 1), :]
    grad_seg = []
    grad_log = jnp.zeros((1, 128), f32)
    for channel in range(3):
        lit = reach * table[pl.ds(channel, cells, stride=4), :]
        grad_colour = 2.0 * (jnp.sum(lit, axis=0, keepdims=True) - target[channel : channel + 1, :])
        behind = jnp.sum(jnp.where(later, lit, 0.0), axis=0, keepdims=True)
        grad_log = grad_log + grad_colour * behind
        grad_seg.append(own_reach * grad_colour)
    weight = shading[3]
    emit = grad_seg[0] * shading[0] + grad_seg[1] * shading[1] + grad_seg[2] * shading[2]
    carried = emit * weight
    running = running_sum(carried)
    after = running[S - 1 : S] - running
    grad_depth = emit * shading[4] - after - grad_log
    grad_rows[...] = jnp.zeros(grad_rows.shape, f32)
    grad_rows[pl.ds(0, S, stride=16), :] = turn(grad_depth * shading[5])
    for channel in range(3):
        colour = shading[channel]
        shade = grad_seg[channel] * weight * colour * (1.0 - colour)
        grad_rows[pl.ds(channel + 1, S, stride=16), :] = turn(shade)


def masked(act, back):
    return jnp.where(act > 0, back.astype(bf16), jnp.zeros((), bf16))


def first_row(rows):
    row = lax.broadcasted_iota(jnp.int32, rows.shape, 0)
    return jnp.where(row == 0, rows, 0.0)


def upper_kernel(
    idx, table, ranks, target, shading, wide_misc, act_two, act_three,
    back_three, grads,
    reach_rows, grad_rows, out_cols, sum_third, sum_out,
):
    step = pl.program_id(0)
    tiles = CHUNK // 128

    @pl.when(step == 0)
    def _():
        composite(idx, table, ranks, target, shading, reach_rows, grad_rows)
        row = lax.broadcasted_iota(jnp.int32, (16, HID), 0)
        out_cols[...] = jnp.where(row < 4, wide_misc[...], 0.0).T.astype(bf16)
        sum_third[...] = jnp.zeros(sum_third.shape, f32)
        sum_out[...] = jnp.zeros(sum_out.shape, f32)

    heads = jnp.concatenate(
        [
            grad_rows[pl.ds(pl.multiple_of((step * tiles + tile) * 16, 16), 16), :]
            for tile in range(tiles)
        ],
        axis=1,
    ).astype(bf16)
    three = act_three[...]
    back = masked(three, dot(out_cols[...], heads))
    back_three[...] = back
    sum_out[...] += dot_last(heads, three)
    ones = jnp.ones((16, CHUNK), bf16)
    sum_third[...] += dot_last(jnp.concatenate([act_two[...], ones], axis=0), back)

    @pl.when(step == pl.num_programs(0) - 1)
    def _():
        grads[0:HID, :] = sum_third[0:HID, :].astype(bf16)
        row = lax.broadcasted_iota(jnp.int32, (16, HID), 0)
        misc = jnp.where(row < 4, sum_out[...], jnp.where(row == 5, sum_third[HID : HID + 16, :], 0.0))
        grads[HID : HID + 16, :] = misc.astype(bf16)


def lower_kernel(
    wide_hid, feats, act_one, act_two, back_three,
    grads,
    sum_second, sum_first,
):
    step = pl.program_id(0)

    @pl.when(step == 0)
    def _():
        sum_second[...] = jnp.zeros(sum_second.shape, f32)
        sum_first[...] = jnp.zeros(sum_first.shape, f32)

    one = act_one[...]
    back_two = masked(act_two[...], dot(wide_hid[1], back_three[...]))
    ones = jnp.ones((16, CHUNK), bf16)
    sum_second[...] += dot_last(jnp.concatenate([one, ones], axis=0), back_two)
    back_one = masked(one, dot(wide_hid[0], back_two))
    sum_first[...] += dot_last(feats[...], back_one)

    @pl.when(step == pl.num_programs(0) - 1)
    def _():
        grads[0:HID, :] = sum_second[0:HID, :].astype(bf16)
        grads[HID : HID + 64, :] = sum_first[...].astype(bf16)
        row = lax.broadcasted_iota(jnp.int32, (16, HID), 0)
        misc = jnp.where(row == 4, sum_second[HID : HID + 16, :], 0.0)
        grads[HID + 64 : HID + 80, :] = misc.astype(bf16)


def adam(grad, first, second, scale):
    scaled = grad * scale
    first = beta_first * first + (1.0 - beta_first) * scaled
    second = beta_second * second + (1.0 - beta_second) * scaled * scaled
    return first, second, learn_rate * first / (jnp.sqrt(second) + adam_eps)


def update_kernel(
    idx,
    upper_0, upper_1, upper_2, upper_3,
    lower_0, lower_1, lower_2, lower_3,
    high_0, high_1, high_2, high_3,
    state_0, state_1, state_2, state_3,
    wide_misc, mom_in, mom_hid, mom_bias, mom_out,
    new_in, new_hid, new_bias, new_out,
    out_in, out_hid, out_bias, out_out,
    upper, lower,
):
    param_count = (ENC + 1) * HID + 2 * HID * HID + 6 * HID
    upper[...] = (upper_0[...].astype(f32) + upper_2[...].astype(f32)) + (
        upper_1[...].astype(f32) + upper_3[...].astype(f32)
    )
    lower[...] = (lower_0[...].astype(f32) + lower_2[...].astype(f32)) + (
        lower_1[...].astype(f32) + lower_3[...].astype(f32)
    )
    squares = jnp.sum(upper[...] * upper[...], axis=0, keepdims=True) + jnp.sum(
        lower[...] * lower[...], axis=0, keepdims=True
    )
    total = jnp.sum(squares, axis=1, keepdims=True)
    scale = lax.rsqrt(total / param_count + norm_eps)

    def fresh(grad, high, state, at, rows):
        _, _, change = adam(
            grad,
            state[BLOCK + at : BLOCK + at + rows, :].astype(f32),
            state[2 * BLOCK + at : 2 * BLOCK + at + rows, :].astype(f32),
            scale,
        )
        value = high[at : at + rows, :].astype(f32) + state[at : at + rows, :].astype(f32)
        return value - change

    highs = (high_0, high_1, high_2, high_3)
    states = (state_0, state_1, state_2, state_3)
    low_misc = jnp.zeros((16, HID), f32)
    first_misc = jnp.zeros((16, HID), f32)
    second_misc = jnp.zeros((16, HID), f32)
    for back in range(N_BATCH):
        owner = (idx[1] + N_BATCH - back) % N_BATCH
        high, state = highs[back], states[back]
        hid = pl.ds(pl.multiple_of(owner * ROWS_HID, 16), ROWS_HID)
        new_hid[0, 0, hid, :] = fresh(lower[hid, :], high, state, ROWS_IN, ROWS_HID)
        new_hid[0, 1, hid, :] = fresh(upper[hid, :], high, state, ROWS_IN + ROWS_HID, ROWS_HID)
        first = pl.ds(pl.multiple_of(owner * ROWS_IN, 16), ROWS_IN)
        grad = lower[pl.ds(pl.multiple_of(HID + owner * ROWS_IN, 16), ROWS_IN), :]
        new_in[0, first, :] = fresh(grad, high, state, 0, ROWS_IN)
        low_misc = low_misc + state[MISC:BLOCK, :].astype(f32)
        first_misc = first_misc + state[BLOCK + MISC : 2 * BLOCK, :].astype(f32)
        second_misc = second_misc + state[2 * BLOCK + MISC : 3 * BLOCK, :].astype(f32)

    grad_misc = upper[HID : HID + 16, :] + lower[HID + 64 : HID + 80, :]
    _, _, change = adam(grad_misc, first_misc, second_misc, scale)
    weights = wide_misc[...]
    new_out[0] = weights[0:4] + low_misc[0:4] - change[0:4]
    new_bias[0] = weights[4:6] + weights[6:8] + weights[8:10] - change[4:6]

    own = pl.ds(pl.multiple_of(idx[1] * ROWS_HID, 16), ROWS_HID)
    for layer, grads in ((0, lower), (1, upper)):
        moments = adam(grads[own, :], mom_hid[0, 0, layer], mom_hid[1, 0, layer], scale)
        out_hid[0, 0, layer] = moments[0]
        out_hid[1, 0, layer] = moments[1]
    grad = lower[pl.ds(pl.multiple_of(HID + idx[1] * ROWS_IN, 16), ROWS_IN), :]
    moments = adam(grad, mom_in[0, 0], mom_in[1, 0], scale)
    out_in[0, 0] = moments[0]
    out_in[1, 0] = moments[1]
    own_misc = jnp.zeros((16, ROWS_HID), f32)
    for owner in range(N_BATCH):
        part = grad_misc[:, owner * ROWS_HID : (owner + 1) * ROWS_HID]
        own_misc = own_misc + jnp.where(idx[1] == owner, part, 0.0)
    moments = adam(own_misc[0:4], mom_out[0, 0], mom_out[1, 0], scale)
    out_out[0, 0] = moments[0]
    out_out[1, 0] = moments[1]
    moments = adam(own_misc[4:6], mom_bias[0, 0], mom_bias[1, 0], scale)
    out_bias[0, 0] = moments[0]
    out_bias[1, 0] = moments[1]


def params(limit=48):
    return pltpu.CompilerParams(vmem_limit_bytes=limit * MIB)


def from_others(block):
    return [
        lax.ppermute(block, "batch", [(i, (i + hop) % N_BATCH) for i in range(N_BATCH)])
        for hop in (1, 2, 3)
    ]


def shape(dims, dtype=f32):
    return jax.ShapeDtypeStruct(dims, dtype)


def body(
    inner,
    features, spacing, counts, depth_rank, target,
    w_in, w_hid, b_hid, w_out,
    mom_in, mom_hid, mom_bias, mom_out,
):
    samples = features.shape[2]
    rays = samples // S
    cells = depth_rank.shape[1]
    steps = samples // CHUNK
    outer = cells // inner
    idx = jnp.stack([lax.axis_index("region"), lax.axis_index("batch")]).astype(jnp.int32)

    block = pl.pallas_call(
        pack_weights,
        out_shape=shape((BLOCK, HID), bf16),
        in_specs=[SMEM_WHOLE] + [VMEM_WHOLE] * 4,
        out_specs=VMEM_WHOLE,
        name="pack_weights",
    )(idx, w_in, w_hid, b_hid, w_out)
    highs = [block] + from_others(block)
    state = pl.pallas_call(
        pack_state,
        out_shape=shape((3 * BLOCK, HID), bf16),
        in_specs=[SMEM_WHOLE] + [VMEM_WHOLE] * 7,
        out_specs=VMEM_WHOLE,
        name="pack_state",
    )(idx, w_in, w_hid, w_out, mom_in, mom_hid, mom_bias, mom_out)
    states = [state] + from_others(state)

    feats = jnp.concatenate([features[0], jnp.ones((1, samples), bf16)], axis=0)
    gaps = spacing[0].reshape(rays // 2, 2 * S)
    live_counts = counts[0].reshape(rays // 2, 2).T.reshape(1, rays)
    ranks = depth_rank.reshape(rays // 2, 2, cells).transpose(2, 1, 0).reshape(cells, rays)
    goal = target.reshape(3, rays // 2, 2).transpose(0, 2, 1).reshape(3, rays)

    columns = lambda rows: pl.BlockSpec((rows, CHUNK), lambda i: (0, i))
    whole = lambda *dims: pl.BlockSpec(dims, lambda i: (0,) * len(dims))
    act = shape((HID, samples), bf16)
    act_one, act_two, act_three, wide_in, wide_hid, wide_misc, shading, summary = pl.pallas_call(
        forward_kernel,
        grid=(steps,),
        out_shape=(
            act, act, act, shape((ENC + 1, HID), bf16), shape((2, HID, HID), bf16),
            shape((16, HID)), shape((6, S, 128)), shape((4, rays)),
        ),
        in_specs=[SMEM_WHOLE] + [whole(BLOCK, HID)] * 4
        + [columns(ENC + 1), whole(rays // 2, 2 * S), whole(1, rays)],
        out_specs=(
            columns(HID), columns(HID), columns(HID), whole(ENC + 1, HID), whole(2, HID, HID),
            whole(16, HID), whole(6, S, 128), whole(4, rays),
        ),
        scratch_shapes=[
            pltpu.VMEM((HID, ENC + 1), bf16),
            pltpu.VMEM((2, HID, HID), bf16),
            pltpu.VMEM((HID, 8), f32),
            pltpu.VMEM((16, HID), bf16),
            pltpu.VMEM((samples // 16, 128), f32),
        ],
        compiler_params=params(),
        name="forward",
    )(idx, *highs, feats, gaps, live_counts)

    near = [[z * inner + i for i in range(inner)] for z in range(outer)]
    far = [[z * inner + i for z in range(outer)] for i in range(inner)]
    some = lax.all_to_all(
        jnp.broadcast_to(summary[None], (inner, 4, rays)), "region", 0, 0,
        axis_index_groups=near, tiled=True,
    )
    table = lax.all_to_all(
        jnp.broadcast_to(some[None], (outer, inner, 4, rays)), "region", 0, 0,
        axis_index_groups=far, tiled=True,
    ).reshape(cells * 4, rays)

    back_three, grads_upper = pl.pallas_call(
        upper_kernel,
        grid=(steps,),
        out_shape=(act, shape((HID + 16, HID), bf16)),
        in_specs=[
            SMEM_WHOLE, whole(cells * 4, rays), whole(cells, rays), whole(3, rays),
            whole(6, S, 128), whole(16, HID), columns(HID), columns(HID),
        ],
        out_specs=(columns(HID), whole(HID + 16, HID)),
        scratch_shapes=[
            pltpu.VMEM((cells, 128), f32),
            pltpu.VMEM((samples // 8, 128), f32),
            pltpu.VMEM((HID, 16), bf16),
            pltpu.VMEM((HID + 16, HID), f32),
            pltpu.VMEM((16, HID), f32),
        ],
        compiler_params=params(),
        name="upper",
    )(idx, table, ranks, goal, shading, wide_misc, act_two, act_three)
    uppers = [grads_upper] + from_others(grads_upper)

    grads_lower = pl.pallas_call(
        lower_kernel,
        grid=(steps,),
        out_shape=shape((HID + 80, HID), bf16),
        in_specs=[
            whole(2, HID, HID), columns(ENC + 1), columns(HID), columns(HID), columns(HID),
        ],
        out_specs=whole(HID + 80, HID),
        scratch_shapes=[
            pltpu.VMEM((HID + 16, HID), f32),
            pltpu.VMEM((64, HID), f32),
        ],
        compiler_params=params(),
        cost_estimate=pl.CostEstimate(
            flops=7 * samples * HID * HID, bytes_accessed=26 * samples * HID // 4, transcendentals=0
        ),
        name="lower",
    )(wide_hid, feats, act_one, act_two, back_three)
    lowers = [grads_lower] + from_others(grads_lower)

    return pl.pallas_call(
        update_kernel,
        out_shape=(
            shape((1, ENC + 1, HID)), shape((1, 2, HID, HID)), shape((1, 2, HID)), shape((1, 4, HID)),
            shape(mom_in.shape), shape(mom_hid.shape), shape(mom_bias.shape), shape(mom_out.shape),
        ),
        in_specs=[SMEM_WHOLE] + [VMEM_WHOLE] * 21,
        out_specs=(VMEM_WHOLE,) * 8,
        scratch_shapes=[
            pltpu.VMEM((HID + 16, HID), f32),
            pltpu.VMEM((HID + 80, HID), f32),
        ],
        compiler_params=params(),
        name="update",
    )(idx, *uppers, *lowers, *highs, *states, wide_misc, mom_in, mom_hid, mom_bias, mom_out)


def solution(mesh):
    cells = mesh.shape["region"]
    inner = 8 if cells % 8 == 0 and cells > 8 else 2
    return jax.shard_map(
        functools.partial(body, inner),
        mesh=mesh,
        in_specs=(
            P("region", None, "batch"),
            P("region", "batch"),
            P("region", "batch"),
            P("batch", None),
            P(None, "batch"),
            P("region", "batch", None),
            P("region", None, "batch", None),
            P("region", None, "batch"),
            P("region", None, "batch"),
            P(None, "region", "batch", None),
            P(None, "region", None, "batch", None),
            P(None, "region", None, "batch"),
            P(None, "region", None, "batch"),
        ),
        out_specs=(
            P("region", None, None),
            P("region", None, None, None),
            P("region", None, None),
            P("region", None, None),
            P(None, "region", "batch", None),
            P(None, "region", None, "batch", None),
            P(None, "region", None, "batch"),
            P(None, "region", None, "batch"),
        ),
        check_vma=False,
    )
```

time: 312 us -> 93.7 us (0.30)
  blocking collectives: 151 us -> 8.52 us
  waiting for transfers between devices: 66.8 us -> 9.7 us
  matrix products: 42.9 us -> 0 us
  Pallas kernels: 0 us -> 33.7 us
  starting transfers between devices: 0.38 us -> 27.6 us
  between operations: 17.5 us -> 0.85 us
  other arithmetic: 14.4 us -> 1.9 us
  local copies, waits for them, and re-layouts: 18.4 us -> 9.74 us
    all_gather x9 -> x0, blocking collectives: 142 us -> none  [the longest x1 52.5 us: body(): table = lax.all_gather(summary, 'region', axis=0, tiled=True)]
    reduce_scatter x2 -> x0, waiting for transfers between devices: 49.8 us -> none  [the longest x1 25.5 us: body(): lax.psum_scatter(grads[1], 'batch', scatter_dimension=1, tiled=True)]
    dot_general x10 -> x0, matrix products: 37.2 us -> none  [the longest x3 12.1 us: contract_last(): lax.dot_general(left, right, (((1,), (1,)), ((), ())), preferred_element_...]
    pallas_call x0 -> x6, Pallas kernels: none -> 33.7 us  [the longest x1 9.44 us: body(): pl.pallas_call(forward_kernel, grid=(steps,), out_shape=(act, act, act, s...]
    ppermute x0 -> x12, starting transfers between devices: none -> 19.2 us  [from_others(): lax.ppermute(block, 'batch', [(i, (i + hop) % N_BATCH) for i in range(N_B...]
    unnamed x6 -> x0, waiting for transfers between devices: 17 us -> none
    psum x1 -> x0, blocking collectives: 8.88 us -> none  [body(): total_sq = lax.psum(local_sq, 'batch')]
    all_to_all x0 -> x1, blocking collectives: none -> 8.52 us  [body(): lax.all_to_all(jnp.broadcast_to(summary[None], (inner, 4, rays)), 'region...]
  transfers between devices with their start and end apart: 4 -> 13, of which waited for: 3 -> 3; matrix products, arithmetic and copies ran while one was open for 10% -> 4% of each run, Pallas kernels for 0% -> 22%
where the time goes in v1:
time: 93.7 us; the launch traced here: 92 us
  Pallas kernels  33.7 us (36%)
  starting transfers between devices  27.6 us (29%)
  local copies, waits for them, and re-layouts  9.74 us (10%)
  waiting for transfers between devices  9.7 us (10%)
  blocking collectives  8.52 us (9%)
  other arithmetic  1.9 us (2%)
    ppermute x12, starting transfers between devices, from_others(): lax.ppermute(block, 'batch', [(i, (i + hop) % N_BATCH) for i in range(N_B...  19.2 us
    pallas_call x1, Pallas kernels, body(): pl.pallas_call(forward_kernel, grid=(steps,), out_shape=(act, act, act, s...  9.44 us
    pallas_call x1, Pallas kernels, body(): pl.pallas_call(lower_kernel, grid=(steps,), out_shape=shape((HID + 80, HI...  9.37 us
    pallas_call x1, Pallas kernels, body(): pl.pallas_call(upper_kernel, grid=(steps,), out_shape=(act, shape((HID +...  9 us
    all_to_all x1, blocking collectives, body(): lax.all_to_all(jnp.broadcast_to(summary[None], (inner, 4, rays)), 'region...  8.52 us
    all_to_all x1, starting transfers between devices, body(): lax.all_to_all(jnp.broadcast_to(some[None], (outer, inner, 4, rays)), 're...  8.45 us
    ppermute x12, waiting for transfers between devices, from_others(): lax.ppermute(block, 'batch', [(i, (i + hop) % N_BATCH) for i in range(N_B...  7.03 us
    unnamed x32, local copies, waits for them, and re-layouts  6.95 us
  transfers between devices with their start and end apart: 13, of which 3 were waited for; matrix products, arithmetic and copies ran while one was open for 4% of the time, Pallas kernels for 22%

profile of v1, /device:TPU:2, one launch (start us, length us, event | category | flops | bytes accessed | tf_op | source)
XLA Modules:
  0.0 92.0 jit_solution(9178365327767918723)
XLA Ops:
  0.7 0.6 pad_add_fusion.idx
  1.2 1.7 %pack_weights.1.own.high_0 = bf16[160,256]{1,0:T(8,128)(2,1)} custom-call(s32[2]{0:T(128)} %pad_add_fusion.idx, f32[1,16,256]{2,1,0:T(8,128)} %w_in.3, f32[1,2,64,256]{3,2,1,0:T(8,128)} %w_hid.3, f32[1,2,64]{2,1,0:T(2,128)} %b_hid.1, f32[1,4,64]{2,1,0:T(4,128)} %w_out.3), custom_call_target="tpu_custom_call" | custom-call | tf_op jit(solution)/shard_map/pack_weights/pallas_call | solution.py:397
  2.9 1.6 %collective-permute-start = (bf16[160,256]{1,0:T(8,128)(2,1)}, bf16[160,256]{1,0:T(8,128)(2,1)S(1)}, u32[]{:S(2)}, u32[]{:S(2)}) collective-permute-start(bf16[160,256]{1,0:T(8,128)(2,1)} %pack_weights.1.own.high_0), channel_id=1, source_target_pairs={{0,1},{1,2},{2,3},{3,0},{4,5},{5,6},{6,7},{7,4},{8,9},{9,10},{10,1... | collective-permute-start | bytes 245768 | tf_op jit(solution)/shard_map/ppermute | solution.py:375
  4.5 2.9 %collective-permute-start.1 = (bf16[160,256]{1,0:T(8,128)(2,1)}, bf16[160,256]{1,0:T(8,128)(2,1)S(1)}, u32[]{:S(2)}, u32[]{:S(2)}) collective-permute-start(bf16[160,256]{1,0:T(8,128)(2,1)} %pack_weights.1.own.high_0), channel_id=1, source_target_pairs={{0,2},{1,3},{2,0},{3,1},{4,6},{5,7},{6,4},{7,5},{8,10},{9,11},{10,... | collective-permute-start | bytes 245768 | tf_op jit(solution)/shard_map/ppermute | solution.py:375
  7.4 1.3 %collective-permute-start.2 = (bf16[160,256]{1,0:T(8,128)(2,1)}, bf16[160,256]{1,0:T(8,128)(2,1)S(1)}, u32[]{:S(2)}, u32[]{:S(2)}) collective-permute-start(bf16[160,256]{1,0:T(8,128)(2,1)} %pack_weights.1.own.high_0), channel_id=1, source_target_pairs={{0,3},{1,0},{2,1},{3,2},{4,7},{5,4},{6,5},{7,6},{8,11},{9,8},{10,9... | collective-permute-start | bytes 245768 | tf_op jit(solution)/shard_map/ppermute | solution.py:375
  8.8 0.5 broadcast.7
  9.3 1.3 %reduce.3 = s32[128]{0:T(128)S(1)} reduce(s32[1,128]{1,0:T(1,128)} %param.15, s32[]{:T(128)} %broadcast.7), dimensions={0}, to_apply=%param.15.reduce_sub_computation.3 | reduce | bytes 1028 | tf_op args[2]
  10.6 0.1 reshape_squeeze.7
  10.7 0.1 copy.24
  10.8 0.1 reshape.36.counts
  10.9 1.3 %concatenate.3.feats = bf16[64,8192]{1,0:T(8,128)(2,1)S(1)} pad(bf16[63,8192]{1,0:T(8,128)(2,1)} %bitcast.12, bf16[]{:T(256)} %constant.10.clone.1), padding=0_1x0_0 | pad | bytes 2080770 | tf_op jit(solution)/shard_map/concatenate | solution.py:414
  12.2 0.0 collective-permute-done.1.from_two.high_2
  12.2 0.0 collective-permute-done.2.from_three.high_3
  12.3 0.9 copy-done.5
  13.1 0.8 copy-done.8
  13.9 0.7 copy-done.10
  14.6 9.4 %forward.1 = (bf16[256,8192]{1,0:T(8,128)(2,1)S(1)}, bf16[256,8192]{1,0:T(8,128)(2,1)}, bf16[256,8192]{1,0:T(8,128)(2,1)}, bf16[64,256]{1,0:T(8,128)(2,1)}, bf16...) custom-call(s32[2]{0:T(128)S(1)} %copy-done.10, ...), custom_call_target="tpu_custom_call" | custom-call | tf_op jit(solution)/shard_map/forward/pallas_call | solution.py:423
  24.0 2.0 %copy-done = bf16[256,8192]{1,0:T(8,128)(2,1)} copy-done((bf16[256,8192]{1,0:T(8,128)(2,1)}, bf16[256,8192]{1,0:T(8,128)(2,1)S(1)}, u32[]{:S(2)}) %copy-start) | copy-done | bytes 4194328
  26.0 8.5 %all_to_all.10 = f32[8,4,128]{2,1,0:T(4,128)S(1)} all-to-all(f32[8,4,128]{2,1,0:T(4,128)S(1)} %broadcast_in_dim.4), channel_id=1, replica_groups={{0,4,8,12,16,20,24,28},{32,36,40,44,48,52,56,60},{64,68,72,76,80,84,88,..., dimensions={0} | all-to-all | bytes 32768 | tf_op jit(solution)/shard_map/all_to_all | solution.py:449
  34.5 0.7 broadcast_in_dim.5
  35.2 8.5 %all-to-all-start.1 = ((f32[8,8,4,128]{3,2,1,0:T(4,128)}), f32[8,8,4,128]{3,2,1,0:T(4,128)S(1)}, u32[]{:S(2)}, u32[]{:S(2)}) async-start(f32[8,8,4,128]{3,2,1,0:T(4,128)} %broadcast_in_dim.5), calls=%async_computation.1 | async-start | bytes 262144 | tf_op jit(solution)/shard_map/all_to_all | solution.py:453
  43.6 1.9 %pack_state.1.state_0 = bf16[480,256]{1,0:T(8,128)(2,1)} custom-call(s32[2]{0:T(128)} %pad_add_fusion.idx, f32[1,16,256]{2,1,0:T(8,128)} %w_in.3, f32[1,2,64,256]{3,2,1,0:T(8,128)} %w_hid.3, f32[1,4,64]{2,1,0:T(4,128)} %w_out.3, f32[2,1,16,256]{3,2,1,0:T(8,128)} %mom_in.3, f32[2,1,2,64,256]{4,3,2,1,0:T(8,128)} %mom_hid.3, f32[2,1,2,64]{3,2,1,0:T(2,128)} %mom_bias.3, ...), custom_call_target="tpu_custom_call" | custom-call | tf_op jit(solution)/shard_map/pack_state/pallas_call | solution.py:405
  45.6 1.8 %collective-permute-start.10 = (bf16[480,256]{1,0:T(8,128)(2,1)}, bf16[480,256]{1,0:T(8,128)(2,1)S(1)}, u32[]{:S(2)}, u32[]{:S(2)}) collective-permute-start(bf16[480,256]{1,0:T(8,128)(2,1)} %pack_state.1.state_0), channel_id=1, source_target_pairs={{0,2},{1,3},{2,0},{3,1},{4,6},{5,7},{6,4},{7,5},{8,10},{9,11},{10,... | collective-permute-start | bytes 737288 | tf_op jit(solution)/shard_map/ppermute | solution.py:375
  47.4 1.5 %collective-permute-start.11 = (bf16[480,256]{1,0:T(8,128)(2,1)}, bf16[480,256]{1,0:T(8,128)(2,1)S(1)}, u32[]{:S(2)}, u32[]{:S(2)}) collective-permute-start(bf16[480,256]{1,0:T(8,128)(2,1)} %pack_state.1.state_0), channel_id=1, source_target_pairs={{0,3},{1,0},{2,1},{3,2},{4,7},{5,4},{6,5},{7,6},{8,11},{9,8},{10,9... | collective-permute-start | bytes 737288 | tf_op jit(solution)/shard_map/ppermute | solution.py:375
  48.9 0.5 collective-permute-start.9
  49.4 0.1 copy.25
  49.5 0.1 copy.26
  49.6 0.1 reshape.39.ranks
  49.7 0.1 reshape.40
  49.9 0.1 copy.27
  50.0 0.1 reshape.41.target
  50.0 2.7 %all-to-all-done.1 = f32[8,8,4,128]{3,2,1,0:T(4,128)S(1)} async-done(((f32[8,8,4,128]{3,2,1,0:T(4,128)}), f32[8,8,4,128]{3,2,1,0:T(4,128)S(1)}, u32[]{:S(2)}, u32[]{:S(2)}) %all-to-all-start.1) | async-done | bytes 131104 | tf_op jit(solution)/shard_map/all_to_all | solution.py:453
  52.7 9.0 %upper.1 = (bf16[256,8192]{1,0:T(8,128)(2,1)S(1)}, bf16[272,256]{1,0:T(8,128)(2,1)S(1)}) custom-call(s32[2]{0:T(128)S(1)} %copy-done.11, f32[256,128]{1,0:T(8,128)S(1)} %bitcast.10, s32[64,128]{1,0:T(8,128)S(1)} %reshape.39.ranks, f32[3,128]{1,0:T(4,128)S(1)} %reshape.41.target, f32[6,64,128]{2,1,0:T(8,128)S(1)} %get-tuple-element.18.shading, ...), custom_call_target="tpu_custom_call" | custom-call | tf_op jit(solution)/shard_map/upper/pallas_call | solution.py:458
  61.7 2.0 %copy-done.2 = bf16[256,8192]{1,0:T(8,128)(2,1)} copy-done((bf16[256,8192]{1,0:T(8,128)(2,1)}, bf16[256,8192]{1,0:T(8,128)(2,1)S(1)}, u32[]{:S(2)}) %copy-start.2) | copy-done | bytes 4194328
  63.8 0.7 collective-permute-start.3
  64.4 0.0 copy-start.7
  64.5 0.0 copy-start.9
  64.5 0.0 copy-start.12
  64.5 9.4 %lower.1.lower_0 = bf16[336,256]{1,0:T(8,128)(2,1)S(1)} custom-call(bf16[2,256,256]{2,1,0:T(8,128)(2,1)S(1)} %get-tuple-element.23.wide_hid, bf16[64,8192]{1,0:T(8,128)(2,1)S(1)} %concatenate.3.feats, bf16[256,8192]{1,0:T(8,128)(2,1)S(1)} %copy-done.1, bf16[256,8192]{1,0:T(8,128)(2,1)} %get-tuple-element.20.act_two, bf16[256,8192]{1,0:T(8,128)(2,1)} %copy-done.2), custom_call_target="tpu_custom_call" | custom-call | flops 3758096384 | bytes 13631488 | tf_op jit(solution)/shard_map/lower/pallas_call | solution.py:479
  73.9 1.2 %collective-permute-start.6 = (bf16[336,256]{1,0:T(8,128)(2,1)S(1)}, bf16[336,256]{1,0:T(8,128)(2,1)S(1)}, u32[]{:S(2)}, u32[]{:S(2)}) collective-permute-start(bf16[336,256]{1,0:T(8,128)(2,1)S(1)} %lower.1.lower_0), channel_id=1, source_target_pairs={{0,1},{1,2},{2,3},{3,0},{4,5},{5,6},{6,7},{7,4},{8,9},{9,10},{10,1... | collective-permute-start | bytes 516104 | tf_op jit(solution)/shard_map/ppermute | solution.py:375
  75.0 0.0 collective-permute-done.10.state_2
  75.0 2.9 %collective-permute-start.7 = (bf16[336,256]{1,0:T(8,128)(2,1)S(1)}, bf16[336,256]{1,0:T(8,128)(2,1)S(1)}, u32[]{:S(2)}, u32[]{:S(2)}) collective-permute-start(bf16[336,256]{1,0:T(8,128)(2,1)S(1)} %lower.1.lower_0), channel_id=1, source_target_pairs={{0,2},{1,3},{2,0},{3,1},{4,6},{5,7},{6,4},{7,5},{8,10},{9,11},{10,... | collective-permute-start | bytes 516104 | tf_op jit(solution)/shard_map/ppermute | solution.py:375
  78.0 1.8 %collective-permute-start.8 = (bf16[336,256]{1,0:T(8,128)(2,1)S(1)}, bf16[336,256]{1,0:T(8,128)(2,1)S(1)}, u32[]{:S(2)}, u32[]{:S(2)}) collective-permute-start(bf16[336,256]{1,0:T(8,128)(2,1)S(1)} %lower.1.lower_0), channel_id=1, source_target_pairs={{0,3},{1,0},{2,1},{3,2},{4,7},{5,4},{6,5},{7,6},{8,11},{9,8},{10,9... | collective-permute-start | bytes 516104 | tf_op jit(solution)/shard_map/ppermute | solution.py:375
  79.8 0.4 collective-permute-start.4
  80.1 2.6 %collective-permute-start.5 = (bf16[272,256]{1,0:T(8,128)(2,1)S(1)}, bf16[272,256]{1,0:T(8,128)(2,1)S(1)}, u32[]{:S(2)}, u32[]{:S(2)}) collective-permute-start(bf16[272,256]{1,0:T(8,128)(2,1)S(1)} %get-tuple-element.22.upper_0), channel_id=1, source_target_pairs={{0,3},{1,0},{2,1},{3,2},{4,7},{5,4},{6,5},{7,6},{8,11},{9,8},{10,9... | collective-permute-start | bytes 417800 | tf_op jit(solution)/shard_map/ppermute | solution.py:375
  82.7 4.1 %collective-permute-done.4.upper_2 = bf16[272,256]{1,0:T(8,128)(2,1)S(1)} collective-permute-done((bf16[272,256]{1,0:T(8,128)(2,1)S(1)}, bf16[272,256]{1,0:T(8,128)(2,1)S(1)}, u32[]{:S(2)}, u32[]{:S(2)}) %collective-permute-start.4) | collective-permute-done | bytes 139296 | tf_op jit(solution)/shard_map/ppermute | solution.py:375
  86.8 2.9 %collective-permute-done.5.upper_3 = bf16[272,256]{1,0:T(8,128)(2,1)S(1)} collective-permute-done((bf16[272,256]{1,0:T(8,128)(2,1)S(1)}, bf16[272,256]{1,0:T(8,128)(2,1)S(1)}, u32[]{:S(2)}, u32[]{:S(2)}) %collective-permute-start.5) | collective-permute-done | bytes 139296 | tf_op jit(solution)/shard_map/ppermute | solution.py:375
  89.8 2.3 %update.1 = (f32[1,64,256]{2,1,0:T(8,128)}, f32[1,2,256,256]{3,2,1,0:T(8,128)}, f32[1,2,256]{2,1,0:T(2,128)}, f32[1,4,256]{2,1,0:T(4,128)}, f32[2,1,16,256]{3,2,...) custom-call(s32[2]{0:T(128)S(1)} %copy-done.11, ...), custom_call_target="tpu_custom_call" | custom-call | tf_op jit(solution)/shard_map/update/pallas_call | solution.py:499
  (30 shorter events, 0.1 us)
Async XLA Ops:
  0.6 48.8 %copy-start.13 = (s32[128,64]{0,1:T(8,128)S(1)}, s32[128,64]{0,1:T(8,128)}, u32[]{:S(2)}) copy-start(s32[128,64]{0,1:T(8,128)} %param.16) | copy-start | bytes 98308
  0.6 49.1 %copy-start.14 = (f32[3,128]{1,0:T(4,128)S(1)}, f32[3,128]{1,0:T(4,128)}, u32[]{:S(2)}) copy-start(f32[3,128]{1,0:T(4,128)} %param.17) | copy-start | bytes 4612
  1.2 51.5 %copy-start.11 = (s32[2]{0:T(128)S(1)}, s32[2]{0:T(128)}, u32[]{:S(2)}) copy-start(s32[2]{0:T(128)} %pad_add_fusion.idx) | copy-start | bytes 28
  2.9 9.3 %collective-permute-start = (bf16[160,256]{1,0:T(8,128)(2,1)}, bf16[160,256]{1,0:T(8,128)(2,1)S(1)}, u32[]{:S(2)}, u32[]{:S(2)}) collective-permute-start(bf16[160,256]{1,0:T(8,128)(2,1)} %pack_weights.1.own.high_0), channel_id=1, source_target_pairs={{0,1},{1,2},{2,3},{3,0},{4,5},{5,6},{6,7},{7,4},{8,9},{9,10},{10,1... | collective-permute-start | bytes 245768 | tf_op jit(solution)/shard_map/ppermute | solution.py:375
  4.5 7.7 %collective-permute-start.1 = (bf16[160,256]{1,0:T(8,128)(2,1)}, bf16[160,256]{1,0:T(8,128)(2,1)S(1)}, u32[]{:S(2)}, u32[]{:S(2)}) collective-permute-start(bf16[160,256]{1,0:T(8,128)(2,1)} %pack_weights.1.own.high_0), channel_id=1, source_target_pairs={{0,2},{1,3},{2,0},{3,1},{4,6},{5,7},{6,4},{7,5},{8,10},{9,11},{10,... | collective-permute-start | bytes 245768 | tf_op jit(solution)/shard_map/ppermute | solution.py:375
  7.4 4.8 %collective-permute-start.2 = (bf16[160,256]{1,0:T(8,128)(2,1)}, bf16[160,256]{1,0:T(8,128)(2,1)S(1)}, u32[]{:S(2)}, u32[]{:S(2)}) collective-permute-start(bf16[160,256]{1,0:T(8,128)(2,1)} %pack_weights.1.own.high_0), channel_id=1, source_target_pairs={{0,3},{1,0},{2,1},{3,2},{4,7},{5,4},{6,5},{7,6},{8,11},{9,8},{10,9... | collective-permute-start | bytes 245768 | tf_op jit(solution)/shard_map/ppermute | solution.py:375
  12.3 0.9 copy-start.5
  13.1 0.8 copy-start.8
  13.9 0.7 copy-start.10
  24.0 2.0 %copy-start = (bf16[256,8192]{1,0:T(8,128)(2,1)}, bf16[256,8192]{1,0:T(8,128)(2,1)S(1)}, u32[]{:S(2)}) copy-start(bf16[256,8192]{1,0:T(8,128)(2,1)S(1)} %get-tuple-element.24.act_one) | copy-start | bytes 12582916
  35.2 17.5 %all-to-all-start.1 = ((f32[8,8,4,128]{3,2,1,0:T(4,128)}), f32[8,8,4,128]{3,2,1,0:T(4,128)S(1)}, u32[]{:S(2)}, u32[]{:S(2)}) async-start(f32[8,8,4,128]{3,2,1,0:T(4,128)} %broadcast_in_dim.5), calls=%async_computation.1 | async-start | bytes 262144 | tf_op jit(solution)/shard_map/all_to_all | solution.py:453
  45.6 29.5 %collective-permute-start.10 = (bf16[480,256]{1,0:T(8,128)(2,1)}, bf16[480,256]{1,0:T(8,128)(2,1)S(1)}, u32[]{:S(2)}, u32[]{:S(2)}) collective-permute-start(bf16[480,256]{1,0:T(8,128)(2,1)} %pack_state.1.state_0), channel_id=1, source_target_pairs={{0,2},{1,3},{2,0},{3,1},{4,6},{5,7},{6,4},{7,5},{8,10},{9,11},{10,... | collective-permute-start | bytes 737288 | tf_op jit(solution)/shard_map/ppermute | solution.py:375
  47.4 30.6 %collective-permute-start.11 = (bf16[480,256]{1,0:T(8,128)(2,1)}, bf16[480,256]{1,0:T(8,128)(2,1)S(1)}, u32[]{:S(2)}, u32[]{:S(2)}) collective-permute-start(bf16[480,256]{1,0:T(8,128)(2,1)} %pack_state.1.state_0), channel_id=1, source_target_pairs={{0,3},{1,0},{2,1},{3,2},{4,7},{5,4},{6,5},{7,6},{8,11},{9,8},{10,9... | collective-permute-start | bytes 737288 | tf_op jit(solution)/shard_map/ppermute | solution.py:375
  48.9 30.8 %collective-permute-start.9 = (bf16[480,256]{1,0:T(8,128)(2,1)}, bf16[480,256]{1,0:T(8,128)(2,1)S(1)}, u32[]{:S(2)}, u32[]{:S(2)}) collective-permute-start(bf16[480,256]{1,0:T(8,128)(2,1)} %pack_state.1.state_0), channel_id=1, source_target_pairs={{0,1},{1,2},{2,3},{3,0},{4,5},{5,6},{6,7},{7,4},{8,9},{9,10},{10,1... | collective-permute-start | bytes 737288 | tf_op jit(solution)/shard_map/ppermute | solution.py:375
  52.7 11.7 %copy-start.1 = (bf16[256,8192]{1,0:T(8,128)(2,1)S(1)}, bf16[256,8192]{1,0:T(8,128)(2,1)}, u32[]{:S(2)}) copy-start(bf16[256,8192]{1,0:T(8,128)(2,1)} %copy-done) | copy-start | bytes 12582916
  61.7 2.0 %copy-start.2 = (bf16[256,8192]{1,0:T(8,128)(2,1)}, bf16[256,8192]{1,0:T(8,128)(2,1)S(1)}, u32[]{:S(2)}) copy-start(bf16[256,8192]{1,0:T(8,128)(2,1)S(1)} %get-tuple-element.25.back_three) | copy-start | bytes 12582916
  63.8 16.4 %collective-permute-start.3 = (bf16[272,256]{1,0:T(8,128)(2,1)S(1)}, bf16[272,256]{1,0:T(8,128)(2,1)S(1)}, u32[]{:S(2)}, u32[]{:S(2)}) collective-permute-start(bf16[272,256]{1,0:T(8,128)(2,1)S(1)} %get-tuple-element.22.upper_0), channel_id=1, source_target_pairs={{0,1},{1,2},{2,3},{3,0},{4,5},{5,6},{6,7},{7,4},{8,9},{9,10},{10,1... | collective-permute-start | bytes 417800 | tf_op jit(solution)/shard_map/ppermute | solution.py:375
  64.4 25.3 %copy-start.3 = (f32[2,1,2,64,256]{4,3,2,1,0:T(8,128)S(1)}, f32[2,1,2,64,256]{4,3,2,1,0:T(8,128)}, u32[]{:S(2)}) copy-start(f32[2,1,2,64,256]{4,3,2,1,0:T(8,128)} %mom_hid.3) | copy-start | bytes 786436
  64.4 25.3 %copy-start.4 = (bf16[480,256]{1,0:T(8,128)(2,1)S(1)}, bf16[480,256]{1,0:T(8,128)(2,1)}, u32[]{:S(2)}) copy-start(bf16[480,256]{1,0:T(8,128)(2,1)} %pack_state.1.state_0) | copy-start | bytes 737284
  64.4 25.3 %copy-start.6 = (bf16[160,256]{1,0:T(8,128)(2,1)S(1)}, bf16[160,256]{1,0:T(8,128)(2,1)}, u32[]{:S(2)}) copy-start(bf16[160,256]{1,0:T(8,128)(2,1)} %pack_weights.1.own.high_0) | copy-start | bytes 245764
  64.4 25.3 %copy-start.7 = (f32[2,1,16,256]{3,2,1,0:T(8,128)S(1)}, f32[2,1,16,256]{3,2,1,0:T(8,128)}, u32[]{:S(2)}) copy-start(f32[2,1,16,256]{3,2,1,0:T(8,128)} %mom_in.3) | copy-start | bytes 98308
  64.5 25.3 %copy-start.9 = (f32[2,1,4,64]{3,2,1,0:T(4,128)S(1)}, f32[2,1,4,64]{3,2,1,0:T(4,128)}, u32[]{:S(2)}) copy-start(f32[2,1,4,64]{3,2,1,0:T(4,128)} %mom_out.3) | copy-start | bytes 6148
  64.5 25.3 %copy-start.12 = (f32[2,1,2,64]{3,2,1,0:T(2,128)S(1)}, f32[2,1,2,64]{3,2,1,0:T(2,128)}, u32[]{:S(2)}) copy-start(f32[2,1,2,64]{3,2,1,0:T(2,128)} %mom_bias.3) | copy-start | bytes 3076
  73.9 15.8 %collective-permute-start.6 = (bf16[336,256]{1,0:T(8,128)(2,1)S(1)}, bf16[336,256]{1,0:T(8,128)(2,1)S(1)}, u32[]{:S(2)}, u32[]{:S(2)}) collective-permute-start(bf16[336,256]{1,0:T(8,128)(2,1)S(1)} %lower.1.lower_0), channel_id=1, source_target_pairs={{0,1},{1,2},{2,3},{3,0},{4,5},{5,6},{6,7},{7,4},{8,9},{9,10},{10,1... | collective-permute-start | bytes 516104 | tf_op jit(solution)/shard_map/ppermute | solution.py:375
  75.0 14.6 %collective-permute-start.7 = (bf16[336,256]{1,0:T(8,128)(2,1)S(1)}, bf16[336,256]{1,0:T(8,128)(2,1)S(1)}, u32[]{:S(2)}, u32[]{:S(2)}) collective-permute-start(bf16[336,256]{1,0:T(8,128)(2,1)S(1)} %lower.1.lower_0), channel_id=1, source_target_pairs={{0,2},{1,3},{2,0},{3,1},{4,6},{5,7},{6,4},{7,5},{8,10},{9,11},{10,... | collective-permute-start | bytes 516104 | tf_op jit(solution)/shard_map/ppermute | solution.py:375
  78.0 11.7 %collective-permute-start.8 = (bf16[336,256]{1,0:T(8,128)(2,1)S(1)}, bf16[336,256]{1,0:T(8,128)(2,1)S(1)}, u32[]{:S(2)}, u32[]{:S(2)}) collective-permute-start(bf16[336,256]{1,0:T(8,128)(2,1)S(1)} %lower.1.lower_0), channel_id=1, source_target_pairs={{0,3},{1,0},{2,1},{3,2},{4,7},{5,4},{6,5},{7,6},{8,11},{9,8},{10,9... | collective-permute-start | bytes 516104 | tf_op jit(solution)/shard_map/ppermute | solution.py:375
  79.8 7.1 %collective-permute-start.4 = (bf16[272,256]{1,0:T(8,128)(2,1)S(1)}, bf16[272,256]{1,0:T(8,128)(2,1)S(1)}, u32[]{:S(2)}, u32[]{:S(2)}) collective-permute-start(bf16[272,256]{1,0:T(8,128)(2,1)S(1)} %get-tuple-element.22.upper_0), channel_id=1, source_target_pairs={{0,2},{1,3},{2,0},{3,1},{4,6},{5,7},{6,4},{7,5},{8,10},{9,11},{10,... | collective-permute-start | bytes 417800 | tf_op jit(solution)/shard_map/ppermute | solution.py:375
  80.1 9.6 %collective-permute-start.5 = (bf16[272,256]{1,0:T(8,128)(2,1)S(1)}, bf16[272,256]{1,0:T(8,128)(2,1)S(1)}, u32[]{:S(2)}, u32[]{:S(2)}) collective-permute-start(bf16[272,256]{1,0:T(8,128)(2,1)S(1)} %get-tuple-element.22.upper_0), channel_id=1, source_target_pairs={{0,3},{1,0},{2,1},{3,2},{4,7},{5,4},{6,5},{7,6},{8,11},{9,8},{10,9... | collective-permute-start | bytes 417800 | tf_op jit(solution)/shard_map/ppermute | solution.py:375

commit v2 on v1

v2 whole, which is shorter than its diff:
```python
import functools

import jax
import jax.numpy as jnp
from jax import lax
from jax.experimental import pallas as pl
from jax.experimental.pallas import tpu as pltpu
from jax.sharding import PartitionSpec as P

ENC = 63
HID = 256
S = 64
N_BATCH = 4
CHUNK = 4096
MIB = 1 << 20
LIMIT = 24

beta_first = 0.9
beta_second = 0.95
learn_rate = 0.01
norm_eps = 1e-06
adam_eps = 1e-08

f32 = jnp.float32
bf16 = jnp.bfloat16

ROWS_IN = HID // 16
ROWS_HID = HID // N_BATCH
MISC = ROWS_IN + 2 * ROWS_HID
BLOCK = MISC + 16


def dot(left, right):
    return lax.dot_general(left, right, (((1,), (0,)), ((), ())), preferred_element_type=f32)


def dot_last(left, right):
    return lax.dot_general(left, right, (((1,), (1,)), ((), ())), preferred_element_type=f32)


def at_own_lanes(rows, own):
    source = lax.broadcasted_iota(jnp.int32, (ROWS_HID, HID), 0)
    lane = lax.broadcasted_iota(jnp.int32, (ROWS_HID, HID), 1)
    place = jnp.where(lane == source + own * ROWS_HID, 1.0, 0.0).astype(bf16)
    return dot(rows, place).astype(bf16)


def pack_weights(w_in, w_hid, b_hid, w_out, out):
    out[0:ROWS_IN, :] = w_in[0].astype(bf16)
    for layer in range(2):
        at = ROWS_IN + layer * ROWS_HID
        out[at : at + ROWS_HID, :] = w_hid[0, layer].astype(bf16)
    bias = b_hid[0]
    top = bias.astype(bf16).astype(f32)
    middle = (bias - top).astype(bf16).astype(f32)
    rest = bias - top - middle
    rows = jnp.concatenate(
        [w_out[0], top, middle, rest, jnp.zeros((6, ROWS_HID), f32)], axis=0
    ).astype(bf16)
    out[MISC:BLOCK, :] = at_own_lanes(rows, lax.axis_index("batch"))


def by_lane(rows):
    ray = lax.broadcasted_iota(jnp.int32, (128, 128), 0)
    lane = lax.broadcasted_iota(jnp.int32, (128, 128), 1)
    place = jnp.where(ray == jnp.where(lane < S, 2 * lane, 2 * (lane - S) + 1), 1.0, 0.0)
    return dot(rows.astype(bf16), place.astype(bf16))


def prepare_kernel(
    w_in, w_hid, w_out, mom_in, mom_hid, mom_bias, mom_out, spacing, counts, ranks, target,
    out, gaps, live_counts, order, goal,
):
    own = lax.axis_index("batch")

    def low(value):
        return (value - value.astype(bf16).astype(f32)).astype(bf16)

    out[0:ROWS_IN, :] = low(w_in[0])
    for layer in range(2):
        at = ROWS_IN + layer * ROWS_HID
        out[at : at + ROWS_HID, :] = low(w_hid[0, layer])
    rest = w_out[0] - w_out[0].astype(bf16).astype(f32)
    rows = jnp.concatenate([rest, jnp.zeros((12, ROWS_HID), f32)], axis=0)
    out[MISC:BLOCK, :] = at_own_lanes(rows.astype(bf16), own)
    for moment in range(2):
        base = BLOCK * (moment + 1)
        out[base : base + ROWS_IN, :] = mom_in[moment, 0].astype(bf16)
        for layer in range(2):
            at = base + ROWS_IN + layer * ROWS_HID
            out[at : at + ROWS_HID, :] = mom_hid[moment, 0, layer].astype(bf16)
        rows = jnp.concatenate(
            [mom_out[moment, 0], mom_bias[moment, 0], jnp.zeros((10, ROWS_HID), f32)], axis=0
        )
        out[base + MISC : base + BLOCK, :] = at_own_lanes(rows.astype(bf16), own)

    gaps[...] = turn(spacing[...])
    order[...] = by_lane(ranks[...].astype(f32))
    top = target[...].astype(bf16).astype(f32)
    middle = (target[...] - top).astype(bf16).astype(f32)
    rest = target[...] - top - middle
    number = counts[...].astype(f32)
    moved = by_lane(jnp.concatenate([top, middle, rest, number, jnp.zeros((6, 128), f32)], axis=0))
    goal[...] = moved[0:3] + moved[3:6] + moved[6:9]
    live_counts[...] = moved[9:10]


def turn(rows):
    turned = jnp.concatenate([rows, rows], axis=0).T
    lane = lax.broadcasted_iota(jnp.int32, (S, 2 * S), 1)
    return jnp.where(lane < S, turned[:S], turned[S:])


def running_sum(values):
    row = lax.broadcasted_iota(jnp.int32, values.shape, 0)
    step = 1
    while step < S:
        values = values + jnp.where(row >= step, pltpu.roll(values, step, 0), 0.0)
        step *= 2
    return values


def one_minus_exp(depth):
    small = depth * (1.0 - depth * (0.5 - depth * (1.0 / 6.0 - depth * (1.0 / 24.0 - depth * (1.0 / 120.0)))))
    return jnp.where(depth < 0.1, small, 1.0 - jnp.exp(-depth))


def rectified(value):
    return jnp.maximum(value.astype(bf16), jnp.zeros((), bf16))


def sigmoid(value):
    return 1.0 / (1.0 + jnp.exp(-value))


def forward_kernel(
    own, from_one, from_two, from_three, feats, gaps, counts,
    act_one, act_two, act_three, wide_hid, wide_misc, shading, summary,
    wide_in, turned_in, turned_hid, bias_cols, out_rows, heads_rows,
):
    me = lax.axis_index("batch")
    misc = jnp.zeros((16, HID), f32)
    for back, block in enumerate((own, from_one, from_two, from_three)):
        owner = lax.rem(me + N_BATCH - back, N_BATCH)
        wide_in[pl.ds(pl.multiple_of(owner * ROWS_IN, 16), ROWS_IN), :] = block[0:ROWS_IN, :]
        for layer in range(2):
            at = ROWS_IN + layer * ROWS_HID
            wide_hid[layer, pl.ds(pl.multiple_of(owner * ROWS_HID, 16), ROWS_HID), :] = block[
                at : at + ROWS_HID, :
            ]
        misc = misc + block[MISC:BLOCK, :].astype(f32)
    wide_misc[...] = misc
    turned_in[...] = wide_in[...].astype(f32).T.astype(bf16)
    for layer in range(2):
        turned_hid[layer] = wide_hid[layer].astype(f32).T.astype(bf16)
    bias = misc[4:6] + misc[6:8] + misc[8:10]
    bias_cols[...] = jnp.concatenate([bias, jnp.zeros((6, HID), f32)], axis=0).T
    row = lax.broadcasted_iota(jnp.int32, (16, HID), 0)
    out_rows[...] = jnp.where(row < 4, misc, 0.0).astype(bf16)

    @pl.loop(0, feats.shape[1] // CHUNK)
    def _(step):
        columns = pl.ds(pl.multiple_of(step * CHUNK, CHUNK), CHUNK)
        one = rectified(dot(turned_in[...], feats[:, columns]))
        act_one[:, columns] = one
        two = rectified(dot(turned_hid[0], one) + bias_cols[:, 0:1])
        act_two[:, columns] = two
        three = rectified(dot(turned_hid[1], two) + bias_cols[:, 1:2])
        act_three[:, columns] = three
        heads = dot(out_rows[...], three)
        for tile in range(CHUNK // 128):
            at = pl.multiple_of((step * (CHUNK // 128) + tile) * 8, 8)
            heads_rows[pl.ds(at, 8), :] = heads[0:8, tile * 128 : (tile + 1) * 128]

    density = turn(heads_rows[pl.ds(0, S, stride=8), :])
    slot = lax.broadcasted_iota(jnp.int32, (S, 128), 0).astype(f32)
    live_gap = jnp.where(slot < counts[...], gaps[...], 0.0)
    soft = jnp.maximum(density, 0.0) + jnp.log1p(jnp.exp(-jnp.abs(density)))
    depth = soft * live_gap
    total = running_sum(depth)
    weight = jnp.exp(-(total - depth)) * one_minus_exp(depth)
    for channel in range(3):
        colour = sigmoid(turn(heads_rows[pl.ds(channel + 1, S, stride=8), :]))
        shading[channel] = colour
        summary[channel : channel + 1, :] = jnp.sum(weight * colour, axis=0, keepdims=True)
    summary[3:4, :] = -total[S - 1 : S]
    shading[3] = weight
    shading[4] = jnp.exp(-total)
    shading[5] = live_gap * sigmoid(density)


def composite(table, ranks, target, shading, reach_rows, grad_rows):
    cells = ranks.shape[0]
    order = ranks[...]
    own = lax.axis_index("region")
    prefix = jnp.zeros((cells, 128), f32)
    for cell in range(cells):
        prefix = prefix + jnp.where(
            ranks[cell : cell + 1, :] < order, table[4 * cell + 3 : 4 * cell + 4, :], 0.0
        )
    reach = jnp.exp(prefix)
    reach_rows[...] = reach
    own_reach = reach_rows[pl.ds(own, 1), :]
    later = order > ranks[pl.ds(own, 1), :]
    grad_seg = []
    grad_log = jnp.zeros((1, 128), f32)
    for channel in range(3):
        lit = reach * table[pl.ds(channel, cells, stride=4), :]
        grad_colour = 2.0 * (jnp.sum(lit, axis=0, keepdims=True) - target[channel : channel + 1, :])
        behind = jnp.sum(jnp.where(later, lit, 0.0), axis=0, keepdims=True)
        grad_log = grad_log + grad_colour * behind
        grad_seg.append(own_reach * grad_colour)
    weight = shading[3]
    emit = grad_seg[0] * shading[0] + grad_seg[1] * shading[1] + grad_seg[2] * shading[2]
    carried = emit * weight
    running = running_sum(carried)
    after = running[S - 1 : S] - running
    grad_depth = emit * shading[4] - after - grad_log
    grad_rows[...] = jnp.zeros(grad_rows.shape, f32)
    grad_rows[pl.ds(0, S, stride=16), :] = turn(grad_depth * shading[5])
    for channel in range(3):
        colour = shading[channel]
        shade = grad_seg[channel] * weight * colour * (1.0 - colour)
        grad_rows[pl.ds(channel + 1, S, stride=16), :] = turn(shade)


def masked(act, back):
    return jnp.where(act > 0, back.astype(bf16), jnp.zeros((), bf16))


def backward_kernel(
    table, ranks, target, shading, wide_hid, wide_misc, feats, act_one, act_two, act_three,
    even, odd,
    reach_rows, grad_rows, out_cols, sum_third, sum_second, sum_first, sum_out,
):
    composite(table, ranks, target, shading, reach_rows, grad_rows)
    row = lax.broadcasted_iota(jnp.int32, (16, HID), 0)
    out_cols[...] = jnp.where(row < 4, wide_misc[...], 0.0).T.astype(bf16)
    for total in (sum_third, sum_second, sum_first, sum_out):
        total[...] = jnp.zeros(total.shape, f32)

    @pl.loop(0, feats.shape[1] // CHUNK)
    def _(step):
        columns = pl.ds(pl.multiple_of(step * CHUNK, CHUNK), CHUNK)
        tiles = CHUNK // 128
        heads = jnp.concatenate(
            [
                grad_rows[pl.ds(pl.multiple_of((step * tiles + tile) * 16, 16), 16), :]
                for tile in range(tiles)
            ],
            axis=1,
        ).astype(bf16)
        ones = jnp.ones((16, CHUNK), bf16)
        one, two, three = act_one[:, columns], act_two[:, columns], act_three[:, columns]
        back_three = masked(three, dot(out_cols[...], heads))
        sum_out[...] += dot_last(heads, three)
        back_two = masked(two, dot(wide_hid[1], back_three))
        sum_third[...] += dot_last(jnp.concatenate([two, ones], axis=0), back_three)
        back_one = masked(one, dot(wide_hid[0], back_two))
        sum_second[...] += dot_last(jnp.concatenate([one, ones], axis=0), back_two)
        sum_first[...] += dot_last(feats[:, columns], back_one)

    misc = jnp.where(row < 4, sum_out[...], 0.0)
    misc = misc + jnp.where(row == 4, sum_second[HID : HID + 16, :], 0.0)
    misc = misc + jnp.where(row == 5, sum_third[HID : HID + 16, :], 0.0)
    even[0:HID, :] = sum_third[0:HID, :].astype(bf16)
    even[HID : HID + 32, :] = sum_first[0:32, :].astype(bf16)
    even[HID + 32 : HID + 48, :] = misc.astype(bf16)
    odd[0:HID, :] = sum_second[0:HID, :].astype(bf16)
    odd[HID : HID + 32, :] = sum_first[32:64, :].astype(bf16)


def pair_kernel(even, even_other, odd, odd_other, even_sum, odd_sum):
    even_sum[...] = (even[...].astype(f32) + even_other[...].astype(f32)).astype(bf16)
    odd_sum[...] = (odd[...].astype(f32) + odd_other[...].astype(f32)).astype(bf16)


def adam(grad, first, second, scale):
    scaled = grad * scale
    first = beta_first * first + (1.0 - beta_first) * scaled
    second = beta_second * second + (1.0 - beta_second) * scaled * scaled
    return first, second, learn_rate * first / (jnp.sqrt(second) + adam_eps)


def update_kernel(
    even, even_other, odd, odd_other,
    high_0, high_1, high_2, high_3,
    state_0, state_1, state_2, state_3,
    wide_misc, mom_in, mom_hid, mom_bias, mom_out,
    new_in, new_hid, new_bias, new_out,
    out_in, out_hid, out_bias, out_out,
    upper, lower, first_rows,
):
    me = lax.axis_index("batch")
    param_count = (ENC + 1) * HID + 2 * HID * HID + 6 * HID
    upper[...] = even[...].astype(f32) + even_other[...].astype(f32)
    lower[...] = odd[...].astype(f32) + odd_other[...].astype(f32)
    first_rows[0:32, :] = upper[HID : HID + 32, :]
    first_rows[32:64, :] = lower[HID : HID + 32, :]
    grad_misc = upper[HID + 32 : HID + 48, :]
    squares = jnp.sum(upper[...] * upper[...], axis=0, keepdims=True) + jnp.sum(
        lower[...] * lower[...], axis=0, keepdims=True
    )
    total = jnp.sum(squares, axis=1, keepdims=True)
    scale = lax.rsqrt(total / param_count + norm_eps)

    def fresh(grad, high, state, at, rows):
        _, _, change = adam(
            grad,
            state[BLOCK + at : BLOCK + at + rows, :].astype(f32),
            state[2 * BLOCK + at : 2 * BLOCK + at + rows, :].astype(f32),
            scale,
        )
        value = high[at : at + rows, :].astype(f32) + state[at : at + rows, :].astype(f32)
        return value - change

    highs = (high_0, high_1, high_2, high_3)
    states = (state_0, state_1, state_2, state_3)
    low_misc = jnp.zeros((16, HID), f32)
    first_misc = jnp.zeros((16, HID), f32)
    second_misc = jnp.zeros((16, HID), f32)
    for back in range(N_BATCH):
        owner = lax.rem(me + N_BATCH - back, N_BATCH)
        high, state = highs[back], states[back]
        hid = pl.ds(pl.multiple_of(owner * ROWS_HID, 16), ROWS_HID)
        new_hid[0, 0, hid, :] = fresh(lower[hid, :], high, state, ROWS_IN, ROWS_HID)
        new_hid[0, 1, hid, :] = fresh(upper[hid, :], high, state, ROWS_IN + ROWS_HID, ROWS_HID)
        first = pl.ds(pl.multiple_of(owner * ROWS_IN, 16), ROWS_IN)
        grad = first_rows[first, :]
        new_in[0, first, :] = fresh(grad, high, state, 0, ROWS_IN)
        low_misc = low_misc + state[MISC:BLOCK, :].astype(f32)
        first_misc = first_misc + state[BLOCK + MISC : 2 * BLOCK, :].astype(f32)
        second_misc = second_misc + state[2 * BLOCK + MISC : 3 * BLOCK, :].astype(f32)

    _, _, change = adam(grad_misc, first_misc, second_misc, scale)
    weights = wide_misc[...]
    new_out[0] = weights[0:4] + low_misc[0:4] - change[0:4]
    new_bias[0] = weights[4:6] + weights[6:8] + weights[8:10] - change[4:6]

    own = pl.ds(pl.multiple_of(me * ROWS_HID, 16), ROWS_HID)
    for layer, grads in ((0, lower), (1, upper)):
        moments = adam(grads[own, :], mom_hid[0, 0, layer], mom_hid[1, 0, layer], scale)
        out_hid[0, 0, layer] = moments[0]
        out_hid[1, 0, layer] = moments[1]
    grad = first_rows[pl.ds(pl.multiple_of(me * ROWS_IN, 16), ROWS_IN), :]
    moments = adam(grad, mom_in[0, 0], mom_in[1, 0], scale)
    out_in[0, 0] = moments[0]
    out_in[1, 0] = moments[1]
    own_misc = jnp.zeros((16, ROWS_HID), f32)
    for owner in range(N_BATCH):
        part = grad_misc[:, owner * ROWS_HID : (owner + 1) * ROWS_HID]
        own_misc = own_misc + jnp.where(me == owner, part, 0.0)
    moments = adam(own_misc[0:4], mom_out[0, 0], mom_out[1, 0], scale)
    out_out[0, 0] = moments[0]
    out_out[1, 0] = moments[1]
    moments = adam(own_misc[4:6], mom_bias[0, 0], mom_bias[1, 0], scale)
    out_bias[0, 0] = moments[0]
    out_bias[1, 0] = moments[1]


def fetched(kernel, fetch, outs):
    def run(*refs):
        sources, rest = refs[:fetch], refs[fetch : fetch + outs]
        copies, sem = refs[fetch + outs : -1], refs[-1]
        moves = [pltpu.make_async_copy(a, b, sem.at[i]) for i, (a, b) in enumerate(zip(sources, copies))]
        for move in moves:
            move.start()
        for move in moves:
            move.wait()
        kernel(*copies, *rest)

    return run


def call_on_hbm(kernel, outs, name, *arrays):
    outs = outs if isinstance(outs, tuple) else (outs,)
    return pl.pallas_call(
        fetched(kernel, len(arrays), len(outs)),
        out_shape=outs,
        in_specs=[pl.BlockSpec(memory_space=pltpu.HBM)] * len(arrays),
        scratch_shapes=[pltpu.VMEM(a.shape, a.dtype) for a in arrays]
        + [pltpu.SemaphoreType.DMA((len(arrays),))],
        compiler_params=pltpu.CompilerParams(vmem_limit_bytes=60 * MIB),
        name=name,
    )(*arrays)


def call(kernel, outs, scratch=(), name=None):
    return pl.pallas_call(
        kernel,
        out_shape=outs,
        scratch_shapes=[pltpu.VMEM(*s) for s in scratch],
        compiler_params=pltpu.CompilerParams(vmem_limit_bytes=LIMIT * MIB),
        name=name,
    )


def from_others(block):
    return [
        lax.ppermute(block, "batch", [(i, (i + hop) % N_BATCH) for i in range(N_BATCH)])
        for hop in (1, 2, 3)
    ]


def swapped(block, first):
    pairs = [(0, 1), (2, 3)] if first else [(1, 2), (3, 0)]
    return lax.ppermute(block, "batch", pairs + [(j, i) for i, j in pairs])


def held(dims, dtype=f32):
    return pltpu.VMEM(dims, dtype)


def shape(dims, dtype=f32):
    return jax.ShapeDtypeStruct(dims, dtype)


def body(
    inner,
    features, spacing, counts, depth_rank, target,
    w_in, w_hid, b_hid, w_out,
    mom_in, mom_hid, mom_bias, mom_out,
):
    samples = features.shape[2]
    rays = samples // S
    cells = depth_rank.shape[1]
    outer = cells // inner

    (block,) = call_on_hbm(
        pack_weights, held((BLOCK, HID), bf16), "pack_weights", w_in, w_hid, b_hid, w_out
    )
    block, spacing = lax.optimization_barrier((block, spacing))
    highs = [block] + from_others(block)
    state, gaps, live_counts, ranks, goal = call_on_hbm(
        prepare_kernel,
        (
            held((3 * BLOCK, HID), bf16), held((S, rays)), held((1, rays)), held((cells, rays)),
            held((3, rays)),
        ),
        "prepare",
        w_in, w_hid, w_out, mom_in, mom_hid, mom_bias, mom_out,
        spacing.reshape(rays // 2, 2 * S), counts, depth_rank.T, target,
    )
    state, highs[1] = lax.optimization_barrier((state, highs[1]))
    states = [state] + from_others(state)
    feats = jnp.concatenate([features[0], jnp.ones((1, samples), bf16)], axis=0)

    act = held((HID, samples), bf16)
    act_one, act_two, act_three, wide_hid, wide_misc, shading, summary = call(
        forward_kernel,
        (
            act, act, act, held((2, HID, HID), bf16),
            held((16, HID)), held((6, S, 128)), held((4, rays)),
        ),
        scratch=[
            ((ENC + 1, HID), bf16), ((HID, ENC + 1), bf16), ((2, HID, HID), bf16), ((HID, 8), f32),
            ((16, HID), bf16), ((samples // 16, 128), f32),
        ],
        name="forward",
    )(*highs, feats, gaps, live_counts)

    summary, *states = lax.optimization_barrier((summary, *states))
    near = [[z * inner + i for i in range(inner)] for z in range(outer)]
    far = [[z * inner + i for z in range(outer)] for i in range(inner)]
    some = lax.all_to_all(
        jnp.broadcast_to(summary[None], (inner, 4, rays)), "region", 0, 0,
        axis_index_groups=near, tiled=True,
    )
    table = lax.all_to_all(
        jnp.broadcast_to(some[None], (outer, inner, 4, rays)), "region", 0, 0,
        axis_index_groups=far, tiled=True,
    ).reshape(cells * 4, rays)

    even, odd = call(
        backward_kernel,
        (held((HID + 48, HID), bf16), held((HID + 32, HID), bf16)),
        scratch=[
            ((cells, 128), f32), ((samples // 8, 128), f32), ((HID, 16), bf16), ((HID + 16, HID), f32),
            ((HID + 16, HID), f32), ((64, HID), f32), ((16, HID), f32),
        ],
        name="backward",
    )(table, ranks, goal, shading, wide_hid, wide_misc, feats, act_one, act_two, act_three)
    even, odd = call(
        pair_kernel, (held(even.shape, bf16), held(odd.shape, bf16)), name="pair"
    )(even, swapped(even, True), odd, swapped(odd, False))

    return call(
        update_kernel,
        (
            shape((1, ENC + 1, HID)), shape((1, 2, HID, HID)), shape((1, 2, HID)), shape((1, 4, HID)),
            shape(mom_in.shape), shape(mom_hid.shape), shape(mom_bias.shape), shape(mom_out.shape),
        ),
        scratch=[((HID + 48, HID), f32), ((HID + 32, HID), f32), ((64, HID), f32)],
        name="update",
    )(
        even, swapped(even, False), odd, swapped(odd, True),
        *highs, *states, wide_misc, mom_in, mom_hid, mom_bias, mom_out,
    )


def solution(mesh):
    cells = mesh.shape["region"]
    inner = 8 if cells % 8 == 0 and cells > 8 else 2
    return jax.shard_map(
        functools.partial(body, inner),
        mesh=mesh,
        in_specs=(
            P("region", None, "batch"),
            P("region", "batch"),
            P("region", "batch"),
            P("batch", None),
            P(None, "batch"),
            P("region", "batch", None),
            P("region", None, "batch", None),
            P("region", None, "batch"),
            P("region", None, "batch"),
            P(None, "region", "batch", None),
            P(None, "region", None, "batch", None),
            P(None, "region", None, "batch"),
            P(None, "region", None, "batch"),
        ),
        out_specs=(
            P("region", None, None),
            P("region", None, None, None),
            P("region", None, None),
            P("region", None, None),
            P(None, "region", "batch", None),
            P(None, "region", None, "batch", None),
            P(None, "region", None, "batch"),
            P(None, "region", None, "batch"),
        ),
        check_vma=False,
    )
```

time: 93.7 us -> 78.8 us (0.84); the launches traced: 92 us -> 78.4 us
  blocking collectives: 8.52 us -> 25.9 us
  Pallas kernels: 33.7 us -> 17.3 us
  starting transfers between devices: 27.6 us -> 12.9 us
  waiting for transfers between devices: 9.7 us -> 20.3 us
  local copies, waits for them, and re-layouts: 9.74 us -> 1.34 us
  other arithmetic: 1.9 us -> 0 us
    all_to_all x0 -> x1, blocking collectives: none -> 17.3 us  [body(): lax.all_to_all(jnp.broadcast_to(some[None], (outer, inner, 4, rays)), 're...]
    pallas_call x6, Pallas kernels: 33.7 us -> 17.3 us  [the longest x1 8.73 us: body(): call(backward_kernel, (held((HID + 48, HID), bf16), held((HID + 32, HID),...]
    ppermute x12 -> x6, starting transfers between devices: 19.2 us -> 9.01 us  [from_others(): lax.ppermute(block, 'batch', [(i, (i + hop) % N_BATCH) for i in range(N_B...]
    ppermute x0 -> x4, waiting for transfers between devices: none -> 9.57 us  [swapped(): return lax.ppermute(block, 'batch', pairs + [(j, i) for i, j in pairs])]
    all_to_all x1 -> x0, starting transfers between devices: 8.45 us -> none  [body(): lax.all_to_all(jnp.broadcast_to(some[None], (outer, inner, 4, rays)), 're...]
    unnamed x32 -> x8, local copies, waits for them, and re-layouts: 6.95 us -> 0.01 us
    ppermute x0 -> x4, starting transfers between devices: none -> 3.9 us  [swapped(): return lax.ppermute(block, 'batch', pairs + [(j, i) for i, j in pairs])]
    ppermute x12 -> x6, waiting for transfers between devices: 7.03 us -> 10.7 us  [from_others(): lax.ppermute(block, 'batch', [(i, (i + hop) % N_BATCH) for i in range(N_B...]
  transfers between devices with their start and end apart: 13 -> 10, of which waited for: 3 -> 5; matrix products, arithmetic and copies ran while one was open for 4% -> 2% of each run, Pallas kernels for 22% -> 7%
where the time goes in v2:
time: 78.8 us; the launch traced here: 78.4 us
  blocking collectives  25.9 us (33%)
  waiting for transfers between devices  20.3 us (26%)
  Pallas kernels  17.3 us (22%)
  starting transfers between devices  12.9 us (16%)
  local copies, waits for them, and re-layouts  1.34 us (2%)
    all_to_all x1, blocking collectives, body(): lax.all_to_all(jnp.broadcast_to(some[None], (outer, inner, 4, rays)), 're...  17.3 us
    ppermute x6, waiting for transfers between devices, from_others(): lax.ppermute(block, 'batch', [(i, (i + hop) % N_BATCH) for i in range(N_B...  10.7 us
    ppermute x4, waiting for transfers between devices, swapped(): return lax.ppermute(block, 'batch', pairs + [(j, i) for i, j in pairs])  9.57 us
    ppermute x6, starting transfers between devices, from_others(): lax.ppermute(block, 'batch', [(i, (i + hop) % N_BATCH) for i in range(N_B...  9.01 us
    pallas_call x1, Pallas kernels, body(): call(backward_kernel, (held((HID + 48, HID), bf16), held((HID + 32, HID),...  8.73 us
    all_to_all x1, blocking collectives, body(): lax.all_to_all(jnp.broadcast_to(summary[None], (inner, 4, rays)), 'region...  8.53 us
    pallas_call x1, Pallas kernels, body(): call(forward_kernel, (act, act, act, held((2, HID, HID), bf16), held((16,...  4.46 us
    ppermute x4, starting transfers between devices, swapped(): return lax.ppermute(block, 'batch', pairs + [(j, i) for i, j in pairs])  3.9 us
  transfers between devices with their start and end apart: 10, of which 5 were waited for; matrix products, arithmetic and copies ran while one was open for 2% of the time, Pallas kernels for 7%

profile of v2, /device:TPU:2, one launch (start us, length us, event | category | flops | bytes accessed | tf_op | source)
XLA Modules:
  0.0 78.4 jit_solution(6548433581990605651)
XLA Ops:
  0.6 1.1 %pack_weights.1.own.high_0 = bf16[160,256]{1,0:T(8,128)(2,1)S(1)} custom-call(f32[1,16,256]{2,1,0:T(8,128)} %refs_0_.3, f32[1,2,64,256]{3,2,1,0:T(8,128)} %refs_1_.3, f32[1,2,64]{2,1,0:T(2,128)} %refs_2_.2, f32[1,4,64]{2,1,0:T(4,128)} %refs_2_.3), custom_call_target="tpu_custom_call" | custom-call | tf_op jit(solution)/shard_map/pack_weights/pallas_call | solution.py:377
  1.7 1.7 %collective-permute-start = (bf16[160,256]{1,0:T(8,128)(2,1)S(1)}, bf16[160,256]{1,0:T(8,128)(2,1)S(1)}, u32[]{:S(2)}, u32[]{:S(2)}) collective-permute-start(bf16[160,256]{1,0:T(8,128)(2,1)S(1)} %pack_weights.1.own.high_0), channel_id=1, source_target_pairs={{0,1},{1,2},{2,3},{3,0},{4,5},{5,6},{6,7},{7,4},{8,9},{9,10},{10,1... | collective-permute-start | bytes 245768 | tf_op jit(solution)/shard_map/ppermute | solution.py:400
  3.4 1.4 %prepare.1 = (bf16[480,256]{1,0:T(8,128)(2,1)S(1)}, f32[64,128]{1,0:T(8,128)S(1)}, f32[1,128]{1,0:T(1,128)S(1)}, f32[64,128]{1,0:T(8,128)S(1)}, f32[3,128]{1,0:T(4,128)S(1)}) custom-call(f32[1,16,256]{2,1,0:T(8,128)} %refs_0_.3, f32[1,2,64,256]{3,2,1,0:T(8,128)} %refs_1_.3, f32[1,4,64]{2,1,0:T(4,128)} %refs_2_.3, f32[2,1,16,256]{3,2,1,0:T(8,128)} %mom_in.1, ...), custom_call_target="tpu_custom_call" | custom-call | tf_op jit(solution)/shard_map/prepare/pallas_call | solution.py:377
  4.8 2.7 %collective-permute-done.from_one.high_1 = bf16[160,256]{1,0:T(8,128)(2,1)S(1)} collective-permute-done((bf16[160,256]{1,0:T(8,128)(2,1)S(1)}, bf16[160,256]{1,0:T(8,128)(2,1)S(1)}, u32[]{:S(2)}, u32[]{:S(2)}) %collective-permute-start) | collective-permute-done | bytes 81952 | tf_op jit(solution)/shard_map/ppermute | solution.py:400
  7.5 1.8 %collective-permute-start.5 = (bf16[480,256]{1,0:T(8,128)(2,1)S(1)}, bf16[480,256]{1,0:T(8,128)(2,1)S(1)}, u32[]{:S(2)}, u32[]{:S(2)}) collective-permute-start(bf16[480,256]{1,0:T(8,128)(2,1)S(1)} %get-tuple-element.54.state_0), channel_id=1, source_target_pairs={{0,3},{1,0},{2,1},{3,2},{4,7},{5,4},{6,5},{7,6},{8,11},{9,8},{10,9... | collective-permute-start | bytes 737288 | tf_op jit(solution)/shard_map/ppermute | solution.py:400
  9.3 0.6 collective-permute-start.4
  9.9 1.0 %collective-permute-start.3 = (bf16[480,256]{1,0:T(8,128)(2,1)S(1)}, bf16[480,256]{1,0:T(8,128)(2,1)S(1)}, u32[]{:S(2)}, u32[]{:S(2)}) collective-permute-start(bf16[480,256]{1,0:T(8,128)(2,1)S(1)} %get-tuple-element.54.state_0), channel_id=1, source_target_pairs={{0,1},{1,2},{2,3},{3,0},{4,5},{5,6},{6,7},{7,4},{8,9},{9,10},{10,1... | collective-permute-start | bytes 737288 | tf_op jit(solution)/shard_map/ppermute | solution.py:400
  10.9 2.3 %collective-permute-start.2 = (bf16[160,256]{1,0:T(8,128)(2,1)S(1)}, bf16[160,256]{1,0:T(8,128)(2,1)S(1)}, u32[]{:S(2)}, u32[]{:S(2)}) collective-permute-start(bf16[160,256]{1,0:T(8,128)(2,1)S(1)} %pack_weights.1.own.high_0), channel_id=1, source_target_pairs={{0,3},{1,0},{2,1},{3,2},{4,7},{5,4},{6,5},{7,6},{8,11},{9,8},{10,9... | collective-permute-start | bytes 245768 | tf_op jit(solution)/shard_map/ppermute | solution.py:400
  13.1 1.7 %collective-permute-start.1 = (bf16[160,256]{1,0:T(8,128)(2,1)S(1)}, bf16[160,256]{1,0:T(8,128)(2,1)S(1)}, u32[]{:S(2)}, u32[]{:S(2)}) collective-permute-start(bf16[160,256]{1,0:T(8,128)(2,1)S(1)} %pack_weights.1.own.high_0), channel_id=1, source_target_pairs={{0,2},{1,3},{2,0},{3,1},{4,6},{5,7},{6,4},{7,5},{8,10},{9,11},{10,... | collective-permute-start | bytes 245768 | tf_op jit(solution)/shard_map/ppermute | solution.py:400
  14.8 1.3 %concatenate.3.feats = bf16[64,8192]{1,0:T(8,128)(2,1)S(1)} pad(bf16[63,8192]{1,0:T(8,128)(2,1)} %bitcast.5, bf16[]{:T(256)} %constant.0.clone.1), padding=0_1x0_0 | pad | bytes 2080770 | tf_op jit(solution)/shard_map/concatenate | solution.py:446
  16.1 6.0 %collective-permute-done.2.from_three.high_3 = bf16[160,256]{1,0:T(8,128)(2,1)S(1)} collective-permute-done((bf16[160,256]{1,0:T(8,128)(2,1)S(1)}, bf16[160,256]{1,0:T(8,128)(2,1)S(1)}, u32[]{:S(2)}, u32[]{:S(2)}) %collective-permute-start.2) | collective-permute-done | bytes 81952 | tf_op jit(solution)/shard_map/ppermute | solution.py:400
  22.1 2.0 %collective-permute-done.1.from_two.high_2 = bf16[160,256]{1,0:T(8,128)(2,1)S(1)} collective-permute-done((bf16[160,256]{1,0:T(8,128)(2,1)S(1)}, bf16[160,256]{1,0:T(8,128)(2,1)S(1)}, u32[]{:S(2)}, u32[]{:S(2)}) %collective-permute-start.1) | collective-permute-done | bytes 81952 | tf_op jit(solution)/shard_map/ppermute | solution.py:400
  24.1 4.5 %forward.1 = (bf16[256,8192]{1,0:T(8,128)(2,1)S(1)}, bf16[256,8192]{1,0:T(8,128)(2,1)S(1)}, bf16[256,8192]{1,0:T(8,128)(2,1)S(1)}, bf16[2,256,256]{2,1,0:T(8,128...) custom-call(bf16[160,256]{1,0:T(8,128)(2,1)S(1)} %pack_weights.1.own.high_0, ...), custom_call_target="tpu_custom_call" | custom-call | tf_op jit(solution)/shard_map/forward/pallas_call | solution.py:449
  28.6 0.0 collective-permute-done.5.state_3
  28.6 0.0 collective-permute-done.4.state_2
  28.6 0.0 collective-permute-done.3.state_1
  28.6 8.5 %all_to_all.10 = f32[8,4,128]{2,1,0:T(4,128)S(1)} all-to-all(f32[8,4,128]{2,1,0:T(4,128)S(1)} %broadcast_in_dim.4), channel_id=1, replica_groups={{0,4,8,12,16,20,24,28},{32,36,40,44,48,52,56,60},{64,68,72,76,80,84,88,..., dimensions={0} | all-to-all | bytes 32768 | tf_op jit(solution)/shard_map/all_to_all | solution.py:465
  37.2 17.3 %all_to_all.11 = f32[8,8,4,128]{3,2,1,0:T(4,128)S(1)} all-to-all(f32[8,8,4,128]{3,2,1,0:T(4,128)S(1)} %broadcast_in_dim.5), channel_id=1, replica_groups={{0,32,64,96,128,160,192,224},{4,36,68,100,132,164,196,228},{8,40,72,104..., dimensions={0} | all-to-all | bytes 262144 | tf_op jit(solution)/shard_map/all_to_all | solution.py:469
  54.5 0.0 copy-start
  54.5 0.0 copy-start.1
  54.5 0.0 copy-start.2
  54.5 0.0 copy-start.3
  54.5 8.7 %backward.1 = (bf16[304,256]{1,0:T(8,128)(2,1)S(1)}, bf16[288,256]{1,0:T(8,128)(2,1)S(1)}) custom-call(f32[256,128]{1,0:T(8,128)S(1)} %bitcast.4, f32[64,128]{1,0:T(8,128)S(1)} %get-tuple-element.42.ranks, f32[3,128]{1,0:T(4,128)S(1)} %get-tuple-element.43.target, f32[6,64,128]{2,1,0:T(8,128)S(1)} %get-tuple-element.44.shading, ...), custom_call_target="tpu_custom_call" | custom-call | tf_op jit(solution)/shard_map/backward/pallas_call | solution.py:474
  63.3 0.1 collective-permute-start.6
  63.4 1.7 %collective-permute-start.7 = (bf16[288,256]{1,0:T(8,128)(2,1)S(1)}, bf16[288,256]{1,0:T(8,128)(2,1)S(1)}, u32[]{:S(2)}, u32[]{:S(2)}) collective-permute-start(bf16[288,256]{1,0:T(8,128)(2,1)S(1)} %get-tuple-element.51.odd), channel_id=1, source_target_pairs={{1,2},{3,0},{2,1},{0,3},{5,6},{7,4},{6,5},{4,7},{9,10},{11,8},{10,... | collective-permute-start | bytes 442376 | tf_op jit(solution)/shard_map/ppermute | solution.py:407
  65.2 4.7 %collective-permute-done.7.odd_other = bf16[288,256]{1,0:T(8,128)(2,1)S(1)} collective-permute-done((bf16[288,256]{1,0:T(8,128)(2,1)S(1)}, bf16[288,256]{1,0:T(8,128)(2,1)S(1)}, u32[]{:S(2)}, u32[]{:S(2)}) %collective-permute-start.7) | collective-permute-done | bytes 147488 | tf_op jit(solution)/shard_map/ppermute | solution.py:407
  69.8 0.0 collective-permute-done.6.even_other
  69.8 0.1 pair.1
  69.9 1.8 %collective-permute-start.8 = (bf16[304,256]{1,0:T(8,128)(2,1)S(1)}, bf16[304,256]{1,0:T(8,128)(2,1)S(1)}, u32[]{:S(2)}, u32[]{:S(2)}) collective-permute-start(bf16[304,256]{1,0:T(8,128)(2,1)S(1)} %get-tuple-element.52.even), channel_id=1, source_target_pairs={{1,2},{3,0},{2,1},{0,3},{5,6},{7,4},{6,5},{4,7},{9,10},{11,8},{10,... | collective-permute-start | bytes 466952 | tf_op jit(solution)/shard_map/ppermute | solution.py:407
  71.7 0.2 collective-permute-start.9
  71.9 4.9 %collective-permute-done.9.odd_other = bf16[288,256]{1,0:T(8,128)(2,1)S(1)} collective-permute-done((bf16[288,256]{1,0:T(8,128)(2,1)S(1)}, bf16[288,256]{1,0:T(8,128)(2,1)S(1)}, u32[]{:S(2)}, u32[]{:S(2)}) %collective-permute-start.9) | collective-permute-done | bytes 147488 | tf_op jit(solution)/shard_map/ppermute | solution.py:407
  76.8 0.0 collective-permute-done.8.even_other
  76.8 0.0 copy-done
  76.8 0.0 copy-done.1
  76.8 0.0 copy-done.2
  76.8 0.0 copy-done.3
  76.9 1.6 %update.1 = (f32[1,64,256]{2,1,0:T(8,128)}, f32[1,2,256,256]{3,2,1,0:T(8,128)}, f32[1,2,256]{2,1,0:T(2,128)}, f32[1,4,256]{2,1,0:T(4,128)}, f32[2,1,16,256]{3,2,...) custom-call(bf16[304,256]{1,0:T(8,128)(2,1)S(1)} %get-tuple-element.52.even, ...), custom_call_target="tpu_custom_call" | custom-call | tf_op jit(solution)/shard_map/update/pallas_call | solution.py:487
  (2 shorter events, 0.0 us)
Async XLA Ops:
  1.7 5.7 %collective-permute-start = (bf16[160,256]{1,0:T(8,128)(2,1)S(1)}, bf16[160,256]{1,0:T(8,128)(2,1)S(1)}, u32[]{:S(2)}, u32[]{:S(2)}) collective-permute-start(bf16[160,256]{1,0:T(8,128)(2,1)S(1)} %pack_weights.1.own.high_0), channel_id=1, source_target_pairs={{0,1},{1,2},{2,3},{3,0},{4,5},{5,6},{6,7},{7,4},{8,9},{9,10},{10,1... | collective-permute-start | bytes 245768 | tf_op jit(solution)/shard_map/ppermute | solution.py:400
  7.5 21.1 %collective-permute-start.5 = (bf16[480,256]{1,0:T(8,128)(2,1)S(1)}, bf16[480,256]{1,0:T(8,128)(2,1)S(1)}, u32[]{:S(2)}, u32[]{:S(2)}) collective-permute-start(bf16[480,256]{1,0:T(8,128)(2,1)S(1)} %get-tuple-element.54.state_0), channel_id=1, source_target_pairs={{0,3},{1,0},{2,1},{3,2},{4,7},{5,4},{6,5},{7,6},{8,11},{9,8},{10,9... | collective-permute-start | bytes 737288 | tf_op jit(solution)/shard_map/ppermute | solution.py:400
  9.3 19.3 %collective-permute-start.4 = (bf16[480,256]{1,0:T(8,128)(2,1)S(1)}, bf16[480,256]{1,0:T(8,128)(2,1)S(1)}, u32[]{:S(2)}, u32[]{:S(2)}) collective-permute-start(bf16[480,256]{1,0:T(8,128)(2,1)S(1)} %get-tuple-element.54.state_0), channel_id=1, source_target_pairs={{0,2},{1,3},{2,0},{3,1},{4,6},{5,7},{6,4},{7,5},{8,10},{9,11},{10,... | collective-permute-start | bytes 737288 | tf_op jit(solution)/shard_map/ppermute | solution.py:400
  9.9 18.7 %collective-permute-start.3 = (bf16[480,256]{1,0:T(8,128)(2,1)S(1)}, bf16[480,256]{1,0:T(8,128)(2,1)S(1)}, u32[]{:S(2)}, u32[]{:S(2)}) collective-permute-start(bf16[480,256]{1,0:T(8,128)(2,1)S(1)} %get-tuple-element.54.state_0), channel_id=1, source_target_pairs={{0,1},{1,2},{2,3},{3,0},{4,5},{5,6},{6,7},{7,4},{8,9},{9,10},{10,1... | collective-permute-start | bytes 737288 | tf_op jit(solution)/shard_map/ppermute | solution.py:400
  10.9 11.3 %collective-permute-start.2 = (bf16[160,256]{1,0:T(8,128)(2,1)S(1)}, bf16[160,256]{1,0:T(8,128)(2,1)S(1)}, u32[]{:S(2)}, u32[]{:S(2)}) collective-permute-start(bf16[160,256]{1,0:T(8,128)(2,1)S(1)} %pack_weights.1.own.high_0), channel_id=1, source_target_pairs={{0,3},{1,0},{2,1},{3,2},{4,7},{5,4},{6,5},{7,6},{8,11},{9,8},{10,9... | collective-permute-start | bytes 245768 | tf_op jit(solution)/shard_map/ppermute | solution.py:400
  13.1 11.0 %collective-permute-start.1 = (bf16[160,256]{1,0:T(8,128)(2,1)S(1)}, bf16[160,256]{1,0:T(8,128)(2,1)S(1)}, u32[]{:S(2)}, u32[]{:S(2)}) collective-permute-start(bf16[160,256]{1,0:T(8,128)(2,1)S(1)} %pack_weights.1.own.high_0), channel_id=1, source_target_pairs={{0,2},{1,3},{2,0},{3,1},{4,6},{5,7},{6,4},{7,5},{8,10},{9,11},{10,... | collective-permute-start | bytes 245768 | tf_op jit(solution)/shard_map/ppermute | solution.py:400
  54.5 22.3 %copy-start = (f32[2,1,2,64,256]{4,3,2,1,0:T(8,128)S(1)}, f32[2,1,2,64,256]{4,3,2,1,0:T(8,128)}, u32[]{:S(2)}) copy-start(f32[2,1,2,64,256]{4,3,2,1,0:T(8,128)} %mom_hid.1) | copy-start | bytes 786436
  54.5 22.3 %copy-start.1 = (f32[2,1,16,256]{3,2,1,0:T(8,128)S(1)}, f32[2,1,16,256]{3,2,1,0:T(8,128)}, u32[]{:S(2)}) copy-start(f32[2,1,16,256]{3,2,1,0:T(8,128)} %mom_in.1) | copy-start | bytes 98308
  54.5 22.3 %copy-start.2 = (f32[2,1,4,64]{3,2,1,0:T(4,128)S(1)}, f32[2,1,4,64]{3,2,1,0:T(4,128)}, u32[]{:S(2)}) copy-start(f32[2,1,4,64]{3,2,1,0:T(4,128)} %mom_out.1) | copy-start | bytes 6148
  54.5 22.3 %copy-start.3 = (f32[2,1,2,64]{3,2,1,0:T(2,128)S(1)}, f32[2,1,2,64]{3,2,1,0:T(2,128)}, u32[]{:S(2)}) copy-start(f32[2,1,2,64]{3,2,1,0:T(2,128)} %mom_bias.1) | copy-start | bytes 3076
  63.3 6.5 %collective-permute-start.6 = (bf16[304,256]{1,0:T(8,128)(2,1)S(1)}, bf16[304,256]{1,0:T(8,128)(2,1)S(1)}, u32[]{:S(2)}, u32[]{:S(2)}) collective-permute-start(bf16[304,256]{1,0:T(8,128)(2,1)S(1)} %get-tuple-element.50.even), channel_id=1, source_target_pairs={{0,1},{2,3},{1,0},{3,2},{4,5},{6,7},{5,4},{7,6},{8,9},{10,11},{9,8... | collective-permute-start | bytes 466952 | tf_op jit(solution)/shard_map/ppermute | solution.py:407
  63.4 6.4 %collective-permute-start.7 = (bf16[288,256]{1,0:T(8,128)(2,1)S(1)}, bf16[288,256]{1,0:T(8,128)(2,1)S(1)}, u32[]{:S(2)}, u32[]{:S(2)}) collective-permute-start(bf16[288,256]{1,0:T(8,128)(2,1)S(1)} %get-tuple-element.51.odd), channel_id=1, source_target_pairs={{1,2},{3,0},{2,1},{0,3},{5,6},{7,4},{6,5},{4,7},{9,10},{11,8},{10,... | collective-permute-start | bytes 442376 | tf_op jit(solution)/shard_map/ppermute | solution.py:407
  69.9 6.9 %collective-permute-start.8 = (bf16[304,256]{1,0:T(8,128)(2,1)S(1)}, bf16[304,256]{1,0:T(8,128)(2,1)S(1)}, u32[]{:S(2)}, u32[]{:S(2)}) collective-permute-start(bf16[304,256]{1,0:T(8,128)(2,1)S(1)} %get-tuple-element.52.even), channel_id=1, source_target_pairs={{1,2},{3,0},{2,1},{0,3},{5,6},{7,4},{6,5},{4,7},{9,10},{11,8},{10,... | collective-permute-start | bytes 466952 | tf_op jit(solution)/shard_map/ppermute | solution.py:407
  71.7 5.1 %collective-permute-start.9 = (bf16[288,256]{1,0:T(8,128)(2,1)S(1)}, bf16[288,256]{1,0:T(8,128)(2,1)S(1)}, u32[]{:S(2)}, u32[]{:S(2)}) collective-permute-start(bf16[288,256]{1,0:T(8,128)(2,1)S(1)} %get-tuple-element.53.odd), channel_id=1, source_target_pairs={{0,1},{2,3},{1,0},{3,2},{4,5},{6,7},{5,4},{7,6},{8,9},{10,11},{9,8... | collective-permute-start | bytes 442376 | tf_op jit(solution)/shard_map/ppermute | solution.py:407

commit v3 on v2

--- a/solution.py
+++ b/solution.py
@@ -441,9 +441,9 @@
         w_in, w_hid, w_out, mom_in, mom_hid, mom_bias, mom_out,
         spacing.reshape(rays // 2, 2 * S), counts, depth_rank.T, target,
     )
-    state, highs[1] = lax.optimization_barrier((state, highs[1]))
+    feats = jnp.concatenate([features[0], jnp.ones((1, samples), bf16)], axis=0)
+    state, feats, *highs[1:] = lax.optimization_barrier((state, feats, *highs[1:]))
     states = [state] + from_others(state)
-    feats = jnp.concatenate([features[0], jnp.ones((1, samples), bf16)], axis=0)
 
     act = held((HID, samples), bf16)
     act_one, act_two, act_three, wide_hid, wide_misc, shading, summary = call(
@@ -459,13 +459,13 @@
         name="forward",
     )(*highs, feats, gaps, live_counts)
 
-    summary, *states = lax.optimization_barrier((summary, *states))
     near = [[z * inner + i for i in range(inner)] for z in range(outer)]
     far = [[z * inner + i for z in range(outer)] for i in range(inner)]
     some = lax.all_to_all(
         jnp.broadcast_to(summary[None], (inner, 4, rays)), "region", 0, 0,
         axis_index_groups=near, tiled=True,
     )
+    some, *states = lax.optimization_barrier((some, *states))
     table = lax.all_to_all(
         jnp.broadcast_to(some[None], (outer, inner, 4, rays)), "region", 0, 0,
         axis_index_groups=far, tiled=True,

time: 78.8 us -> 71.6 us (0.909)
  waiting for transfers between devices: 20.3 us -> 11.7 us
  starting transfers between devices: 12.9 us -> 14.3 us
    ppermute x6, waiting for transfers between devices: 10.7 us -> 2.88 us  [from_others(): lax.ppermute(block, 'batch', [(i, (i + hop) % N_BATCH) for i in range(N_B...]
    ppermute x4, starting transfers between devices: 3.9 us -> 7.28 us  [swapped(): return lax.ppermute(block, 'batch', pairs + [(j, i) for i, j in pairs])]
    ppermute x6, starting transfers between devices: 9.01 us -> 6.98 us  [from_others(): lax.ppermute(block, 'batch', [(i, (i + hop) % N_BATCH) for i in range(N_B...]
  transfers between devices with their start and end apart: 10 -> 10, of which waited for: 5 -> 4; matrix products, arithmetic and copies ran while one was open for 2% -> 2% of each run, Pallas kernels for 7% -> 8%
where the time goes in v3:
time: 71.6 us; the launch traced here: 71.2 us
  blocking collectives  25.9 us (36%)
  Pallas kernels  17.3 us (24%)
  starting transfers between devices  14.3 us (20%)
  waiting for transfers between devices  11.7 us (16%)
  local copies, waits for them, and re-layouts  1.34 us (2%)
  between operations  0.74 us (1%)
    all_to_all x1, blocking collectives, body(): lax.all_to_all(jnp.broadcast_to(some[None], (outer, inner, 4, rays)), 're...  17.3 us
    ppermute x4, waiting for transfers between devices, swapped(): return lax.ppermute(block, 'batch', pairs + [(j, i) for i, j in pairs])  8.83 us
    pallas_call x1, Pallas kernels, body(): call(backward_kernel, (held((HID + 48, HID), bf16), held((HID + 32, HID),...  8.73 us
    all_to_all x1, blocking collectives, body(): lax.all_to_all(jnp.broadcast_to(summary[None], (inner, 4, rays)), 'region...  8.53 us
    ppermute x4, starting transfers between devices, swapped(): return lax.ppermute(block, 'batch', pairs + [(j, i) for i, j in pairs])  7.28 us
    ppermute x6, starting transfers between devices, from_others(): lax.ppermute(block, 'batch', [(i, (i + hop) % N_BATCH) for i in range(N_B...  6.98 us
    pallas_call x1, Pallas kernels, body(): call(forward_kernel, (act, act, act, held((2, HID, HID), bf16), held((16,...  4.47 us
    ppermute x6, waiting for transfers between devices, from_others(): lax.ppermute(block, 'batch', [(i, (i + hop) % N_BATCH) for i in range(N_B...  2.88 us
  transfers between devices with their start and end apart: 10, of which 4 were waited for; matrix products, arithmetic and copies ran while one was open for 2% of the time, Pallas kernels for 8%

profile of v3, /device:TPU:2, one launch (start us, length us, event | category | flops | bytes accessed | tf_op | source)
XLA Modules:
  0.0 71.2 jit_solution(8204689331448425996)
XLA Ops:
  0.6 1.1 %pack_weights.1.own.high_0 = bf16[160,256]{1,0:T(8,128)(2,1)S(1)} custom-call(f32[1,16,256]{2,1,0:T(8,128)} %refs_0_.3, f32[1,2,64,256]{3,2,1,0:T(8,128)} %refs_1_.3, f32[1,2,64]{2,1,0:T(2,128)} %refs_2_.2, f32[1,4,64]{2,1,0:T(4,128)} %refs_2_.3), custom_call_target="tpu_custom_call" | custom-call | tf_op jit(solution)/shard_map/pack_weights/pallas_call | solution.py:377
  1.7 3.1 %collective-permute-start.2 = (bf16[160,256]{1,0:T(8,128)(2,1)S(1)}, bf16[160,256]{1,0:T(8,128)(2,1)S(1)}, u32[]{:S(2)}, u32[]{:S(2)}) collective-permute-start(bf16[160,256]{1,0:T(8,128)(2,1)S(1)} %pack_weights.1.own.high_0), channel_id=1, source_target_pairs={{0,3},{1,0},{2,1},{3,2},{4,7},{5,4},{6,5},{7,6},{8,11},{9,8},{10,9... | collective-permute-start | bytes 245768 | tf_op jit(solution)/shard_map/ppermute | solution.py:400
  4.8 0.6 collective-permute-start.1
  5.5 1.0 %collective-permute-start = (bf16[160,256]{1,0:T(8,128)(2,1)S(1)}, bf16[160,256]{1,0:T(8,128)(2,1)S(1)}, u32[]{:S(2)}, u32[]{:S(2)}) collective-permute-start(bf16[160,256]{1,0:T(8,128)(2,1)S(1)} %pack_weights.1.own.high_0), channel_id=1, source_target_pairs={{0,1},{1,2},{2,3},{3,0},{4,5},{5,6},{6,7},{7,4},{8,9},{9,10},{10,1... | collective-permute-start | bytes 245768 | tf_op jit(solution)/shard_map/ppermute | solution.py:400
  6.4 1.3 %concatenate.3.feats = bf16[64,8192]{1,0:T(8,128)(2,1)S(1)} pad(bf16[63,8192]{1,0:T(8,128)(2,1)} %bitcast.5, bf16[]{:T(256)} %constant.0.clone.1), padding=0_1x0_0 | pad | bytes 2080770 | tf_op jit(solution)/shard_map/concatenate | solution.py:444
  7.7 1.4 %prepare.1 = (bf16[480,256]{1,0:T(8,128)(2,1)S(1)}, f32[64,128]{1,0:T(8,128)S(1)}, f32[1,128]{1,0:T(1,128)S(1)}, f32[64,128]{1,0:T(8,128)S(1)}, f32[3,128]{1,0:T(4,128)S(1)}) custom-call(f32[1,16,256]{2,1,0:T(8,128)} %refs_0_.3, f32[1,2,64,256]{3,2,1,0:T(8,128)} %refs_1_.3, f32[1,4,64]{2,1,0:T(4,128)} %refs_2_.3, f32[2,1,16,256]{3,2,1,0:T(8,128)} %mom_in.1, ...), custom_call_target="tpu_custom_call" | custom-call | tf_op jit(solution)/shard_map/prepare/pallas_call | solution.py:377
  9.1 0.0 collective-permute-done.2.from_three.high_3
  9.1 2.0 %collective-permute-done.1.from_two.high_2 = bf16[160,256]{1,0:T(8,128)(2,1)S(1)} collective-permute-done((bf16[160,256]{1,0:T(8,128)(2,1)S(1)}, bf16[160,256]{1,0:T(8,128)(2,1)S(1)}, u32[]{:S(2)}, u32[]{:S(2)}) %collective-permute-start.1) | collective-permute-done | bytes 81952 | tf_op jit(solution)/shard_map/ppermute | solution.py:400
  11.2 0.8 %collective-permute-done.from_one.high_1 = bf16[160,256]{1,0:T(8,128)(2,1)S(1)} collective-permute-done((bf16[160,256]{1,0:T(8,128)(2,1)S(1)}, bf16[160,256]{1,0:T(8,128)(2,1)S(1)}, u32[]{:S(2)}, u32[]{:S(2)}) %collective-permute-start) | collective-permute-done | bytes 81952 | tf_op jit(solution)/shard_map/ppermute | solution.py:400
  12.0 0.6 collective-permute-start.5
  12.6 0.6 collective-permute-start.4
  13.2 1.1 %collective-permute-start.3 = (bf16[480,256]{1,0:T(8,128)(2,1)S(1)}, bf16[480,256]{1,0:T(8,128)(2,1)S(1)}, u32[]{:S(2)}, u32[]{:S(2)}) collective-permute-start(bf16[480,256]{1,0:T(8,128)(2,1)S(1)} %get-tuple-element.60.state_0), channel_id=1, source_target_pairs={{0,1},{1,2},{2,3},{3,0},{4,5},{5,6},{6,7},{7,4},{8,9},{9,10},{10,1... | collective-permute-start | bytes 737288 | tf_op jit(solution)/shard_map/ppermute | solution.py:400
  14.3 4.5 %forward.1 = (bf16[256,8192]{1,0:T(8,128)(2,1)S(1)}, bf16[256,8192]{1,0:T(8,128)(2,1)S(1)}, bf16[256,8192]{1,0:T(8,128)(2,1)S(1)}, bf16[2,256,256]{2,1,0:T(8,128...) custom-call(bf16[160,256]{1,0:T(8,128)(2,1)S(1)} %pack_weights.1.own.high_0, ...), custom_call_target="tpu_custom_call" | custom-call | tf_op jit(solution)/shard_map/forward/pallas_call | solution.py:449
  18.8 8.5 %all_to_all.10 = f32[8,4,128]{2,1,0:T(4,128)S(1)} all-to-all(f32[8,4,128]{2,1,0:T(4,128)S(1)} %broadcast_in_dim.4), channel_id=1, replica_groups={{0,4,8,12,16,20,24,28},{32,36,40,44,48,52,56,60},{64,68,72,76,80,84,88,..., dimensions={0} | all-to-all | bytes 32768 | tf_op jit(solution)/shard_map/all_to_all | solution.py:464
  27.3 0.0 collective-permute-done.5.state_3
  27.3 0.0 collective-permute-done.4.state_2
  27.3 0.0 collective-permute-done.3.state_1
  27.3 17.3 %all_to_all.11 = f32[8,8,4,128]{3,2,1,0:T(4,128)S(1)} all-to-all(f32[8,8,4,128]{3,2,1,0:T(4,128)S(1)} %broadcast_in_dim.5), channel_id=1, replica_groups={{0,32,64,96,128,160,192,224},{4,36,68,100,132,164,196,228},{8,40,72,104..., dimensions={0} | all-to-all | bytes 262144 | tf_op jit(solution)/shard_map/all_to_all | solution.py:469
  44.7 0.0 copy-start
  44.7 0.0 copy-start.1
  44.7 0.0 copy-start.2
  44.7 0.0 copy-start.3
  44.7 8.7 %backward.1 = (bf16[304,256]{1,0:T(8,128)(2,1)S(1)}, bf16[288,256]{1,0:T(8,128)(2,1)S(1)}) custom-call(f32[256,128]{1,0:T(8,128)S(1)} %bitcast.4, f32[64,128]{1,0:T(8,128)S(1)} %get-tuple-element.48.ranks, f32[3,128]{1,0:T(4,128)S(1)} %get-tuple-element.49.target, f32[6,64,128]{2,1,0:T(8,128)S(1)} %get-tuple-element.50.shading, ...), custom_call_target="tpu_custom_call" | custom-call | tf_op jit(solution)/shard_map/backward/pallas_call | solution.py:474
  53.4 1.8 %collective-permute-start.6 = (bf16[304,256]{1,0:T(8,128)(2,1)S(1)}, bf16[304,256]{1,0:T(8,128)(2,1)S(1)}, u32[]{:S(2)}, u32[]{:S(2)}) collective-permute-start(bf16[304,256]{1,0:T(8,128)(2,1)S(1)} %get-tuple-element.56.even), channel_id=1, source_target_pairs={{0,1},{2,3},{1,0},{3,2},{4,5},{6,7},{5,4},{7,6},{8,9},{10,11},{9,8... | collective-permute-start | bytes 466952 | tf_op jit(solution)/shard_map/ppermute | solution.py:407
  55.3 2.7 %collective-permute-start.7 = (bf16[288,256]{1,0:T(8,128)(2,1)S(1)}, bf16[288,256]{1,0:T(8,128)(2,1)S(1)}, u32[]{:S(2)}, u32[]{:S(2)}) collective-permute-start(bf16[288,256]{1,0:T(8,128)(2,1)S(1)} %get-tuple-element.57.odd), channel_id=1, source_target_pairs={{1,2},{3,0},{2,1},{0,3},{5,6},{7,4},{6,5},{4,7},{9,10},{11,8},{10,... | collective-permute-start | bytes 442376 | tf_op jit(solution)/shard_map/ppermute | solution.py:407
  57.9 3.7 %collective-permute-done.7.odd_other = bf16[288,256]{1,0:T(8,128)(2,1)S(1)} collective-permute-done((bf16[288,256]{1,0:T(8,128)(2,1)S(1)}, bf16[288,256]{1,0:T(8,128)(2,1)S(1)}, u32[]{:S(2)}, u32[]{:S(2)}) %collective-permute-start.7) | collective-permute-done | bytes 147488 | tf_op jit(solution)/shard_map/ppermute | solution.py:407
  61.6 0.0 collective-permute-done.6.even_other
  61.6 0.1 pair.1
  61.7 2.8 %collective-permute-start.8 = (bf16[304,256]{1,0:T(8,128)(2,1)S(1)}, bf16[304,256]{1,0:T(8,128)(2,1)S(1)}, u32[]{:S(2)}, u32[]{:S(2)}) collective-permute-start(bf16[304,256]{1,0:T(8,128)(2,1)S(1)} %get-tuple-element.58.even), channel_id=1, source_target_pairs={{1,2},{3,0},{2,1},{0,3},{5,6},{7,4},{6,5},{4,7},{9,10},{11,8},{10,... | collective-permute-start | bytes 466952 | tf_op jit(solution)/shard_map/ppermute | solution.py:407
  64.5 0.0 collective-permute-start.9
  64.5 5.1 %collective-permute-done.9.odd_other = bf16[288,256]{1,0:T(8,128)(2,1)S(1)} collective-permute-done((bf16[288,256]{1,0:T(8,128)(2,1)S(1)}, bf16[288,256]{1,0:T(8,128)(2,1)S(1)}, u32[]{:S(2)}, u32[]{:S(2)}) %collective-permute-start.9) | collective-permute-done | bytes 147488 | tf_op jit(solution)/shard_map/ppermute | solution.py:407
  69.6 0.0 collective-permute-done.8.even_other
  69.6 0.0 copy-done
  69.6 0.0 copy-done.1
  69.6 0.0 copy-done.2
  69.6 0.0 copy-done.3
  69.6 1.6 %update.1 = (f32[1,64,256]{2,1,0:T(8,128)}, f32[1,2,256,256]{3,2,1,0:T(8,128)}, f32[1,2,256]{2,1,0:T(2,128)}, f32[1,4,256]{2,1,0:T(4,128)}, f32[2,1,16,256]{3,2,...) custom-call(bf16[304,256]{1,0:T(8,128)(2,1)S(1)} %get-tuple-element.58.even, ...), custom_call_target="tpu_custom_call" | custom-call | tf_op jit(solution)/shard_map/update/pallas_call | solution.py:487
  (2 shorter events, 0.0 us)
Async XLA Ops:
  1.7 7.4 %collective-permute-start.2 = (bf16[160,256]{1,0:T(8,128)(2,1)S(1)}, bf16[160,256]{1,0:T(8,128)(2,1)S(1)}, u32[]{:S(2)}, u32[]{:S(2)}) collective-permute-start(bf16[160,256]{1,0:T(8,128)(2,1)S(1)} %pack_weights.1.own.high_0), channel_id=1, source_target_pairs={{0,3},{1,0},{2,1},{3,2},{4,7},{5,4},{6,5},{7,6},{8,11},{9,8},{10,9... | collective-permute-start | bytes 245768 | tf_op jit(solution)/shard_map/ppermute | solution.py:400
  4.8 6.3 %collective-permute-start.1 = (bf16[160,256]{1,0:T(8,128)(2,1)S(1)}, bf16[160,256]{1,0:T(8,128)(2,1)S(1)}, u32[]{:S(2)}, u32[]{:S(2)}) collective-permute-start(bf16[160,256]{1,0:T(8,128)(2,1)S(1)} %pack_weights.1.own.high_0), channel_id=1, source_target_pairs={{0,2},{1,3},{2,0},{3,1},{4,6},{5,7},{6,4},{7,5},{8,10},{9,11},{10,... | collective-permute-start | bytes 245768 | tf_op jit(solution)/shard_map/ppermute | solution.py:400
  5.5 6.5 %collective-permute-start = (bf16[160,256]{1,0:T(8,128)(2,1)S(1)}, bf16[160,256]{1,0:T(8,128)(2,1)S(1)}, u32[]{:S(2)}, u32[]{:S(2)}) collective-permute-start(bf16[160,256]{1,0:T(8,128)(2,1)S(1)} %pack_weights.1.own.high_0), channel_id=1, source_target_pairs={{0,1},{1,2},{2,3},{3,0},{4,5},{5,6},{6,7},{7,4},{8,9},{9,10},{10,1... | collective-permute-start | bytes 245768 | tf_op jit(solution)/shard_map/ppermute | solution.py:400
  12.0 15.3 %collective-permute-start.5 = (bf16[480,256]{1,0:T(8,128)(2,1)S(1)}, bf16[480,256]{1,0:T(8,128)(2,1)S(1)}, u32[]{:S(2)}, u32[]{:S(2)}) collective-permute-start(bf16[480,256]{1,0:T(8,128)(2,1)S(1)} %get-tuple-element.60.state_0), channel_id=1, source_target_pairs={{0,3},{1,0},{2,1},{3,2},{4,7},{5,4},{6,5},{7,6},{8,11},{9,8},{10,9... | collective-permute-start | bytes 737288 | tf_op jit(solution)/shard_map/ppermute | solution.py:400
  12.6 14.7 %collective-permute-start.4 = (bf16[480,256]{1,0:T(8,128)(2,1)S(1)}, bf16[480,256]{1,0:T(8,128)(2,1)S(1)}, u32[]{:S(2)}, u32[]{:S(2)}) collective-permute-start(bf16[480,256]{1,0:T(8,128)(2,1)S(1)} %get-tuple-element.60.state_0), channel_id=1, source_target_pairs={{0,2},{1,3},{2,0},{3,1},{4,6},{5,7},{6,4},{7,5},{8,10},{9,11},{10,... | collective-permute-start | bytes 737288 | tf_op jit(solution)/shard_map/ppermute | solution.py:400
  13.2 14.1 %collective-permute-start.3 = (bf16[480,256]{1,0:T(8,128)(2,1)S(1)}, bf16[480,256]{1,0:T(8,128)(2,1)S(1)}, u32[]{:S(2)}, u32[]{:S(2)}) collective-permute-start(bf16[480,256]{1,0:T(8,128)(2,1)S(1)} %get-tuple-element.60.state_0), channel_id=1, source_target_pairs={{0,1},{1,2},{2,3},{3,0},{4,5},{5,6},{6,7},{7,4},{8,9},{9,10},{10,1... | collective-permute-start | bytes 737288 | tf_op jit(solution)/shard_map/ppermute | solution.py:400
  44.7 24.9 %copy-start = (f32[2,1,2,64,256]{4,3,2,1,0:T(8,128)S(1)}, f32[2,1,2,64,256]{4,3,2,1,0:T(8,128)}, u32[]{:S(2)}) copy-start(f32[2,1,2,64,256]{4,3,2,1,0:T(8,128)} %mom_hid.1) | copy-start | bytes 786436
  44.7 24.9 %copy-start.1 = (f32[2,1,16,256]{3,2,1,0:T(8,128)S(1)}, f32[2,1,16,256]{3,2,1,0:T(8,128)}, u32[]{:S(2)}) copy-start(f32[2,1,16,256]{3,2,1,0:T(8,128)} %mom_in.1) | copy-start | bytes 98308
  44.7 24.9 %copy-start.2 = (f32[2,1,4,64]{3,2,1,0:T(4,128)S(1)}, f32[2,1,4,64]{3,2,1,0:T(4,128)}, u32[]{:S(2)}) copy-start(f32[2,1,4,64]{3,2,1,0:T(4,128)} %mom_out.1) | copy-start | bytes 6148
  44.7 24.9 %copy-start.3 = (f32[2,1,2,64]{3,2,1,0:T(2,128)S(1)}, f32[2,1,2,64]{3,2,1,0:T(2,128)}, u32[]{:S(2)}) copy-start(f32[2,1,2,64]{3,2,1,0:T(2,128)} %mom_bias.1) | copy-start | bytes 3076
  53.4 8.2 %collective-permute-start.6 = (bf16[304,256]{1,0:T(8,128)(2,1)S(1)}, bf16[304,256]{1,0:T(8,128)(2,1)S(1)}, u32[]{:S(2)}, u32[]{:S(2)}) collective-permute-start(bf16[304,256]{1,0:T(8,128)(2,1)S(1)} %get-tuple-element.56.even), channel_id=1, source_target_pairs={{0,1},{2,3},{1,0},{3,2},{4,5},{6,7},{5,4},{7,6},{8,9},{10,11},{9,8... | collective-permute-start | bytes 466952 | tf_op jit(solution)/shard_map/ppermute | solution.py:407
  55.3 6.4 %collective-permute-start.7 = (bf16[288,256]{1,0:T(8,128)(2,1)S(1)}, bf16[288,256]{1,0:T(8,128)(2,1)S(1)}, u32[]{:S(2)}, u32[]{:S(2)}) collective-permute-start(bf16[288,256]{1,0:T(8,128)(2,1)S(1)} %get-tuple-element.57.odd), channel_id=1, source_target_pairs={{1,2},{3,0},{2,1},{0,3},{5,6},{7,4},{6,5},{4,7},{9,10},{11,8},{10,... | collective-permute-start | bytes 442376 | tf_op jit(solution)/shard_map/ppermute | solution.py:407
  61.7 7.9 %collective-permute-start.8 = (bf16[304,256]{1,0:T(8,128)(2,1)S(1)}, bf16[304,256]{1,0:T(8,128)(2,1)S(1)}, u32[]{:S(2)}, u32[]{:S(2)}) collective-permute-start(bf16[304,256]{1,0:T(8,128)(2,1)S(1)} %get-tuple-element.58.even), channel_id=1, source_target_pairs={{1,2},{3,0},{2,1},{0,3},{5,6},{7,4},{6,5},{4,7},{9,10},{11,8},{10,... | collective-permute-start | bytes 466952 | tf_op jit(solution)/shard_map/ppermute | solution.py:407
  64.5 5.1 %collective-permute-start.9 = (bf16[288,256]{1,0:T(8,128)(2,1)S(1)}, bf16[288,256]{1,0:T(8,128)(2,1)S(1)}, u32[]{:S(2)}, u32[]{:S(2)}) collective-permute-start(bf16[288,256]{1,0:T(8,128)(2,1)S(1)} %get-tuple-element.59.odd), channel_id=1, source_target_pairs={{0,1},{2,3},{1,0},{3,2},{4,5},{6,7},{5,4},{7,6},{8,9},{10,11},{9,8... | collective-permute-start | bytes 442376 | tf_op jit(solution)/shard_map/ppermute | solution.py:407

commit v4 on v3

--- a/solution.py
+++ b/solution.py
@@ -1,5 +1,3 @@
-import functools
-
 import jax
 import jax.numpy as jnp
 from jax import lax
@@ -11,7 +9,7 @@
 HID = 256
 S = 64
 N_BATCH = 4
-CHUNK = 4096
+CHUNK = 8192
 MIB = 1 << 20
 LIMIT = 24
 
@@ -270,9 +268,8 @@
     odd[HID : HID + 32, :] = sum_first[32:64, :].astype(bf16)
 
 
-def pair_kernel(even, even_other, odd, odd_other, even_sum, odd_sum):
-    even_sum[...] = (even[...].astype(f32) + even_other[...].astype(f32)).astype(bf16)
-    odd_sum[...] = (odd[...].astype(f32) + odd_other[...].astype(f32)).astype(bf16)
+def pair_kernel(own, other, total):
+    total[...] = (own[...].astype(f32) + other[...].astype(f32)).astype(bf16)
 
 
 def adam(grad, first, second, scale):
@@ -416,7 +413,6 @@
 
 
 def body(
-    inner,
     features, spacing, counts, depth_rank, target,
     w_in, w_hid, b_hid, w_out,
     mom_in, mom_hid, mom_bias, mom_out,
@@ -424,7 +420,6 @@
     samples = features.shape[2]
     rays = samples // S
     cells = depth_rank.shape[1]
-    outer = cells // inner
 
     (block,) = call_on_hbm(
         pack_weights, held((BLOCK, HID), bf16), "pack_weights", w_in, w_hid, b_hid, w_out
@@ -443,7 +438,10 @@
     )
     feats = jnp.concatenate([features[0], jnp.ones((1, samples), bf16)], axis=0)
     state, feats, *highs[1:] = lax.optimization_barrier((state, feats, *highs[1:]))
-    states = [state] + from_others(state)
+    sides = [
+        lax.ppermute(state, "batch", [(i, (i + hop) % N_BATCH) for i in range(N_BATCH)])
+        for hop in (1, 3)
+    ]
 
     act = held((HID, samples), bf16)
     act_one, act_two, act_three, wide_hid, wide_misc, shading, summary = call(
@@ -459,17 +457,12 @@
         name="forward",
     )(*highs, feats, gaps, live_counts)
 
-    near = [[z * inner + i for i in range(inner)] for z in range(outer)]
-    far = [[z * inner + i for z in range(outer)] for i in range(inner)]
-    some = lax.all_to_all(
-        jnp.broadcast_to(summary[None], (inner, 4, rays)), "region", 0, 0,
-        axis_index_groups=near, tiled=True,
-    )
-    some, *states = lax.optimization_barrier((some, *states))
+    summary, *sides = lax.optimization_barrier((summary, *sides))
     table = lax.all_to_all(
-        jnp.broadcast_to(some[None], (outer, inner, 4, rays)), "region", 0, 0,
-        axis_index_groups=far, tiled=True,
+        jnp.broadcast_to(summary[None], (cells, 4, rays)), "region", 0, 0, tiled=True
     ).reshape(cells * 4, rays)
+    table, state = lax.optimization_barrier((table, state))
+    opposite = lax.ppermute(state, "batch", [(i, (i + 2) % N_BATCH) for i in range(N_BATCH)])
 
     even, odd = call(
         backward_kernel,
@@ -480,9 +473,12 @@
         ],
         name="backward",
     )(table, ranks, goal, shading, wide_hid, wide_misc, feats, act_one, act_two, act_three)
-    even, odd = call(
-        pair_kernel, (held(even.shape, bf16), held(odd.shape, bf16)), name="pair"
-    )(even, swapped(even, True), odd, swapped(odd, False))
+    even, odd, opposite = lax.optimization_barrier((even, odd, opposite))
+    states = [state, sides[0], opposite, sides[1]]
+    even, odd = [
+        call(pair_kernel, held(own.shape, bf16), name="pair")(own, swapped(own, first))
+        for own, first in ((even, True), (odd, False))
+    ]
 
     return call(
         update_kernel,
@@ -499,10 +495,8 @@
 
 
 def solution(mesh):
-    cells = mesh.shape["region"]
-    inner = 8 if cells % 8 == 0 and cells > 8 else 2
     return jax.shard_map(
-        functools.partial(body, inner),
+        body,
         mesh=mesh,
         in_specs=(
             P("region", None, "batch"),

time: 71.6 us -> 67.1 us (0.937)
  blocking collectives: 25.9 us -> 21.8 us
    all_to_all x2 -> x1, blocking collectives: 25.9 us -> 21.8 us  [body(): lax.all_to_all(jnp.broadcast_to(summary[None], (cells, 4, rays)), 'region...]
    ppermute x0 -> x3, starting transfers between devices: none -> 2.88 us  [the longest x2 2.03 us: body(): lax.ppermute(state, 'batch', [(i, (i + hop) % N_BATCH) for i in range(N_B...]
    ppermute x6 -> x3, starting transfers between devices: 6.98 us -> 4.69 us  [from_others(): lax.ppermute(block, 'batch', [(i, (i + hop) % N_BATCH) for i in range(N_B...]
    ppermute x0 -> x3, waiting for transfers between devices: none -> 2.07 us  [the longest x2 1.99 us: body(): lax.ppermute(state, 'batch', [(i, (i + hop) % N_BATCH) for i in range(N_B...]
    ppermute x4, waiting for transfers between devices: 8.83 us -> 7.39 us  [swapped(): return lax.ppermute(block, 'batch', pairs + [(j, i) for i, j in pairs])]
    ppermute x4, starting transfers between devices: 7.28 us -> 6.06 us  [swapped(): return lax.ppermute(block, 'batch', pairs + [(j, i) for i, j in pairs])]
    ppermute x6 -> x3, waiting for transfers between devices: 2.88 us -> 2.87 us  [from_others(): lax.ppermute(block, 'batch', [(i, (i + hop) % N_BATCH) for i in range(N_B...]
  transfers between devices with their start and end apart: 10 -> 10, of which waited for: 4 -> 7; matrix products, arithmetic and copies ran while one was open for 2% -> 2% of each run, Pallas kernels for 8% -> 21%
where the time goes in v4:
time: 67.1 us; the launch traced here: 66.8 us
  blocking collectives  21.8 us (32%)
  Pallas kernels  17 us (25%)
  starting transfers between devices  13.6 us (20%)
  waiting for transfers between devices  12.3 us (18%)
  local copies, waits for them, and re-layouts  1.34 us (2%)
  between operations  0.72 us (1%)
    all_to_all x1, blocking collectives, body(): lax.all_to_all(jnp.broadcast_to(summary[None], (cells, 4, rays)), 'region...  21.8 us
    pallas_call x1, Pallas kernels, body(): call(backward_kernel, (held((HID + 48, HID), bf16), held((HID + 32, HID),...  8.53 us
    ppermute x4, waiting for transfers between devices, swapped(): return lax.ppermute(block, 'batch', pairs + [(j, i) for i, j in pairs])  7.39 us
    ppermute x4, starting transfers between devices, swapped(): return lax.ppermute(block, 'batch', pairs + [(j, i) for i, j in pairs])  6.06 us
    ppermute x3, starting transfers between devices, from_others(): lax.ppermute(block, 'batch', [(i, (i + hop) % N_BATCH) for i in range(N_B...  4.69 us
    pallas_call x1, Pallas kernels, body(): call(forward_kernel, (act, act, act, held((2, HID, HID), bf16), held((16,...  4.36 us
    ppermute x3, waiting for transfers between devices, from_others(): lax.ppermute(block, 'batch', [(i, (i + hop) % N_BATCH) for i in range(N_B...  2.87 us
    pallas_call x2, Pallas kernels, call_on_hbm(): pl.pallas_call(fetched(kernel, len(arrays), len(outs)), out_shape=outs, i...  2.47 us
  transfers between devices with their start and end apart: 10, of which 7 were waited for; matrix products, arithmetic and copies ran while one was open for 2% of the time, Pallas kernels for 21%

profile of v4, /device:TPU:2, one launch (start us, length us, event | category | flops | bytes accessed | tf_op | source)
XLA Modules:
  0.0 66.8 jit_solution(8528259246860380598)
XLA Ops:
  0.6 1.1 %pack_weights.1.own.high_0 = bf16[160,256]{1,0:T(8,128)(2,1)S(1)} custom-call(f32[1,16,256]{2,1,0:T(8,128)} %refs_0_.3, f32[1,2,64,256]{3,2,1,0:T(8,128)} %refs_1_.3, f32[1,2,64]{2,1,0:T(2,128)} %refs_2_.2, f32[1,4,64]{2,1,0:T(4,128)} %refs_2_.3), custom_call_target="tpu_custom_call" | custom-call | tf_op jit(solution)/shard_map/pack_weights/pallas_call | solution.py:374
  1.7 3.1 %collective-permute-start.2 = (bf16[160,256]{1,0:T(8,128)(2,1)S(1)}, bf16[160,256]{1,0:T(8,128)(2,1)S(1)}, u32[]{:S(2)}, u32[]{:S(2)}) collective-permute-start(bf16[160,256]{1,0:T(8,128)(2,1)S(1)} %pack_weights.1.own.high_0), channel_id=1, source_target_pairs={{0,3},{1,0},{2,1},{3,2},{4,7},{5,4},{6,5},{7,6},{8,11},{9,8},{10,9... | collective-permute-start | bytes 245768 | tf_op jit(solution)/shard_map/ppermute | solution.py:397
  4.8 0.6 collective-permute-start.1
  5.5 1.0 %collective-permute-start = (bf16[160,256]{1,0:T(8,128)(2,1)S(1)}, bf16[160,256]{1,0:T(8,128)(2,1)S(1)}, u32[]{:S(2)}, u32[]{:S(2)}) collective-permute-start(bf16[160,256]{1,0:T(8,128)(2,1)S(1)} %pack_weights.1.own.high_0), channel_id=1, source_target_pairs={{0,1},{1,2},{2,3},{3,0},{4,5},{5,6},{6,7},{7,4},{8,9},{9,10},{10,1... | collective-permute-start | bytes 245768 | tf_op jit(solution)/shard_map/ppermute | solution.py:397
  6.4 1.3 %concatenate.3.feats = bf16[64,8192]{1,0:T(8,128)(2,1)S(1)} pad(bf16[63,8192]{1,0:T(8,128)(2,1)} %bitcast.5, bf16[]{:T(256)} %constant.0.clone.1), padding=0_1x0_0 | pad | bytes 2080770 | tf_op jit(solution)/shard_map/concatenate | solution.py:439
  7.7 1.4 %prepare.1 = (bf16[480,256]{1,0:T(8,128)(2,1)S(1)}, f32[64,128]{1,0:T(8,128)S(1)}, f32[1,128]{1,0:T(1,128)S(1)}, f32[64,128]{1,0:T(8,128)S(1)}, f32[3,128]{1,0:T(4,128)S(1)}) custom-call(f32[1,16,256]{2,1,0:T(8,128)} %refs_0_.3, f32[1,2,64,256]{3,2,1,0:T(8,128)} %refs_1_.3, f32[1,4,64]{2,1,0:T(4,128)} %refs_2_.3, f32[2,1,16,256]{3,2,1,0:T(8,128)} %mom_in.1, ...), custom_call_target="tpu_custom_call" | custom-call | tf_op jit(solution)/shard_map/prepare/pallas_call | solution.py:374
  9.1 0.0 collective-permute-done.2.from_three.high_3
  9.1 2.0 %collective-permute-done.1.from_two.high_2 = bf16[160,256]{1,0:T(8,128)(2,1)S(1)} collective-permute-done((bf16[160,256]{1,0:T(8,128)(2,1)S(1)}, bf16[160,256]{1,0:T(8,128)(2,1)S(1)}, u32[]{:S(2)}, u32[]{:S(2)}) %collective-permute-start.1) | collective-permute-done | bytes 81952 | tf_op jit(solution)/shard_map/ppermute | solution.py:397
  11.2 0.8 %collective-permute-done.from_one.high_1 = bf16[160,256]{1,0:T(8,128)(2,1)S(1)} collective-permute-done((bf16[160,256]{1,0:T(8,128)(2,1)S(1)}, bf16[160,256]{1,0:T(8,128)(2,1)S(1)}, u32[]{:S(2)}, u32[]{:S(2)}) %collective-permute-start) | collective-permute-done | bytes 81952 | tf_op jit(solution)/shard_map/ppermute | solution.py:397
  12.0 0.6 collective-permute-start.4
  12.6 1.5 %collective-permute-start.3 = (bf16[480,256]{1,0:T(8,128)(2,1)S(1)}, bf16[480,256]{1,0:T(8,128)(2,1)S(1)}, u32[]{:S(2)}, u32[]{:S(2)}) collective-permute-start(bf16[480,256]{1,0:T(8,128)(2,1)S(1)} %get-tuple-element.60.state_0), channel_id=1, source_target_pairs={{0,1},{1,2},{2,3},{3,0},{4,5},{5,6},{6,7},{7,4},{8,9},{9,10},{10,1... | collective-permute-start | bytes 737288 | tf_op jit(solution)/shard_map/ppermute | solution.py:442
  14.0 4.4 %forward.1 = (bf16[256,8192]{1,0:T(8,128)(2,1)S(1)}, bf16[256,8192]{1,0:T(8,128)(2,1)S(1)}, bf16[256,8192]{1,0:T(8,128)(2,1)S(1)}, bf16[2,256,256]{2,1,0:T(8,128...) custom-call(bf16[160,256]{1,0:T(8,128)(2,1)S(1)} %pack_weights.1.own.high_0, ...), custom_call_target="tpu_custom_call" | custom-call | tf_op jit(solution)/shard_map/forward/pallas_call | solution.py:447
  18.4 0.8 %collective-permute-done.4.state_3 = bf16[480,256]{1,0:T(8,128)(2,1)S(1)} collective-permute-done((bf16[480,256]{1,0:T(8,128)(2,1)S(1)}, bf16[480,256]{1,0:T(8,128)(2,1)S(1)}, u32[]{:S(2)}, u32[]{:S(2)}) %collective-permute-start.4) | collective-permute-done | bytes 245792 | tf_op jit(solution)/shard_map/ppermute | solution.py:442
  19.2 1.2 %collective-permute-done.3.state_1 = bf16[480,256]{1,0:T(8,128)(2,1)S(1)} collective-permute-done((bf16[480,256]{1,0:T(8,128)(2,1)S(1)}, bf16[480,256]{1,0:T(8,128)(2,1)S(1)}, u32[]{:S(2)}, u32[]{:S(2)}) %collective-permute-start.3) | collective-permute-done | bytes 245792 | tf_op jit(solution)/shard_map/ppermute | solution.py:442
  20.4 21.8 %all_to_all.5 = f32[64,4,128]{2,1,0:T(4,128)S(1)} all-to-all(f32[64,4,128]{2,1,0:T(4,128)S(1)} %broadcast_in_dim.2), channel_id=1, replica_groups=mesh['region'=64,'batch'=4] {'region'}, dimensions={0} | all-to-all | bytes 262144 | tf_op jit(solution)/shard_map/all_to_all | solution.py:461
  42.2 0.9 %collective-permute-start.5 = (bf16[480,256]{1,0:T(8,128)(2,1)S(1)}, bf16[480,256]{1,0:T(8,128)(2,1)S(1)}, u32[]{:S(2)}, u32[]{:S(2)}) collective-permute-start(bf16[480,256]{1,0:T(8,128)(2,1)S(1)} %get-tuple-element.60.state_0), channel_id=1, source_target_pairs={{0,2},{1,3},{2,0},{3,1},{4,6},{5,7},{6,4},{7,5},{8,10},{9,11},{10,... | collective-permute-start | bytes 737288 | tf_op jit(solution)/shard_map/ppermute | solution.py:465
  43.0 0.0 copy-start
  43.0 0.0 copy-start.1
  43.0 0.0 copy-start.2
  43.0 0.0 copy-start.3
  43.0 8.5 %backward.1 = (bf16[304,256]{1,0:T(8,128)(2,1)S(1)}, bf16[288,256]{1,0:T(8,128)(2,1)S(1)}) custom-call(f32[256,128]{1,0:T(8,128)S(1)} %bitcast.4, f32[64,128]{1,0:T(8,128)S(1)} %get-tuple-element.50.ranks, f32[3,128]{1,0:T(4,128)S(1)} %get-tuple-element.51.target, f32[6,64,128]{2,1,0:T(8,128)S(1)} %get-tuple-element.52.shading, ...), custom_call_target="tpu_custom_call" | custom-call | tf_op jit(solution)/shard_map/backward/pallas_call | solution.py:467
  51.6 0.1 collective-permute-done.5.state_2
  51.7 0.5 collective-permute-start.6
  52.2 2.7 %collective-permute-start.8 = (bf16[288,256]{1,0:T(8,128)(2,1)S(1)}, bf16[288,256]{1,0:T(8,128)(2,1)S(1)}, u32[]{:S(2)}, u32[]{:S(2)}) collective-permute-start(bf16[288,256]{1,0:T(8,128)(2,1)S(1)} %get-tuple-element.62.own), channel_id=1, source_target_pairs={{1,2},{3,0},{2,1},{0,3},{5,6},{7,4},{6,5},{4,7},{9,10},{11,8},{10,... | collective-permute-start | bytes 442376 | tf_op jit(solution)/shard_map/ppermute | solution.py:404
  54.9 2.5 %collective-permute-done.6.other = bf16[304,256]{1,0:T(8,128)(2,1)S(1)} collective-permute-done((bf16[304,256]{1,0:T(8,128)(2,1)S(1)}, bf16[304,256]{1,0:T(8,128)(2,1)S(1)}, u32[]{:S(2)}, u32[]{:S(2)}) %collective-permute-start.6) | collective-permute-done | bytes 155680 | tf_op jit(solution)/shard_map/ppermute | solution.py:404
  57.5 2.4 %collective-permute-start.7 = (bf16[304,256]{1,0:T(8,128)(2,1)S(1)}, bf16[304,256]{1,0:T(8,128)(2,1)S(1)}, u32[]{:S(2)}, u32[]{:S(2)}) collective-permute-start(bf16[304,256]{1,0:T(8,128)(2,1)S(1)} %pair.2.even), channel_id=1, source_target_pairs={{1,2},{3,0},{2,1},{0,3},{5,6},{7,4},{6,5},{4,7},{9,10},{11,8},{10,... | collective-permute-start | bytes 466952 | tf_op jit(solution)/shard_map/ppermute | solution.py:404
  59.9 0.0 collective-permute-done.8.other
  60.0 0.4 collective-permute-start.9
  60.3 4.9 %collective-permute-done.9.odd_other = bf16[288,256]{1,0:T(8,128)(2,1)S(1)} collective-permute-done((bf16[288,256]{1,0:T(8,128)(2,1)S(1)}, bf16[288,256]{1,0:T(8,128)(2,1)S(1)}, u32[]{:S(2)}, u32[]{:S(2)}) %collective-permute-start.9) | collective-permute-done | bytes 147488 | tf_op jit(solution)/shard_map/ppermute | solution.py:404
  65.2 0.0 collective-permute-done.7.even_other
  65.2 0.0 copy-done
  65.2 0.0 copy-done.1
  65.2 0.0 copy-done.2
  65.2 0.0 copy-done.3
  65.2 1.6 %update.1 = (f32[1,64,256]{2,1,0:T(8,128)}, f32[1,2,256,256]{3,2,1,0:T(8,128)}, f32[1,2,256]{2,1,0:T(2,128)}, f32[1,4,256]{2,1,0:T(4,128)}, f32[2,1,16,256]{3,2,...) custom-call(bf16[304,256]{1,0:T(8,128)(2,1)S(1)} %pair.2.even, ...), custom_call_target="tpu_custom_call" | custom-call | tf_op jit(solution)/shard_map/update/pallas_call | solution.py:483
  (3 shorter events, 0.1 us)
Async XLA Ops:
  1.7 7.4 %collective-permute-start.2 = (bf16[160,256]{1,0:T(8,128)(2,1)S(1)}, bf16[160,256]{1,0:T(8,128)(2,1)S(1)}, u32[]{:S(2)}, u32[]{:S(2)}) collective-permute-start(bf16[160,256]{1,0:T(8,128)(2,1)S(1)} %pack_weights.1.own.high_0), channel_id=1, source_target_pairs={{0,3},{1,0},{2,1},{3,2},{4,7},{5,4},{6,5},{7,6},{8,11},{9,8},{10,9... | collective-permute-start | bytes 245768 | tf_op jit(solution)/shard_map/ppermute | solution.py:397
  4.8 6.3 %collective-permute-start.1 = (bf16[160,256]{1,0:T(8,128)(2,1)S(1)}, bf16[160,256]{1,0:T(8,128)(2,1)S(1)}, u32[]{:S(2)}, u32[]{:S(2)}) collective-permute-start(bf16[160,256]{1,0:T(8,128)(2,1)S(1)} %pack_weights.1.own.high_0), channel_id=1, source_target_pairs={{0,2},{1,3},{2,0},{3,1},{4,6},{5,7},{6,4},{7,5},{8,10},{9,11},{10,... | collective-permute-start | bytes 245768 | tf_op jit(solution)/shard_map/ppermute | solution.py:397
  5.5 6.5 %collective-permute-start = (bf16[160,256]{1,0:T(8,128)(2,1)S(1)}, bf16[160,256]{1,0:T(8,128)(2,1)S(1)}, u32[]{:S(2)}, u32[]{:S(2)}) collective-permute-start(bf16[160,256]{1,0:T(8,128)(2,1)S(1)} %pack_weights.1.own.high_0), channel_id=1, source_target_pairs={{0,1},{1,2},{2,3},{3,0},{4,5},{5,6},{6,7},{7,4},{8,9},{9,10},{10,1... | collective-permute-start | bytes 245768 | tf_op jit(solution)/shard_map/ppermute | solution.py:397
  12.0 7.2 %collective-permute-start.4 = (bf16[480,256]{1,0:T(8,128)(2,1)S(1)}, bf16[480,256]{1,0:T(8,128)(2,1)S(1)}, u32[]{:S(2)}, u32[]{:S(2)}) collective-permute-start(bf16[480,256]{1,0:T(8,128)(2,1)S(1)} %get-tuple-element.60.state_0), channel_id=1, source_target_pairs={{0,3},{1,0},{2,1},{3,2},{4,7},{5,4},{6,5},{7,6},{8,11},{9,8},{10,9... | collective-permute-start | bytes 737288 | tf_op jit(solution)/shard_map/ppermute | solution.py:442
  12.6 7.8 %collective-permute-start.3 = (bf16[480,256]{1,0:T(8,128)(2,1)S(1)}, bf16[480,256]{1,0:T(8,128)(2,1)S(1)}, u32[]{:S(2)}, u32[]{:S(2)}) collective-permute-start(bf16[480,256]{1,0:T(8,128)(2,1)S(1)} %get-tuple-element.60.state_0), channel_id=1, source_target_pairs={{0,1},{1,2},{2,3},{3,0},{4,5},{5,6},{6,7},{7,4},{8,9},{9,10},{10,1... | collective-permute-start | bytes 737288 | tf_op jit(solution)/shard_map/ppermute | solution.py:442
  42.2 9.5 %collective-permute-start.5 = (bf16[480,256]{1,0:T(8,128)(2,1)S(1)}, bf16[480,256]{1,0:T(8,128)(2,1)S(1)}, u32[]{:S(2)}, u32[]{:S(2)}) collective-permute-start(bf16[480,256]{1,0:T(8,128)(2,1)S(1)} %get-tuple-element.60.state_0), channel_id=1, source_target_pairs={{0,2},{1,3},{2,0},{3,1},{4,6},{5,7},{6,4},{7,5},{8,10},{9,11},{10,... | collective-permute-start | bytes 737288 | tf_op jit(solution)/shard_map/ppermute | solution.py:465
  43.0 22.2 %copy-start = (f32[2,1,2,64,256]{4,3,2,1,0:T(8,128)S(1)}, f32[2,1,2,64,256]{4,3,2,1,0:T(8,128)}, u32[]{:S(2)}) copy-start(f32[2,1,2,64,256]{4,3,2,1,0:T(8,128)} %mom_hid.1) | copy-start | bytes 786436
  43.0 22.2 %copy-start.1 = (f32[2,1,16,256]{3,2,1,0:T(8,128)S(1)}, f32[2,1,16,256]{3,2,1,0:T(8,128)}, u32[]{:S(2)}) copy-start(f32[2,1,16,256]{3,2,1,0:T(8,128)} %mom_in.1) | copy-start | bytes 98308
  43.0 22.2 %copy-start.2 = (f32[2,1,4,64]{3,2,1,0:T(4,128)S(1)}, f32[2,1,4,64]{3,2,1,0:T(4,128)}, u32[]{:S(2)}) copy-start(f32[2,1,4,64]{3,2,1,0:T(4,128)} %mom_out.1) | copy-start | bytes 6148
  43.0 22.2 %copy-start.3 = (f32[2,1,2,64]{3,2,1,0:T(2,128)S(1)}, f32[2,1,2,64]{3,2,1,0:T(2,128)}, u32[]{:S(2)}) copy-start(f32[2,1,2,64]{3,2,1,0:T(2,128)} %mom_bias.1) | copy-start | bytes 3076
  51.7 5.8 %collective-permute-start.6 = (bf16[304,256]{1,0:T(8,128)(2,1)S(1)}, bf16[304,256]{1,0:T(8,128)(2,1)S(1)}, u32[]{:S(2)}, u32[]{:S(2)}) collective-permute-start(bf16[304,256]{1,0:T(8,128)(2,1)S(1)} %get-tuple-element.61.own), channel_id=1, source_target_pairs={{0,1},{2,3},{1,0},{3,2},{4,5},{6,7},{5,4},{7,6},{8,9},{10,11},{9,8... | collective-permute-start | bytes 466952 | tf_op jit(solution)/shard_map/ppermute | solution.py:404
  52.2 7.7 %collective-permute-start.8 = (bf16[288,256]{1,0:T(8,128)(2,1)S(1)}, bf16[288,256]{1,0:T(8,128)(2,1)S(1)}, u32[]{:S(2)}, u32[]{:S(2)}) collective-permute-start(bf16[288,256]{1,0:T(8,128)(2,1)S(1)} %get-tuple-element.62.own), channel_id=1, source_target_pairs={{1,2},{3,0},{2,1},{0,3},{5,6},{7,4},{6,5},{4,7},{9,10},{11,8},{10,... | collective-permute-start | bytes 442376 | tf_op jit(solution)/shard_map/ppermute | solution.py:404
  57.5 7.7 %collective-permute-start.7 = (bf16[304,256]{1,0:T(8,128)(2,1)S(1)}, bf16[304,256]{1,0:T(8,128)(2,1)S(1)}, u32[]{:S(2)}, u32[]{:S(2)}) collective-permute-start(bf16[304,256]{1,0:T(8,128)(2,1)S(1)} %pair.2.even), channel_id=1, source_target_pairs={{1,2},{3,0},{2,1},{0,3},{5,6},{7,4},{6,5},{4,7},{9,10},{11,8},{10,... | collective-permute-start | bytes 466952 | tf_op jit(solution)/shard_map/ppermute | solution.py:404
  60.0 5.2 %collective-permute-start.9 = (bf16[288,256]{1,0:T(8,128)(2,1)S(1)}, bf16[288,256]{1,0:T(8,128)(2,1)S(1)}, u32[]{:S(2)}, u32[]{:S(2)}) collective-permute-start(bf16[288,256]{1,0:T(8,128)(2,1)S(1)} %pair.3.odd), channel_id=1, source_target_pairs={{0,1},{2,3},{1,0},{3,2},{4,5},{6,7},{5,4},{7,6},{8,9},{10,11},{9,8... | collective-permute-start | bytes 442376 | tf_op jit(solution)/shard_map/ppermute | solution.py:404

commit v5 on v4

--- a/solution.py
+++ b/solution.py
@@ -9,9 +9,8 @@
 HID = 256
 S = 64
 N_BATCH = 4
-CHUNK = 8192
 MIB = 1 << 20
-LIMIT = 24
+LIMIT = 32
 
 beta_first = 0.9
 beta_second = 0.95
@@ -131,10 +130,25 @@
     return 1.0 / (1.0 + jnp.exp(-value))
 
 
+def turn_weights(wide_in, wide_hid, misc, turned_in, turned_hid, bias_cols):
+    turned_in[...] = wide_in[...].astype(f32).T.astype(bf16)
+    for layer in range(2):
+        turned_hid[layer] = wide_hid[layer].astype(f32).T.astype(bf16)
+    bias = misc[4:6] + misc[6:8] + misc[8:10]
+    bias_cols[...] = jnp.concatenate([bias, jnp.zeros((6, HID), f32)], axis=0).T
+
+
+def layers(samples, turned_in, turned_hid, bias_cols):
+    one = rectified(dot(turned_in[...], samples))
+    two = rectified(dot(turned_hid[0], one) + bias_cols[:, 0:1])
+    three = rectified(dot(turned_hid[1], two) + bias_cols[:, 1:2])
+    return one, two, three
+
+
 def forward_kernel(
     own, from_one, from_two, from_three, feats, gaps, counts,
-    act_one, act_two, act_three, wide_hid, wide_misc, shading, summary,
-    wide_in, turned_in, turned_hid, bias_cols, out_rows, heads_rows,
+    wide_in, wide_hid, wide_misc, shading, summary,
+    turned_in, turned_hid, bias_cols, out_rows, heads_rows,
 ):
     me = lax.axis_index("batch")
     misc = jnp.zeros((16, HID), f32)
@@ -148,27 +162,14 @@
             ]
         misc = misc + block[MISC:BLOCK, :].astype(f32)
     wide_misc[...] = misc
-    turned_in[...] = wide_in[...].astype(f32).T.astype(bf16)
-    for layer in range(2):
-        turned_hid[layer] = wide_hid[layer].astype(f32).T.astype(bf16)
-    bias = misc[4:6] + misc[6:8] + misc[8:10]
-    bias_cols[...] = jnp.concatenate([bias, jnp.zeros((6, HID), f32)], axis=0).T
+    turn_weights(wide_in, wide_hid, misc, turned_in, turned_hid, bias_cols)
     row = lax.broadcasted_iota(jnp.int32, (16, HID), 0)
     out_rows[...] = jnp.where(row < 4, misc, 0.0).astype(bf16)
 
-    @pl.loop(0, feats.shape[1] // CHUNK)
-    def _(step):
-        columns = pl.ds(pl.multiple_of(step * CHUNK, CHUNK), CHUNK)
-        one = rectified(dot(turned_in[...], feats[:, columns]))
-        act_one[:, columns] = one
-        two = rectified(dot(turned_hid[0], one) + bias_cols[:, 0:1])
-        act_two[:, columns] = two
-        three = rectified(dot(turned_hid[1], two) + bias_cols[:, 1:2])
-        act_three[:, columns] = three
-        heads = dot(out_rows[...], three)
-        for tile in range(CHUNK // 128):
-            at = pl.multiple_of((step * (CHUNK // 128) + tile) * 8, 8)
-            heads_rows[pl.ds(at, 8), :] = heads[0:8, tile * 128 : (tile + 1) * 128]
+    _, _, three = layers(feats[...], turned_in, turned_hid, bias_cols)
+    heads = dot(out_rows[...], three)
+    for tile in range(feats.shape[1] // 128):
+        heads_rows[tile * 8 : tile * 8 + 8, :] = heads[0:8, tile * 128 : (tile + 1) * 128]
 
     density = turn(heads_rows[pl.ds(0, S, stride=8), :])
     slot = lax.broadcasted_iota(jnp.int32, (S, 128), 0).astype(f32)
@@ -227,38 +228,30 @@
 
 
 def backward_kernel(
-    table, ranks, target, shading, wide_hid, wide_misc, feats, act_one, act_two, act_three,
+    table, ranks, target, shading, wide_in, wide_hid, wide_misc, feats,
     even, odd,
-    reach_rows, grad_rows, out_cols, sum_third, sum_second, sum_first, sum_out,
+    reach_rows, grad_rows, out_cols, turned_in, turned_hid, bias_cols, act_one, act_two, act_three,
 ):
+    turn_weights(wide_in, wide_hid, wide_misc[...], turned_in, turned_hid, bias_cols)
     composite(table, ranks, target, shading, reach_rows, grad_rows)
     row = lax.broadcasted_iota(jnp.int32, (16, HID), 0)
     out_cols[...] = jnp.where(row < 4, wide_misc[...], 0.0).T.astype(bf16)
-    for total in (sum_third, sum_second, sum_first, sum_out):
-        total[...] = jnp.zeros(total.shape, f32)
-
-    @pl.loop(0, feats.shape[1] // CHUNK)
-    def _(step):
-        columns = pl.ds(pl.multiple_of(step * CHUNK, CHUNK), CHUNK)
-        tiles = CHUNK // 128
-        heads = jnp.concatenate(
-            [
-                grad_rows[pl.ds(pl.multiple_of((step * tiles + tile) * 16, 16), 16), :]
-                for tile in range(tiles)
-            ],
-            axis=1,
-        ).astype(bf16)
-        ones = jnp.ones((16, CHUNK), bf16)
-        one, two, three = act_one[:, columns], act_two[:, columns], act_three[:, columns]
-        back_three = masked(three, dot(out_cols[...], heads))
-        sum_out[...] += dot_last(heads, three)
-        back_two = masked(two, dot(wide_hid[1], back_three))
-        sum_third[...] += dot_last(jnp.concatenate([two, ones], axis=0), back_three)
-        back_one = masked(one, dot(wide_hid[0], back_two))
-        sum_second[...] += dot_last(jnp.concatenate([one, ones], axis=0), back_two)
-        sum_first[...] += dot_last(feats[:, columns], back_one)
-
-    misc = jnp.where(row < 4, sum_out[...], 0.0)
+    samples = feats[...]
+    act_one[...], act_two[...], act_three[...] = layers(samples, turned_in, turned_hid, bias_cols)
+    one, two, three = act_one[...], act_two[...], act_three[...]
+    heads = jnp.concatenate(
+        [grad_rows[tile * 16 : tile * 16 + 16, :] for tile in range(feats.shape[1] // 128)], axis=1
+    ).astype(bf16)
+    ones = jnp.ones((16, feats.shape[1]), bf16)
+    back_three = masked(three, dot(out_cols[...], heads))
+    sum_out = dot_last(heads, three)
+    back_two = masked(two, dot(wide_hid[1], back_three))
+    sum_third = dot_last(jnp.concatenate([two, ones], axis=0), back_three)
+    back_one = masked(one, dot(wide_hid[0], back_two))
+    sum_second = dot_last(jnp.concatenate([one, ones], axis=0), back_two)
+    sum_first = dot_last(samples, back_one)
+
+    misc = jnp.where(row < 4, sum_out, 0.0)
     misc = misc + jnp.where(row == 4, sum_second[HID : HID + 16, :], 0.0)
     misc = misc + jnp.where(row == 5, sum_third[HID : HID + 16, :], 0.0)
     even[0:HID, :] = sum_third[0:HID, :].astype(bf16)
@@ -438,43 +431,32 @@
     )
     feats = jnp.concatenate([features[0], jnp.ones((1, samples), bf16)], axis=0)
     state, feats, *highs[1:] = lax.optimization_barrier((state, feats, *highs[1:]))
-    sides = [
-        lax.ppermute(state, "batch", [(i, (i + hop) % N_BATCH) for i in range(N_BATCH)])
-        for hop in (1, 3)
-    ]
-
-    act = held((HID, samples), bf16)
-    act_one, act_two, act_three, wide_hid, wide_misc, shading, summary = call(
+    states = [state] + from_others(state)
+
+    turned = [((HID, ENC + 1), bf16), ((2, HID, HID), bf16), ((HID, 8), f32)]
+    wide_in, wide_hid, wide_misc, shading, summary = call(
         forward_kernel,
         (
-            act, act, act, held((2, HID, HID), bf16),
-            held((16, HID)), held((6, S, 128)), held((4, rays)),
+            held((ENC + 1, HID), bf16), held((2, HID, HID), bf16), held((16, HID)), held((6, S, 128)),
+            held((4, rays)),
         ),
-        scratch=[
-            ((ENC + 1, HID), bf16), ((HID, ENC + 1), bf16), ((2, HID, HID), bf16), ((HID, 8), f32),
-            ((16, HID), bf16), ((samples // 16, 128), f32),
-        ],
+        scratch=turned + [((16, HID), bf16), ((samples // 16, 128), f32)],
         name="forward",
     )(*highs, feats, gaps, live_counts)
 
-    summary, *sides = lax.optimization_barrier((summary, *sides))
     table = lax.all_to_all(
         jnp.broadcast_to(summary[None], (cells, 4, rays)), "region", 0, 0, tiled=True
     ).reshape(cells * 4, rays)
-    table, state = lax.optimization_barrier((table, state))
-    opposite = lax.ppermute(state, "batch", [(i, (i + 2) % N_BATCH) for i in range(N_BATCH)])
 
     even, odd = call(
         backward_kernel,
         (held((HID + 48, HID), bf16), held((HID + 32, HID), bf16)),
-        scratch=[
-            ((cells, 128), f32), ((samples // 8, 128), f32), ((HID, 16), bf16), ((HID + 16, HID), f32),
-            ((HID + 16, HID), f32), ((64, HID), f32), ((16, HID), f32),
-        ],
+        scratch=[((cells, 128), f32), ((samples // 8, 128), f32), ((HID, 16), bf16)]
+        + turned
+        + [((HID, samples), bf16)] * 3,
         name="backward",
-    )(table, ranks, goal, shading, wide_hid, wide_misc, feats, act_one, act_two, act_three)
-    even, odd, opposite = lax.optimization_barrier((even, odd, opposite))
-    states = [state, sides[0], opposite, sides[1]]
+    )(table, ranks, goal, shading, wide_in, wide_hid, wide_misc, feats)
+    even, odd, *states = lax.optimization_barrier((even, odd, *states))
     even, odd = [
         call(pair_kernel, held(own.shape, bf16), name="pair")(own, swapped(own, first))
         for own, first in ((even, True), (odd, False))

time: 67.1 us -> 66.2 us (0.987)
  blocking collectives: 21.8 us -> 0 us
  starting transfers between devices: 13.6 us -> 28.2 us
  Pallas kernels: 17 us -> 20.6 us
  waiting for transfers between devices: 12.3 us -> 14.1 us
    all_to_all x1 -> x0, blocking collectives: 21.8 us -> none  [body(): lax.all_to_all(jnp.broadcast_to(summary[None], (cells, 4, rays)), 'region...]
    all_to_all x0 -> x1, starting transfers between devices: none -> 12 us  [body(): lax.all_to_all(jnp.broadcast_to(summary[None], (cells, 4, rays)), 'region...]
    ppermute x3 -> x6, starting transfers between devices: 4.69 us -> 10.6 us  [from_others(): lax.ppermute(block, 'batch', [(i, (i + hop) % N_BATCH) for i in range(N_B...]
    all_to_all x0 -> x1, waiting for transfers between devices: none -> 5.23 us  [body(): lax.all_to_all(jnp.broadcast_to(summary[None], (cells, 4, rays)), 'region...]
    pallas_call x1, Pallas kernels: 8.53 us -> 12 us  [body(): call(backward_kernel, (held((HID + 48, HID), bf16), held((HID + 32, HID),...]
    ppermute x3 -> x0, starting transfers between devices: 2.88 us -> none  [the longest x2 2.03 us: body(): lax.ppermute(state, 'batch', [(i, (i + hop) % N_BATCH) for i in range(N_B...]
    ppermute x3 -> x6, waiting for transfers between devices: 2.87 us -> 0.4 us  [from_others(): lax.ppermute(block, 'batch', [(i, (i + hop) % N_BATCH) for i in range(N_B...]
    ppermute x3 -> x0, waiting for transfers between devices: 2.07 us -> none  [the longest x2 1.99 us: body(): lax.ppermute(state, 'batch', [(i, (i + hop) % N_BATCH) for i in range(N_B...]
  transfers between devices with their start and end apart: 10 -> 11, of which waited for: 7 -> 4; matrix products, arithmetic and copies ran while one was open for 2% -> 2% of each run, Pallas kernels for 21% -> 20%
where the time goes in v5:
time: 66.2 us; the launch traced here: 65.7 us
  starting transfers between devices  28.2 us (43%)
  Pallas kernels  20.6 us (31%)
  waiting for transfers between devices  14.1 us (21%)
  local copies, waits for them, and re-layouts  2 us (3%)
  between operations  0.79 us (1%)
    pallas_call x1, Pallas kernels, body(): call(backward_kernel, (held((HID + 48, HID), bf16), held((HID + 32, HID),...  12 us
    all_to_all x1, starting transfers between devices, body(): lax.all_to_all(jnp.broadcast_to(summary[None], (cells, 4, rays)), 'region...  12 us
    ppermute x6, starting transfers between devices, from_others(): lax.ppermute(block, 'batch', [(i, (i + hop) % N_BATCH) for i in range(N_B...  10.6 us
    ppermute x4, waiting for transfers between devices, swapped(): return lax.ppermute(block, 'batch', pairs + [(j, i) for i, j in pairs])  8.5 us
    ppermute x4, starting transfers between devices, swapped(): return lax.ppermute(block, 'batch', pairs + [(j, i) for i, j in pairs])  5.53 us
    all_to_all x1, waiting for transfers between devices, body(): lax.all_to_all(jnp.broadcast_to(summary[None], (cells, 4, rays)), 'region...  5.23 us
    pallas_call x1, Pallas kernels, body(): call(forward_kernel, (held((ENC + 1, HID), bf16), held((2, HID, HID), bf1...  4.46 us
    pallas_call x2, Pallas kernels, call_on_hbm(): pl.pallas_call(fetched(kernel, len(arrays), len(outs)), out_shape=outs, i...  2.47 us
  transfers between devices with their start and end apart: 11, of which 4 were waited for; matrix products, arithmetic and copies ran while one was open for 2% of the time, Pallas kernels for 20%

profile of v5, /device:TPU:2, one launch (start us, length us, event | category | flops | bytes accessed | tf_op | source)
XLA Modules:
  0.0 65.7 jit_solution(15462699141547930591)
XLA Ops:
  0.6 1.1 %pack_weights.1.own.high_0 = bf16[160,256]{1,0:T(8,128)(2,1)S(1)} custom-call(f32[1,16,256]{2,1,0:T(8,128)} %refs_0_.3, f32[1,2,64,256]{3,2,1,0:T(8,128)} %refs_1_.3, f32[1,2,64]{2,1,0:T(2,128)} %refs_2_.2, f32[1,4,64]{2,1,0:T(4,128)} %refs_2_.3), custom_call_target="tpu_custom_call" | custom-call | tf_op jit(solution)/shard_map/pack_weights/pallas_call | solution.py:367
  1.7 1.7 %collective-permute-start = (bf16[160,256]{1,0:T(8,128)(2,1)S(1)}, bf16[160,256]{1,0:T(8,128)(2,1)S(1)}, u32[]{:S(2)}, u32[]{:S(2)}) collective-permute-start(bf16[160,256]{1,0:T(8,128)(2,1)S(1)} %pack_weights.1.own.high_0), channel_id=1, source_target_pairs={{0,1},{1,2},{2,3},{3,0},{4,5},{5,6},{6,7},{7,4},{8,9},{9,10},{10,1... | collective-permute-start | bytes 245768 | tf_op jit(solution)/shard_map/ppermute | solution.py:390
  3.4 2.9 %collective-permute-start.1 = (bf16[160,256]{1,0:T(8,128)(2,1)S(1)}, bf16[160,256]{1,0:T(8,128)(2,1)S(1)}, u32[]{:S(2)}, u32[]{:S(2)}) collective-permute-start(bf16[160,256]{1,0:T(8,128)(2,1)S(1)} %pack_weights.1.own.high_0), channel_id=1, source_target_pairs={{0,2},{1,3},{2,0},{3,1},{4,6},{5,7},{6,4},{7,5},{8,10},{9,11},{10,... | collective-permute-start | bytes 245768 | tf_op jit(solution)/shard_map/ppermute | solution.py:390
  6.3 1.3 %collective-permute-start.2 = (bf16[160,256]{1,0:T(8,128)(2,1)S(1)}, bf16[160,256]{1,0:T(8,128)(2,1)S(1)}, u32[]{:S(2)}, u32[]{:S(2)}) collective-permute-start(bf16[160,256]{1,0:T(8,128)(2,1)S(1)} %pack_weights.1.own.high_0), channel_id=1, source_target_pairs={{0,3},{1,0},{2,1},{3,2},{4,7},{5,4},{6,5},{7,6},{8,11},{9,8},{10,9... | collective-permute-start | bytes 245768 | tf_op jit(solution)/shard_map/ppermute | solution.py:390
  7.6 1.3 %concatenate.3.feats = bf16[64,8192]{1,0:T(8,128)(2,1)S(1)} pad(bf16[63,8192]{1,0:T(8,128)(2,1)} %bitcast.5, bf16[]{:T(256)} %constant.0.clone.1), padding=0_1x0_0 | pad | bytes 2080770 | tf_op jit(solution)/shard_map/concatenate | solution.py:432
  9.0 1.4 %prepare.1 = (bf16[480,256]{1,0:T(8,128)(2,1)S(1)}, f32[64,128]{1,0:T(8,128)S(1)}, f32[1,128]{1,0:T(1,128)S(1)}, f32[64,128]{1,0:T(8,128)S(1)}, f32[3,128]{1,0:T(4,128)S(1)}) custom-call(f32[1,16,256]{2,1,0:T(8,128)} %refs_0_.3, f32[1,2,64,256]{3,2,1,0:T(8,128)} %refs_1_.3, f32[1,4,64]{2,1,0:T(4,128)} %refs_2_.3, f32[2,1,16,256]{3,2,1,0:T(8,128)} %mom_in.1, ...), custom_call_target="tpu_custom_call" | custom-call | tf_op jit(solution)/shard_map/prepare/pallas_call | solution.py:367
  10.3 0.0 collective-permute-done.from_one.high_1
  10.3 0.0 collective-permute-done.1.from_two.high_2
  10.3 0.4 collective-permute-done.2.from_three.high_3
  10.7 4.5 %forward.1 = (bf16[64,256]{1,0:T(8,128)(2,1)S(1)}, bf16[2,256,256]{2,1,0:T(8,128)(2,1)S(1)}, f32[16,256]{1,0:T(8,128)S(1)}, f32[6,64,128]{2,1,0:T(8,128)S(1)}, f32[4,128]{1,0:T(4,128)S(1)}) custom-call(bf16[160,256]{1,0:T(8,128)(2,1)S(1)} %pack_weights.1.own.high_0, bf16[160,256]{1,0:T(8,128)(2,1)S(1)} %collective-permute-done.from_one.high_1, ...), custom_call_target="tpu_custom_call" | custom-call | tf_op jit(solution)/shard_map/forward/pallas_call | solution.py:437
  15.2 0.7 %broadcast_in_dim.2 = f32[64,4,128]{2,1,0:T(4,128)} broadcast(f32[4,128]{1,0:T(4,128)S(1)} %get-tuple-element.42), dimensions={1,2} | broadcast | bytes 133120 | tf_op jit(solution)/shard_map/broadcast_in_dim | solution.py:448
  15.9 12.0 %all-to-all-start = ((f32[64,4,128]{2,1,0:T(4,128)}), f32[64,4,128]{2,1,0:T(4,128)S(1)}, u32[]{:S(2)}, u32[]{:S(2)}) async-start(f32[64,4,128]{2,1,0:T(4,128)} %broadcast_in_dim.2), calls=%async_computation | async-start | bytes 262144 | tf_op jit(solution)/shard_map/all_to_all | solution.py:447
  27.9 0.8 %collective-permute-start.3 = (bf16[480,256]{1,0:T(8,128)(2,1)S(1)}, bf16[480,256]{1,0:T(8,128)(2,1)S(1)}, u32[]{:S(2)}, u32[]{:S(2)}) collective-permute-start(bf16[480,256]{1,0:T(8,128)(2,1)S(1)} %get-tuple-element.54.state_0), channel_id=1, source_target_pairs={{0,1},{1,2},{2,3},{3,0},{4,5},{5,6},{6,7},{7,4},{8,9},{9,10},{10,1... | collective-permute-start | bytes 737288 | tf_op jit(solution)/shard_map/ppermute | solution.py:390
  28.7 3.3 %collective-permute-start.4 = (bf16[480,256]{1,0:T(8,128)(2,1)S(1)}, bf16[480,256]{1,0:T(8,128)(2,1)S(1)}, u32[]{:S(2)}, u32[]{:S(2)}) collective-permute-start(bf16[480,256]{1,0:T(8,128)(2,1)S(1)} %get-tuple-element.54.state_0), channel_id=1, source_target_pairs={{0,2},{1,3},{2,0},{3,1},{4,6},{5,7},{6,4},{7,5},{8,10},{9,11},{10,... | collective-permute-start | bytes 737288 | tf_op jit(solution)/shard_map/ppermute | solution.py:390
  32.0 0.6 collective-permute-start.5
  32.6 5.2 %all-to-all-done = f32[64,4,128]{2,1,0:T(4,128)S(1)} async-done(((f32[64,4,128]{2,1,0:T(4,128)}), f32[64,4,128]{2,1,0:T(4,128)S(1)}, u32[]{:S(2)}, u32[]{:S(2)}) %all-to-all-start) | async-done | bytes 131104 | tf_op jit(solution)/shard_map/all_to_all | solution.py:447
  37.8 12.0 %backward.1 = (bf16[304,256]{1,0:T(8,128)(2,1)S(1)}, bf16[288,256]{1,0:T(8,128)(2,1)S(1)}) custom-call(f32[256,128]{1,0:T(8,128)S(1)} %bitcast.4, f32[64,128]{1,0:T(8,128)S(1)} %get-tuple-element.43.ranks, f32[3,128]{1,0:T(4,128)S(1)} %get-tuple-element.44.target, f32[6,64,128]{2,1,0:T(8,128)S(1)} %get-tuple-element.45.shading, ...), custom_call_target="tpu_custom_call" | custom-call | tf_op jit(solution)/shard_map/backward/pallas_call | solution.py:451
  49.9 0.0 collective-permute-done.3.state_1
  49.9 0.0 collective-permute-done.4.state_2
  49.9 0.0 collective-permute-done.5.state_3
  49.9 0.8 %collective-permute-start.6 = (bf16[304,256]{1,0:T(8,128)(2,1)S(1)}, bf16[304,256]{1,0:T(8,128)(2,1)S(1)}, u32[]{:S(2)}, u32[]{:S(2)}) collective-permute-start(bf16[304,256]{1,0:T(8,128)(2,1)S(1)} %get-tuple-element.52.own), channel_id=1, source_target_pairs={{0,1},{2,3},{1,0},{3,2},{4,5},{6,7},{5,4},{7,6},{8,9},{10,11},{9,8... | collective-permute-start | bytes 466952 | tf_op jit(solution)/shard_map/ppermute | solution.py:397
  50.7 2.0 %collective-permute-start.8 = (bf16[288,256]{1,0:T(8,128)(2,1)S(1)}, bf16[288,256]{1,0:T(8,128)(2,1)S(1)}, u32[]{:S(2)}, u32[]{:S(2)}) collective-permute-start(bf16[288,256]{1,0:T(8,128)(2,1)S(1)} %get-tuple-element.53.own), channel_id=1, source_target_pairs={{1,2},{3,0},{2,1},{0,3},{5,6},{7,4},{6,5},{4,7},{9,10},{11,8},{10,... | collective-permute-start | bytes 442376 | tf_op jit(solution)/shard_map/ppermute | solution.py:397
  52.7 3.4 %collective-permute-done.6.other = bf16[304,256]{1,0:T(8,128)(2,1)S(1)} collective-permute-done((bf16[304,256]{1,0:T(8,128)(2,1)S(1)}, bf16[304,256]{1,0:T(8,128)(2,1)S(1)}, u32[]{:S(2)}, u32[]{:S(2)}) %collective-permute-start.6) | collective-permute-done | bytes 155680 | tf_op jit(solution)/shard_map/ppermute | solution.py:397
  56.1 0.0 copy-start
  56.1 0.0 copy-start.1
  56.1 0.0 copy-start.2
  56.1 0.0 copy-start.3
  56.1 2.7 %collective-permute-start.7 = (bf16[304,256]{1,0:T(8,128)(2,1)S(1)}, bf16[304,256]{1,0:T(8,128)(2,1)S(1)}, u32[]{:S(2)}, u32[]{:S(2)}) collective-permute-start(bf16[304,256]{1,0:T(8,128)(2,1)S(1)} %pair.2.even), channel_id=1, source_target_pairs={{1,2},{3,0},{2,1},{0,3},{5,6},{7,4},{6,5},{4,7},{9,10},{11,8},{10,... | collective-permute-start | bytes 466952 | tf_op jit(solution)/shard_map/ppermute | solution.py:397
  58.8 0.0 collective-permute-done.8.other
  58.8 0.1 collective-permute-start.9
  58.9 5.1 %collective-permute-done.9.odd_other = bf16[288,256]{1,0:T(8,128)(2,1)S(1)} collective-permute-done((bf16[288,256]{1,0:T(8,128)(2,1)S(1)}, bf16[288,256]{1,0:T(8,128)(2,1)S(1)}, u32[]{:S(2)}, u32[]{:S(2)}) %collective-permute-start.9) | collective-permute-done | bytes 147488 | tf_op jit(solution)/shard_map/ppermute | solution.py:397
  64.1 0.0 collective-permute-done.7.even_other
  64.1 0.0 copy-done
  64.1 0.0 copy-done.1
  64.1 0.0 copy-done.2
  64.1 0.0 copy-done.3
  64.1 1.6 %update.1 = (f32[1,64,256]{2,1,0:T(8,128)}, f32[1,2,256,256]{3,2,1,0:T(8,128)}, f32[1,2,256]{2,1,0:T(2,128)}, f32[1,4,256]{2,1,0:T(4,128)}, f32[2,1,16,256]{3,2,...) custom-call(bf16[304,256]{1,0:T(8,128)(2,1)S(1)} %pair.2.even, ...), custom_call_target="tpu_custom_call" | custom-call | tf_op jit(solution)/shard_map/update/pallas_call | solution.py:465
  (2 shorter events, 0.1 us)
Async XLA Ops:
  1.7 8.6 %collective-permute-start = (bf16[160,256]{1,0:T(8,128)(2,1)S(1)}, bf16[160,256]{1,0:T(8,128)(2,1)S(1)}, u32[]{:S(2)}, u32[]{:S(2)}) collective-permute-start(bf16[160,256]{1,0:T(8,128)(2,1)S(1)} %pack_weights.1.own.high_0), channel_id=1, source_target_pairs={{0,1},{1,2},{2,3},{3,0},{4,5},{5,6},{6,7},{7,4},{8,9},{9,10},{10,1... | collective-permute-start | bytes 245768 | tf_op jit(solution)/shard_map/ppermute | solution.py:390
  3.4 6.9 %collective-permute-start.1 = (bf16[160,256]{1,0:T(8,128)(2,1)S(1)}, bf16[160,256]{1,0:T(8,128)(2,1)S(1)}, u32[]{:S(2)}, u32[]{:S(2)}) collective-permute-start(bf16[160,256]{1,0:T(8,128)(2,1)S(1)} %pack_weights.1.own.high_0), channel_id=1, source_target_pairs={{0,2},{1,3},{2,0},{3,1},{4,6},{5,7},{6,4},{7,5},{8,10},{9,11},{10,... | collective-permute-start | bytes 245768 | tf_op jit(solution)/shard_map/ppermute | solution.py:390
  6.3 4.4 %collective-permute-start.2 = (bf16[160,256]{1,0:T(8,128)(2,1)S(1)}, bf16[160,256]{1,0:T(8,128)(2,1)S(1)}, u32[]{:S(2)}, u32[]{:S(2)}) collective-permute-start(bf16[160,256]{1,0:T(8,128)(2,1)S(1)} %pack_weights.1.own.high_0), channel_id=1, source_target_pairs={{0,3},{1,0},{2,1},{3,2},{4,7},{5,4},{6,5},{7,6},{8,11},{9,8},{10,9... | collective-permute-start | bytes 245768 | tf_op jit(solution)/shard_map/ppermute | solution.py:390
  15.9 22.0 %all-to-all-start = ((f32[64,4,128]{2,1,0:T(4,128)}), f32[64,4,128]{2,1,0:T(4,128)S(1)}, u32[]{:S(2)}, u32[]{:S(2)}) async-start(f32[64,4,128]{2,1,0:T(4,128)} %broadcast_in_dim.2), calls=%async_computation | async-start | bytes 262144 | tf_op jit(solution)/shard_map/all_to_all | solution.py:447
  27.9 22.0 %collective-permute-start.3 = (bf16[480,256]{1,0:T(8,128)(2,1)S(1)}, bf16[480,256]{1,0:T(8,128)(2,1)S(1)}, u32[]{:S(2)}, u32[]{:S(2)}) collective-permute-start(bf16[480,256]{1,0:T(8,128)(2,1)S(1)} %get-tuple-element.54.state_0), channel_id=1, source_target_pairs={{0,1},{1,2},{2,3},{3,0},{4,5},{5,6},{6,7},{7,4},{8,9},{9,10},{10,1... | collective-permute-start | bytes 737288 | tf_op jit(solution)/shard_map/ppermute | solution.py:390
  28.7 21.2 %collective-permute-start.4 = (bf16[480,256]{1,0:T(8,128)(2,1)S(1)}, bf16[480,256]{1,0:T(8,128)(2,1)S(1)}, u32[]{:S(2)}, u32[]{:S(2)}) collective-permute-start(bf16[480,256]{1,0:T(8,128)(2,1)S(1)} %get-tuple-element.54.state_0), channel_id=1, source_target_pairs={{0,2},{1,3},{2,0},{3,1},{4,6},{5,7},{6,4},{7,5},{8,10},{9,11},{10,... | collective-permute-start | bytes 737288 | tf_op jit(solution)/shard_map/ppermute | solution.py:390
  32.0 17.9 %collective-permute-start.5 = (bf16[480,256]{1,0:T(8,128)(2,1)S(1)}, bf16[480,256]{1,0:T(8,128)(2,1)S(1)}, u32[]{:S(2)}, u32[]{:S(2)}) collective-permute-start(bf16[480,256]{1,0:T(8,128)(2,1)S(1)} %get-tuple-element.54.state_0), channel_id=1, source_target_pairs={{0,3},{1,0},{2,1},{3,2},{4,7},{5,4},{6,5},{7,6},{8,11},{9,8},{10,9... | collective-permute-start | bytes 737288 | tf_op jit(solution)/shard_map/ppermute | solution.py:390
  49.9 6.1 %collective-permute-start.6 = (bf16[304,256]{1,0:T(8,128)(2,1)S(1)}, bf16[304,256]{1,0:T(8,128)(2,1)S(1)}, u32[]{:S(2)}, u32[]{:S(2)}) collective-permute-start(bf16[304,256]{1,0:T(8,128)(2,1)S(1)} %get-tuple-element.52.own), channel_id=1, source_target_pairs={{0,1},{2,3},{1,0},{3,2},{4,5},{6,7},{5,4},{7,6},{8,9},{10,11},{9,8... | collective-permute-start | bytes 466952 | tf_op jit(solution)/shard_map/ppermute | solution.py:397
  50.7 8.1 %collective-permute-start.8 = (bf16[288,256]{1,0:T(8,128)(2,1)S(1)}, bf16[288,256]{1,0:T(8,128)(2,1)S(1)}, u32[]{:S(2)}, u32[]{:S(2)}) collective-permute-start(bf16[288,256]{1,0:T(8,128)(2,1)S(1)} %get-tuple-element.53.own), channel_id=1, source_target_pairs={{1,2},{3,0},{2,1},{0,3},{5,6},{7,4},{6,5},{4,7},{9,10},{11,8},{10,... | collective-permute-start | bytes 442376 | tf_op jit(solution)/shard_map/ppermute | solution.py:397
  56.1 8.0 %copy-start = (f32[2,1,2,64,256]{4,3,2,1,0:T(8,128)S(1)}, f32[2,1,2,64,256]{4,3,2,1,0:T(8,128)}, u32[]{:S(2)}) copy-start(f32[2,1,2,64,256]{4,3,2,1,0:T(8,128)} %mom_hid.1) | copy-start | bytes 786436
  56.1 8.0 %copy-start.1 = (f32[2,1,16,256]{3,2,1,0:T(8,128)S(1)}, f32[2,1,16,256]{3,2,1,0:T(8,128)}, u32[]{:S(2)}) copy-start(f32[2,1,16,256]{3,2,1,0:T(8,128)} %mom_in.1) | copy-start | bytes 98308
  56.1 8.0 %copy-start.2 = (f32[2,1,4,64]{3,2,1,0:T(4,128)S(1)}, f32[2,1,4,64]{3,2,1,0:T(4,128)}, u32[]{:S(2)}) copy-start(f32[2,1,4,64]{3,2,1,0:T(4,128)} %mom_out.1) | copy-start | bytes 6148
  56.1 8.0 %copy-start.3 = (f32[2,1,2,64]{3,2,1,0:T(2,128)S(1)}, f32[2,1,2,64]{3,2,1,0:T(2,128)}, u32[]{:S(2)}) copy-start(f32[2,1,2,64]{3,2,1,0:T(2,128)} %mom_bias.1) | copy-start | bytes 3076
  56.1 7.9 %collective-permute-start.7 = (bf16[304,256]{1,0:T(8,128)(2,1)S(1)}, bf16[304,256]{1,0:T(8,128)(2,1)S(1)}, u32[]{:S(2)}, u32[]{:S(2)}) collective-permute-start(bf16[304,256]{1,0:T(8,128)(2,1)S(1)} %pair.2.even), channel_id=1, source_target_pairs={{1,2},{3,0},{2,1},{0,3},{5,6},{7,4},{6,5},{4,7},{9,10},{11,8},{10,... | collective-permute-start | bytes 466952 | tf_op jit(solution)/shard_map/ppermute | solution.py:397
  58.8 5.2 %collective-permute-start.9 = (bf16[288,256]{1,0:T(8,128)(2,1)S(1)}, bf16[288,256]{1,0:T(8,128)(2,1)S(1)}, u32[]{:S(2)}, u32[]{:S(2)}) collective-permute-start(bf16[288,256]{1,0:T(8,128)(2,1)S(1)} %pair.3.odd), channel_id=1, source_target_pairs={{0,1},{2,3},{1,0},{3,2},{4,5},{6,7},{5,4},{7,6},{8,9},{10,11},{9,8... | collective-permute-start | bytes 442376 | tf_op jit(solution)/shard_map/ppermute | solution.py:397

commit v6 on v5

--- a/solution.py
+++ b/solution.py
@@ -147,8 +147,8 @@
 
 def forward_kernel(
     own, from_one, from_two, from_three, feats, gaps, counts,
-    wide_in, wide_hid, wide_misc, shading, summary,
-    turned_in, turned_hid, bias_cols, out_rows, heads_rows,
+    wide_in, wide_hid, wide_misc, shading, sent,
+    turned_in, turned_hid, bias_cols, out_rows, heads_rows, summary,
 ):
     me = lax.axis_index("batch")
     misc = jnp.zeros((16, HID), f32)
@@ -186,6 +186,8 @@
     shading[3] = weight
     shading[4] = jnp.exp(-total)
     shading[5] = live_gap * sigmoid(density)
+    for cell in range(sent.shape[0]):
+        sent[cell] = summary[...]
 
 
 def composite(table, ranks, target, shading, reach_rows, grad_rows):
@@ -434,19 +436,17 @@
     states = [state] + from_others(state)
 
     turned = [((HID, ENC + 1), bf16), ((2, HID, HID), bf16), ((HID, 8), f32)]
-    wide_in, wide_hid, wide_misc, shading, summary = call(
+    wide_in, wide_hid, wide_misc, shading, sent = call(
         forward_kernel,
         (
             held((ENC + 1, HID), bf16), held((2, HID, HID), bf16), held((16, HID)), held((6, S, 128)),
-            held((4, rays)),
+            shape((cells, 4, rays)),
         ),
-        scratch=turned + [((16, HID), bf16), ((samples // 16, 128), f32)],
+        scratch=turned + [((16, HID), bf16), ((samples // 16, 128), f32), ((4, rays), f32)],
         name="forward",
     )(*highs, feats, gaps, live_counts)
 
-    table = lax.all_to_all(
-        jnp.broadcast_to(summary[None], (cells, 4, rays)), "region", 0, 0, tiled=True
-    ).reshape(cells * 4, rays)
+    table = lax.all_to_all(sent, "region", 0, 0, tiled=True).reshape(cells * 4, rays)
 
     even, odd = call(
         backward_kernel,

time: 66.2 us -> 66.2 us (level)
  Pallas kernels: 20.6 us -> 21.3 us
  local copies, waits for them, and re-layouts: 2 us -> 1.33 us
    pallas_call x1, Pallas kernels: 4.46 us -> 5.14 us  [body(): call(forward_kernel, (held((ENC + 1, HID), bf16), held((2, HID, HID), bf1...]
    broadcast_in_dim x1 -> x0, local copies, waits for them, and re-layouts: 0.67 us -> none  [body(): jnp.broadcast_to(summary[None], (cells, 4, rays))]
where the time goes in v6:
time: 66.2 us; the launch traced here: 65.7 us
  starting transfers between devices  28.1 us (42%)
  Pallas kernels  21.3 us (32%)
  waiting for transfers between devices  14.1 us (21%)
  local copies, waits for them, and re-layouts  1.33 us (2%)
  between operations  0.78 us (1%)
    pallas_call x1, Pallas kernels, body(): call(backward_kernel, (held((HID + 48, HID), bf16), held((HID + 32, HID),...  12 us
    all_to_all x1, starting transfers between devices, body(): lax.all_to_all(sent, 'region', 0, 0, tiled=True).reshape(cells * 4, rays)  12 us
    ppermute x6, starting transfers between devices, from_others(): lax.ppermute(block, 'batch', [(i, (i + hop) % N_BATCH) for i in range(N_B...  10.6 us
    ppermute x4, waiting for transfers between devices, swapped(): return lax.ppermute(block, 'batch', pairs + [(j, i) for i, j in pairs])  8.51 us
    ppermute x4, starting transfers between devices, swapped(): return lax.ppermute(block, 'batch', pairs + [(j, i) for i, j in pairs])  5.51 us
    all_to_all x1, waiting for transfers between devices, body(): lax.all_to_all(sent, 'region', 0, 0, tiled=True).reshape(cells * 4, rays)  5.24 us
    pallas_call x1, Pallas kernels, body(): call(forward_kernel, (held((ENC + 1, HID), bf16), held((2, HID, HID), bf1...  5.14 us
    pallas_call x2, Pallas kernels, call_on_hbm(): pl.pallas_call(fetched(kernel, len(arrays), len(outs)), out_shape=outs, i...  2.47 us
  transfers between devices with their start and end apart: 11, of which 4 were waited for; matrix products, arithmetic and copies ran while one was open for 2% of the time, Pallas kernels for 20%

profile of v6, /device:TPU:2, one launch (start us, length us, event | category | flops | bytes accessed | tf_op | source)
XLA Modules:
  0.0 65.7 jit_solution(4571090976576689099)
XLA Ops:
  0.6 1.1 %pack_weights.1.own.high_0 = bf16[160,256]{1,0:T(8,128)(2,1)S(1)} custom-call(f32[1,16,256]{2,1,0:T(8,128)} %refs_0_.3, f32[1,2,64,256]{3,2,1,0:T(8,128)} %refs_1_.3, f32[1,2,64]{2,1,0:T(2,128)} %refs_2_.2, f32[1,4,64]{2,1,0:T(4,128)} %refs_2_.3), custom_call_target="tpu_custom_call" | custom-call | tf_op jit(solution)/shard_map/pack_weights/pallas_call | solution.py:369
  1.7 1.7 %collective-permute-start = (bf16[160,256]{1,0:T(8,128)(2,1)S(1)}, bf16[160,256]{1,0:T(8,128)(2,1)S(1)}, u32[]{:S(2)}, u32[]{:S(2)}) collective-permute-start(bf16[160,256]{1,0:T(8,128)(2,1)S(1)} %pack_weights.1.own.high_0), channel_id=1, source_target_pairs={{0,1},{1,2},{2,3},{3,0},{4,5},{5,6},{6,7},{7,4},{8,9},{9,10},{10,1... | collective-permute-start | bytes 245768 | tf_op jit(solution)/shard_map/ppermute | solution.py:392
  3.4 2.9 %collective-permute-start.1 = (bf16[160,256]{1,0:T(8,128)(2,1)S(1)}, bf16[160,256]{1,0:T(8,128)(2,1)S(1)}, u32[]{:S(2)}, u32[]{:S(2)}) collective-permute-start(bf16[160,256]{1,0:T(8,128)(2,1)S(1)} %pack_weights.1.own.high_0), channel_id=1, source_target_pairs={{0,2},{1,3},{2,0},{3,1},{4,6},{5,7},{6,4},{7,5},{8,10},{9,11},{10,... | collective-permute-start | bytes 245768 | tf_op jit(solution)/shard_map/ppermute | solution.py:392
  6.3 1.3 %collective-permute-start.2 = (bf16[160,256]{1,0:T(8,128)(2,1)S(1)}, bf16[160,256]{1,0:T(8,128)(2,1)S(1)}, u32[]{:S(2)}, u32[]{:S(2)}) collective-permute-start(bf16[160,256]{1,0:T(8,128)(2,1)S(1)} %pack_weights.1.own.high_0), channel_id=1, source_target_pairs={{0,3},{1,0},{2,1},{3,2},{4,7},{5,4},{6,5},{7,6},{8,11},{9,8},{10,9... | collective-permute-start | bytes 245768 | tf_op jit(solution)/shard_map/ppermute | solution.py:392
  7.6 1.3 %concatenate.3.feats = bf16[64,8192]{1,0:T(8,128)(2,1)S(1)} pad(bf16[63,8192]{1,0:T(8,128)(2,1)} %bitcast.5, bf16[]{:T(256)} %constant.0.clone.1), padding=0_1x0_0 | pad | bytes 2080770 | tf_op jit(solution)/shard_map/concatenate | solution.py:434
  9.0 1.4 %prepare.1 = (bf16[480,256]{1,0:T(8,128)(2,1)S(1)}, f32[64,128]{1,0:T(8,128)S(1)}, f32[1,128]{1,0:T(1,128)S(1)}, f32[64,128]{1,0:T(8,128)S(1)}, f32[3,128]{1,0:T(4,128)S(1)}) custom-call(f32[1,16,256]{2,1,0:T(8,128)} %refs_0_.3, f32[1,2,64,256]{3,2,1,0:T(8,128)} %refs_1_.3, f32[1,4,64]{2,1,0:T(4,128)} %refs_2_.3, f32[2,1,16,256]{3,2,1,0:T(8,128)} %mom_in.1, ...), custom_call_target="tpu_custom_call" | custom-call | tf_op jit(solution)/shard_map/prepare/pallas_call | solution.py:369
  10.3 0.0 collective-permute-done.from_one.high_1
  10.3 0.0 collective-permute-done.1.from_two.high_2
  10.3 0.4 collective-permute-done.2.from_three.high_3
  10.7 5.1 %forward.1 = (bf16[64,256]{1,0:T(8,128)(2,1)S(1)}, bf16[2,256,256]{2,1,0:T(8,128)(2,1)S(1)}, f32[16,256]{1,0:T(8,128)S(1)}, f32[6,64,128]{2,1,0:T(8,128)S(1)}, f32[64,4,128]{2,1,0:T(4,128)}) custom-call(bf16[160,256]{1,0:T(8,128)(2,1)S(1)} %pack_weights.1.own.high_0, bf16[160,256]{1,0:T(8,128)(2,1)S(1)} %collective-permute-done.from_one.high_1, ...), custom_call_target="tpu_custom_call" | custom-call | tf_op jit(solution)/shard_map/forward/pallas_call | solution.py:439
  15.9 12.0 %all-to-all-start = ((f32[64,4,128]{2,1,0:T(4,128)}), f32[64,4,128]{2,1,0:T(4,128)S(1)}, u32[]{:S(2)}, u32[]{:S(2)}) async-start(f32[64,4,128]{2,1,0:T(4,128)} %get-tuple-element.42), calls=%async_computation | async-start | bytes 262144 | tf_op jit(solution)/shard_map/all_to_all | solution.py:449
  27.9 0.8 %collective-permute-start.3 = (bf16[480,256]{1,0:T(8,128)(2,1)S(1)}, bf16[480,256]{1,0:T(8,128)(2,1)S(1)}, u32[]{:S(2)}, u32[]{:S(2)}) collective-permute-start(bf16[480,256]{1,0:T(8,128)(2,1)S(1)} %get-tuple-element.54.state_0), channel_id=1, source_target_pairs={{0,1},{1,2},{2,3},{3,0},{4,5},{5,6},{6,7},{7,4},{8,9},{9,10},{10,1... | collective-permute-start | bytes 737288 | tf_op jit(solution)/shard_map/ppermute | solution.py:392
  28.7 3.3 %collective-permute-start.4 = (bf16[480,256]{1,0:T(8,128)(2,1)S(1)}, bf16[480,256]{1,0:T(8,128)(2,1)S(1)}, u32[]{:S(2)}, u32[]{:S(2)}) collective-permute-start(bf16[480,256]{1,0:T(8,128)(2,1)S(1)} %get-tuple-element.54.state_0), channel_id=1, source_target_pairs={{0,2},{1,3},{2,0},{3,1},{4,6},{5,7},{6,4},{7,5},{8,10},{9,11},{10,... | collective-permute-start | bytes 737288 | tf_op jit(solution)/shard_map/ppermute | solution.py:392
  32.0 0.6 collective-permute-start.5
  32.6 5.2 %all-to-all-done = f32[64,4,128]{2,1,0:T(4,128)S(1)} async-done(((f32[64,4,128]{2,1,0:T(4,128)}), f32[64,4,128]{2,1,0:T(4,128)S(1)}, u32[]{:S(2)}, u32[]{:S(2)}) %all-to-all-start) | async-done | bytes 131104 | tf_op jit(solution)/shard_map/all_to_all | solution.py:449
  37.8 12.0 %backward.1 = (bf16[304,256]{1,0:T(8,128)(2,1)S(1)}, bf16[288,256]{1,0:T(8,128)(2,1)S(1)}) custom-call(f32[256,128]{1,0:T(8,128)S(1)} %bitcast.4, f32[64,128]{1,0:T(8,128)S(1)} %get-tuple-element.43.ranks, f32[3,128]{1,0:T(4,128)S(1)} %get-tuple-element.44.target, f32[6,64,128]{2,1,0:T(8,128)S(1)} %get-tuple-element.45.shading, ...), custom_call_target="tpu_custom_call" | custom-call | tf_op jit(solution)/shard_map/backward/pallas_call | solution.py:451
  49.9 0.0 collective-permute-done.3.state_1
  49.9 0.0 collective-permute-done.4.state_2
  49.9 0.0 collective-permute-done.5.state_3
  49.9 0.8 %collective-permute-start.6 = (bf16[304,256]{1,0:T(8,128)(2,1)S(1)}, bf16[304,256]{1,0:T(8,128)(2,1)S(1)}, u32[]{:S(2)}, u32[]{:S(2)}) collective-permute-start(bf16[304,256]{1,0:T(8,128)(2,1)S(1)} %get-tuple-element.52.own), channel_id=1, source_target_pairs={{0,1},{2,3},{1,0},{3,2},{4,5},{6,7},{5,4},{7,6},{8,9},{10,11},{9,8... | collective-permute-start | bytes 466952 | tf_op jit(solution)/shard_map/ppermute | solution.py:399
  50.7 2.0 %collective-permute-start.8 = (bf16[288,256]{1,0:T(8,128)(2,1)S(1)}, bf16[288,256]{1,0:T(8,128)(2,1)S(1)}, u32[]{:S(2)}, u32[]{:S(2)}) collective-permute-start(bf16[288,256]{1,0:T(8,128)(2,1)S(1)} %get-tuple-element.53.own), channel_id=1, source_target_pairs={{1,2},{3,0},{2,1},{0,3},{5,6},{7,4},{6,5},{4,7},{9,10},{11,8},{10,... | collective-permute-start | bytes 442376 | tf_op jit(solution)/shard_map/ppermute | solution.py:399
  52.7 3.4 %collective-permute-done.6.other = bf16[304,256]{1,0:T(8,128)(2,1)S(1)} collective-permute-done((bf16[304,256]{1,0:T(8,128)(2,1)S(1)}, bf16[304,256]{1,0:T(8,128)(2,1)S(1)}, u32[]{:S(2)}, u32[]{:S(2)}) %collective-permute-start.6) | collective-permute-done | bytes 155680 | tf_op jit(solution)/shard_map/ppermute | solution.py:399
  56.1 0.0 copy-start
  56.1 0.0 copy-start.1
  56.1 0.0 copy-start.2
  56.1 0.0 copy-start.3
  56.1 2.7 %collective-permute-start.7 = (bf16[304,256]{1,0:T(8,128)(2,1)S(1)}, bf16[304,256]{1,0:T(8,128)(2,1)S(1)}, u32[]{:S(2)}, u32[]{:S(2)}) collective-permute-start(bf16[304,256]{1,0:T(8,128)(2,1)S(1)} %pair.2.even), channel_id=1, source_target_pairs={{1,2},{3,0},{2,1},{0,3},{5,6},{7,4},{6,5},{4,7},{9,10},{11,8},{10,... | collective-permute-start | bytes 466952 | tf_op jit(solution)/shard_map/ppermute | solution.py:399
  58.8 0.0 collective-permute-done.8.other
  58.8 0.1 collective-permute-start.9
  58.9 5.1 %collective-permute-done.9.odd_other = bf16[288,256]{1,0:T(8,128)(2,1)S(1)} collective-permute-done((bf16[288,256]{1,0:T(8,128)(2,1)S(1)}, bf16[288,256]{1,0:T(8,128)(2,1)S(1)}, u32[]{:S(2)}, u32[]{:S(2)}) %collective-permute-start.9) | collective-permute-done | bytes 147488 | tf_op jit(solution)/shard_map/ppermute | solution.py:399
  64.1 0.0 collective-permute-done.7.even_other
  64.1 0.0 copy-done
  64.1 0.0 copy-done.1
  64.1 0.0 copy-done.2
  64.1 0.0 copy-done.3
  64.1 1.6 %update.1 = (f32[1,64,256]{2,1,0:T(8,128)}, f32[1,2,256,256]{3,2,1,0:T(8,128)}, f32[1,2,256]{2,1,0:T(2,128)}, f32[1,4,256]{2,1,0:T(4,128)}, f32[2,1,16,256]{3,2,...) custom-call(bf16[304,256]{1,0:T(8,128)(2,1)S(1)} %pair.2.even, ...), custom_call_target="tpu_custom_call" | custom-call | tf_op jit(solution)/shard_map/update/pallas_call | solution.py:465
  (2 shorter events, 0.1 us)
Async XLA Ops:
  1.7 8.6 %collective-permute-start = (bf16[160,256]{1,0:T(8,128)(2,1)S(1)}, bf16[160,256]{1,0:T(8,128)(2,1)S(1)}, u32[]{:S(2)}, u32[]{:S(2)}) collective-permute-start(bf16[160,256]{1,0:T(8,128)(2,1)S(1)} %pack_weights.1.own.high_0), channel_id=1, source_target_pairs={{0,1},{1,2},{2,3},{3,0},{4,5},{5,6},{6,7},{7,4},{8,9},{9,10},{10,1... | collective-permute-start | bytes 245768 | tf_op jit(solution)/shard_map/ppermute | solution.py:392
  3.4 6.9 %collective-permute-start.1 = (bf16[160,256]{1,0:T(8,128)(2,1)S(1)}, bf16[160,256]{1,0:T(8,128)(2,1)S(1)}, u32[]{:S(2)}, u32[]{:S(2)}) collective-permute-start(bf16[160,256]{1,0:T(8,128)(2,1)S(1)} %pack_weights.1.own.high_0), channel_id=1, source_target_pairs={{0,2},{1,3},{2,0},{3,1},{4,6},{5,7},{6,4},{7,5},{8,10},{9,11},{10,... | collective-permute-start | bytes 245768 | tf_op jit(solution)/shard_map/ppermute | solution.py:392
  6.3 4.4 %collective-permute-start.2 = (bf16[160,256]{1,0:T(8,128)(2,1)S(1)}, bf16[160,256]{1,0:T(8,128)(2,1)S(1)}, u32[]{:S(2)}, u32[]{:S(2)}) collective-permute-start(bf16[160,256]{1,0:T(8,128)(2,1)S(1)} %pack_weights.1.own.high_0), channel_id=1, source_target_pairs={{0,3},{1,0},{2,1},{3,2},{4,7},{5,4},{6,5},{7,6},{8,11},{9,8},{10,9... | collective-permute-start | bytes 245768 | tf_op jit(solution)/shard_map/ppermute | solution.py:392
  15.9 22.0 %all-to-all-start = ((f32[64,4,128]{2,1,0:T(4,128)}), f32[64,4,128]{2,1,0:T(4,128)S(1)}, u32[]{:S(2)}, u32[]{:S(2)}) async-start(f32[64,4,128]{2,1,0:T(4,128)} %get-tuple-element.42), calls=%async_computation | async-start | bytes 262144 | tf_op jit(solution)/shard_map/all_to_all | solution.py:449
  27.9 22.0 %collective-permute-start.3 = (bf16[480,256]{1,0:T(8,128)(2,1)S(1)}, bf16[480,256]{1,0:T(8,128)(2,1)S(1)}, u32[]{:S(2)}, u32[]{:S(2)}) collective-permute-start(bf16[480,256]{1,0:T(8,128)(2,1)S(1)} %get-tuple-element.54.state_0), channel_id=1, source_target_pairs={{0,1},{1,2},{2,3},{3,0},{4,5},{5,6},{6,7},{7,4},{8,9},{9,10},{10,1... | collective-permute-start | bytes 737288 | tf_op jit(solution)/shard_map/ppermute | solution.py:392
  28.7 21.2 %collective-permute-start.4 = (bf16[480,256]{1,0:T(8,128)(2,1)S(1)}, bf16[480,256]{1,0:T(8,128)(2,1)S(1)}, u32[]{:S(2)}, u32[]{:S(2)}) collective-permute-start(bf16[480,256]{1,0:T(8,128)(2,1)S(1)} %get-tuple-element.54.state_0), channel_id=1, source_target_pairs={{0,2},{1,3},{2,0},{3,1},{4,6},{5,7},{6,4},{7,5},{8,10},{9,11},{10,... | collective-permute-start | bytes 737288 | tf_op jit(solution)/shard_map/ppermute | solution.py:392
  32.0 17.9 %collective-permute-start.5 = (bf16[480,256]{1,0:T(8,128)(2,1)S(1)}, bf16[480,256]{1,0:T(8,128)(2,1)S(1)}, u32[]{:S(2)}, u32[]{:S(2)}) collective-permute-start(bf16[480,256]{1,0:T(8,128)(2,1)S(1)} %get-tuple-element.54.state_0), channel_id=1, source_target_pairs={{0,3},{1,0},{2,1},{3,2},{4,7},{5,4},{6,5},{7,6},{8,11},{9,8},{10,9... | collective-permute-start | bytes 737288 | tf_op jit(solution)/shard_map/ppermute | solution.py:392
  49.9 6.1 %collective-permute-start.6 = (bf16[304,256]{1,0:T(8,128)(2,1)S(1)}, bf16[304,256]{1,0:T(8,128)(2,1)S(1)}, u32[]{:S(2)}, u32[]{:S(2)}) collective-permute-start(bf16[304,256]{1,0:T(8,128)(2,1)S(1)} %get-tuple-element.52.own), channel_id=1, source_target_pairs={{0,1},{2,3},{1,0},{3,2},{4,5},{6,7},{5,4},{7,6},{8,9},{10,11},{9,8... | collective-permute-start | bytes 466952 | tf_op jit(solution)/shard_map/ppermute | solution.py:399
  50.7 8.1 %collective-permute-start.8 = (bf16[288,256]{1,0:T(8,128)(2,1)S(1)}, bf16[288,256]{1,0:T(8,128)(2,1)S(1)}, u32[]{:S(2)}, u32[]{:S(2)}) collective-permute-start(bf16[288,256]{1,0:T(8,128)(2,1)S(1)} %get-tuple-element.53.own), channel_id=1, source_target_pairs={{1,2},{3,0},{2,1},{0,3},{5,6},{7,4},{6,5},{4,7},{9,10},{11,8},{10,... | collective-permute-start | bytes 442376 | tf_op jit(solution)/shard_map/ppermute | solution.py:399
  56.1 8.0 %copy-start = (f32[2,1,2,64,256]{4,3,2,1,0:T(8,128)S(1)}, f32[2,1,2,64,256]{4,3,2,1,0:T(8,128)}, u32[]{:S(2)}) copy-start(f32[2,1,2,64,256]{4,3,2,1,0:T(8,128)} %mom_hid.1) | copy-start | bytes 786436
  56.1 8.0 %copy-start.1 = (f32[2,1,16,256]{3,2,1,0:T(8,128)S(1)}, f32[2,1,16,256]{3,2,1,0:T(8,128)}, u32[]{:S(2)}) copy-start(f32[2,1,16,256]{3,2,1,0:T(8,128)} %mom_in.1) | copy-start | bytes 98308
  56.1 8.0 %copy-start.2 = (f32[2,1,4,64]{3,2,1,0:T(4,128)S(1)}, f32[2,1,4,64]{3,2,1,0:T(4,128)}, u32[]{:S(2)}) copy-start(f32[2,1,4,64]{3,2,1,0:T(4,128)} %mom_out.1) | copy-start | bytes 6148
  56.1 8.0 %copy-start.3 = (f32[2,1,2,64]{3,2,1,0:T(2,128)S(1)}, f32[2,1,2,64]{3,2,1,0:T(2,128)}, u32[]{:S(2)}) copy-start(f32[2,1,2,64]{3,2,1,0:T(2,128)} %mom_bias.1) | copy-start | bytes 3076
  56.1 7.9 %collective-permute-start.7 = (bf16[304,256]{1,0:T(8,128)(2,1)S(1)}, bf16[304,256]{1,0:T(8,128)(2,1)S(1)}, u32[]{:S(2)}, u32[]{:S(2)}) collective-permute-start(bf16[304,256]{1,0:T(8,128)(2,1)S(1)} %pair.2.even), channel_id=1, source_target_pairs={{1,2},{3,0},{2,1},{0,3},{5,6},{7,4},{6,5},{4,7},{9,10},{11,8},{10,... | collective-permute-start | bytes 466952 | tf_op jit(solution)/shard_map/ppermute | solution.py:399
  58.8 5.2 %collective-permute-start.9 = (bf16[288,256]{1,0:T(8,128)(2,1)S(1)}, bf16[288,256]{1,0:T(8,128)(2,1)S(1)}, u32[]{:S(2)}, u32[]{:S(2)}) collective-permute-start(bf16[288,256]{1,0:T(8,128)(2,1)S(1)} %pair.3.odd), channel_id=1, source_target_pairs={{0,1},{2,3},{1,0},{3,2},{4,5},{6,7},{5,4},{7,6},{8,9},{10,11},{9,8... | collective-permute-start | bytes 442376 | tf_op jit(solution)/shard_map/ppermute | solution.py:399
